TPU v7x, 256 devices: a whole 4x4x8 slice. The times are simulated.
256 devices in a mesh: prow: 16 (over x, y), pcol: 16 (over z, core).
Axes of the slice: x: 4, y: 4, z: 8, core: 2. Of those that a mesh axis runs over, the one named last changes fastest.
Arguments:
- seeds: int32 [64, 400], P(None, 'pcol'), may hold values from 0 to 1073741823
- tile_owner: int32 [64], replicated, may hold values from 0 to 15, as said below
- vector: float32 [204800], P(('pcol', 'prow')), may hold values from -6 to 6
- rhs: float32 [32768], P('prow'), may hold values from -6 to 6
- panel: bfloat16 [32768, 4096], P('prow', 'pcol'), may hold values from -0.25 to 0.25
- tile_scales: float32 [64, 8], P('prow'), may hold values from 0.1 to 0.5
- inverses: bfloat16 [4096, 512], P('pcol'), as said below
Outputs:
- solved: float32 [4096], P('pcol')
- updated: float32 [32768], P(('prow', 'pcol'))
Inputs may be any that keep to these rules, and one draw needn't show every extreme that they name: tile_owner[i] = (i + a) mod (16) for one a (so a = tile_owner[0]). Each block of 512 rows of inverses is unit lower triangular.
All inputs are finite; a program needn't handle non-finite values.
Results may differ from a plain program's by a relative error of at most 0.0003.
Values sent between devices are 32-bit elements; how exact they have to be, the bound alone decides.
No kernel may reach another device: no remote copies, remote signals or barrier semaphores. Data moves between devices by JAX's collectives and lax.ppermute only.
A program may use at most 64 MiB of HBM per device.

v0:
```python
import jax
import jax.numpy as jnp
from jax import lax
from jax.sharding import PartitionSpec as P

NB = 512
KB = 8
RT_DEV = 4


def from_root(value, axis, source):
    kept = jnp.where(lax.axis_index(axis) == source, value, 0).astype(value.dtype)
    return lax.psum(kept, axis)


def scramble(offsets, seed_values):
    mixed = offsets * jnp.int32(1103515245) + seed_values
    mixed = mixed ^ lax.shift_right_logical(mixed, jnp.int32(15))
    mixed = mixed * jnp.int32(747796405)
    mixed = mixed ^ lax.shift_right_logical(mixed, jnp.int32(13))
    mixed = mixed * jnp.int32(1274126177)
    mixed = mixed ^ lax.shift_right_logical(mixed, jnp.int32(16))
    return lax.shift_right_logical(mixed, jnp.int32(8)).astype(jnp.float32) * 2.0 ** (
        -32
    ) - 2.0 ** (-9)


def make_tiles(seed_cols, row_tiles, col_global):
    inner = jnp.arange(NB, dtype=jnp.int32)
    offsets = inner[:, None] * NB + jnp.mod(col_global, NB)[None, :]
    values = scramble(offsets[None, :, :], seed_cols[:, None, :])
    row_global = row_tiles[:, None] * NB + inner[None, :]
    on_diag = row_global[:, :, None] == col_global[None, None, :]
    values = jnp.where(on_diag, values + 1.0, values)
    return values.reshape(-1, col_global.shape[0])


def pick_seeds(seed_rows, local_tiles):
    match = local_tiles[:, None] == jnp.arange(seed_rows.shape[1], dtype=jnp.int32)[None, :]
    return jnp.sum(jnp.where(match[None, :, :], seed_rows[:, None, :], 0), axis=2)


def global_columns(local_cols, pcol_index, pcol_count):
    return (local_cols // NB * pcol_count + pcol_index) * NB + jnp.mod(local_cols, NB)


def body(seeds, tile_owner, vector, rhs, panel, tile_scales, inverses):
    grid_rows = lax.axis_size("prow")
    grid_cols = lax.axis_size("pcol")
    row_index = lax.axis_index("prow")
    col_index = lax.axis_index("pcol")
    anchor = tile_owner[0]
    row_count = RT_DEV * NB
    my_tiles = jnp.arange(RT_DEV, dtype=jnp.int32) * grid_rows + jnp.mod(
        row_index - anchor, grid_rows
    )
    seed_rows = lax.dynamic_slice_in_dim(seeds, row_index * RT_DEV, RT_DEV, 0)
    piece = lax.all_gather(vector, "prow", axis=0, tiled=True)
    first_col = jnp.int32(0)
    length = piece.shape[0]
    width = max((d for d in range(1, min(length, 1024) + 1) if length % d == 0))

    def column_block(block_number, inner_sum):
        local_cols = first_col + block_number * width + jnp.arange(width, dtype=jnp.int32)
        seed_cols = pick_seeds(seed_rows, local_cols // NB)
        block = make_tiles(seed_cols, my_tiles, global_columns(local_cols, col_index, grid_cols))
        entries = lax.dynamic_slice_in_dim(piece, block_number * width, width)
        return inner_sum + jnp.dot(
            block, entries, precision=lax.Precision.HIGHEST, preferred_element_type=jnp.float32
        )

    partial_rows = lax.fori_loop(
        0, length // width, column_block, jnp.zeros((row_count,), jnp.float32)
    )
    baseline = rhs - lax.psum(partial_rows, "pcol")
    pending = jnp.zeros((row_count,), jnp.float32)
    panel_wide = panel.astype(jnp.float32)
    inverse_rows = inverses.astype(jnp.float32)
    width_cols = panel.shape[1]
    my_block = col_index * width_cols // NB
    solved_mine = jnp.zeros((width_cols,), jnp.float32)
    for block_col in range(KB):
        owner = tile_owner[block_col]
        local_tile = block_col // grid_rows
        pending_tile = pending[local_tile * NB : (local_tile + 1) * NB]
        base_tile = baseline[local_tile * NB : (local_tile + 1) * NB]
        diag_rows = base_tile - lax.psum(pending_tile, "pcol")
        solution_here = jnp.dot(
            inverse_rows,
            diag_rows,
            precision=lax.Precision.HIGHEST,
            preferred_element_type=jnp.float32,
        )
        solution = from_root(solution_here, "prow", owner)
        holds_block = my_block == block_col
        solved_mine = jnp.where(holds_block, solution, solved_mine)
        factor = jnp.where(
            (my_tiles > block_col) & holds_block, tile_scales[:, block_col], jnp.float32(0.0)
        )
        update = jnp.dot(
            panel_wide,
            solution,
            precision=lax.Precision.HIGHEST,
            preferred_element_type=jnp.float32,
        ).reshape(RT_DEV, NB)
        pending = pending + (update * factor[:, None]).reshape(row_count)
    share = row_count // grid_cols
    totals = lax.psum_scatter(pending, "pcol", scatter_dimension=0, tiled=True)
    updated = lax.dynamic_slice_in_dim(baseline, col_index * share, share) - totals
    return (solved_mine, updated)


def solution(mesh):
    placed = (
        P(None, "pcol"),
        P(),
        P(("pcol", "prow")),
        P("prow"),
        P("prow", "pcol"),
        P("prow", None),
        P("pcol", None),
    )
    return jax.shard_map(
        body,
        mesh=mesh,
        in_specs=placed,
        out_specs=(P("pcol"), P(("prow", "pcol"))),
        check_vma=False,
    )
```

profile of v0, /device:TPU:29, one launch (start us, length us, event | category | flops | bytes accessed | tf_op | source)
XLA Modules:
  0.0 782.2 jit_solution(284113186840660215)
XLA Ops:
  4.4 50.2 %all-reduce = f32[12800]{0:T(1024)S(1)} all-reduce(f32[12800]{0:T(1024)S(1)} %dynamic-update-slice), channel_id=1, replica_groups=mesh['prow'=16,'pcol'=16] {'prow'}, use_global_device_ids=true, to_apply=%add | all-reduce | flops 12800 | bytes 102400
  56.9 185.6 %while.18 = (s32[]{:T(128)}, f32[2048]{0:T(1024)S(1)}, s32[]{:T(128)}, s32[4,25]{0,1:T(8,128)S(1)}, f32[12800]{0:T(1024)S(1)}, /*index=5*/s32[]{:T(128)}, s32[]{:T(128)}, s32[]{:T(128)}, s32[]{:T(128)}, s32[]{:T(128)}) while((s32[]{:T(128)}, f32[2048]{0:T(1024)S(1)}, s32[]{:T(128)}, s32[4,25]{0,1:T(8,128)S(1)}, ...), condition=%wide.region_2.3_spmd.clone, body=%wide.region_0.2_spmd.clone.sunk | while | flops 46918672 | bytes 29662248 | solution.py:72
  58.0 3.3 fusion.97
  61.3 7.2 fusion.98
  69.6 3.3 fusion.97
  72.9 7.2 fusion.98
  81.2 3.3 fusion.97
  84.6 7.2 fusion.98
  92.8 3.3 fusion.97
  96.2 7.2 fusion.98
  104.4 3.3 fusion.97
  107.8 7.2 fusion.98
  116.0 3.3 fusion.97
  119.4 7.2 fusion.98
  127.6 3.3 fusion.97
  131.0 7.2 fusion.98
  139.2 3.3 fusion.97
  142.6 7.2 fusion.98
  150.8 3.3 fusion.97
  154.2 7.2 fusion.98
  162.4 3.3 fusion.97
  165.8 7.2 fusion.98
  174.0 3.3 fusion.97
  177.4 7.2 fusion.98
  185.6 3.3 fusion.97
  189.0 7.2 fusion.98
  200.6 7.2 fusion.98
  208.8 3.3 fusion.97
  212.2 7.2 fusion.98
  223.8 7.2 fusion.98
  235.4 7.2 fusion.98
  242.6 40.7 %psum.115 = f32[2048]{0:T(1024)S(1)} all-reduce(f32[2048]{0:T(1024)S(1)} %get-tuple-element.205), channel_id=1, replica_groups=mesh['prow'=16,'pcol'=16] {'pcol'}, use_global_device_ids=true, to_apply=%region_3.4 | all-reduce | flops 2048 | bytes 16384 | tf_op jit(solution)/shard_map/psum | solution.py:75
  284.4 30.7 %psum.116 = f32[256]{0:T(256)S(1)} all-reduce(f32[256]{0:T(256)S(1)} %broadcast_select_fusion.6), channel_id=1, replica_groups=mesh['prow'=16,'pcol'=16] {'prow'}, use_global_device_ids=true, to_apply=%region_4.5 | all-reduce | flops 256 | bytes 2048 | tf_op jit(solution)/shard_map/psum | solution.py:13
  316.4 30.1 %psum.117 = f32[512]{0:T(512)S(1)} all-reduce(f32[512]{0:T(512)S(1)} %bitcast.152), channel_id=1, replica_groups=mesh['prow'=16,'pcol'=16] {'pcol'}, use_global_device_ids=true, to_apply=%region_5.6 | all-reduce | flops 512 | bytes 4096 | tf_op jit(solution)/shard_map/psum | solution.py:87
  347.4 28.6 %psum.118 = f32[256]{0:T(256)S(1)} all-reduce(f32[256]{0:T(256)S(1)} %broadcast_select_fusion.5), channel_id=1, replica_groups=mesh['prow'=16,'pcol'=16] {'prow'}, use_global_device_ids=true, to_apply=%region_6.7 | all-reduce | flops 256 | bytes 2048 | tf_op jit(solution)/shard_map/psum | solution.py:13
  377.0 30.5 %psum.119 = f32[512]{0:T(512)S(1)} all-reduce(f32[512]{0:T(512)S(1)} %slice.112), channel_id=1, replica_groups=mesh['prow'=16,'pcol'=16] {'pcol'}, use_global_device_ids=true, to_apply=%region_7.8 | all-reduce | flops 512 | bytes 4096 | tf_op jit(solution)/shard_map/psum | solution.py:87
  408.4 30.4 %psum.120 = f32[256]{0:T(256)S(1)} all-reduce(f32[256]{0:T(256)S(1)} %broadcast_select_fusion.4), channel_id=1, replica_groups=mesh['prow'=16,'pcol'=16] {'prow'}, use_global_device_ids=true, to_apply=%region_8.9 | all-reduce | flops 256 | bytes 2048 | tf_op jit(solution)/shard_map/psum | solution.py:13
  439.8 30.8 %psum.121 = f32[512]{0:T(512)S(1)} all-reduce(f32[512]{0:T(512)S(1)} %slice.113), channel_id=1, replica_groups=mesh['prow'=16,'pcol'=16] {'pcol'}, use_global_device_ids=true, to_apply=%region_9.10 | all-reduce | flops 512 | bytes 4096 | tf_op jit(solution)/shard_map/psum | solution.py:87
  471.6 28.6 %psum.122 = f32[256]{0:T(256)S(1)} all-reduce(f32[256]{0:T(256)S(1)} %broadcast_select_fusion.3), channel_id=1, replica_groups=mesh['prow'=16,'pcol'=16] {'prow'}, use_global_device_ids=true, to_apply=%region_10.11 | all-reduce | flops 256 | bytes 2048 | tf_op jit(solution)/shard_map/psum | solution.py:13
  501.1 30.5 %psum.123 = f32[512]{0:T(512)S(1)} all-reduce(f32[512]{0:T(512)S(1)} %slice.114), channel_id=1, replica_groups=mesh['prow'=16,'pcol'=16] {'pcol'}, use_global_device_ids=true, to_apply=%region_11.12 | all-reduce | flops 512 | bytes 4096 | tf_op jit(solution)/shard_map/psum | solution.py:87
  532.5 30.2 %psum.124 = f32[256]{0:T(256)S(1)} all-reduce(f32[256]{0:T(256)S(1)} %broadcast_select_fusion.2), channel_id=1, replica_groups=mesh['prow'=16,'pcol'=16] {'prow'}, use_global_device_ids=true, to_apply=%region_12.13 | all-reduce | flops 256 | bytes 2048 | tf_op jit(solution)/shard_map/psum | solution.py:13
  563.7 30.8 %psum.125 = f32[512]{0:T(512)S(1)} all-reduce(f32[512]{0:T(512)S(1)} %slice.115), channel_id=1, replica_groups=mesh['prow'=16,'pcol'=16] {'pcol'}, use_global_device_ids=true, to_apply=%region_13.14 | all-reduce | flops 512 | bytes 4096 | tf_op jit(solution)/shard_map/psum | solution.py:87
  595.4 28.6 %psum.126 = f32[256]{0:T(256)S(1)} all-reduce(f32[256]{0:T(256)S(1)} %broadcast_select_fusion.1), channel_id=1, replica_groups=mesh['prow'=16,'pcol'=16] {'prow'}, use_global_device_ids=true, to_apply=%region_14.15 | all-reduce | flops 256 | bytes 2048 | tf_op jit(solution)/shard_map/psum | solution.py:13
  624.9 30.5 %psum.127 = f32[512]{0:T(512)S(1)} all-reduce(f32[512]{0:T(512)S(1)} %slice.116), channel_id=1, replica_groups=mesh['prow'=16,'pcol'=16] {'pcol'}, use_global_device_ids=true, to_apply=%region_15.16 | all-reduce | flops 512 | bytes 4096 | tf_op jit(solution)/shard_map/psum | solution.py:87
  656.3 30.2 %psum.128 = f32[256]{0:T(256)S(1)} all-reduce(f32[256]{0:T(256)S(1)} %broadcast_select_fusion), channel_id=1, replica_groups=mesh['prow'=16,'pcol'=16] {'prow'}, use_global_device_ids=true, to_apply=%region_16.17 | all-reduce | flops 256 | bytes 2048 | tf_op jit(solution)/shard_map/psum | solution.py:13
  687.6 30.8 %psum.129 = f32[512]{0:T(512)S(1)} all-reduce(f32[512]{0:T(512)S(1)} %slice.117), channel_id=1, replica_groups=mesh['prow'=16,'pcol'=16] {'pcol'}, use_global_device_ids=true, to_apply=%region_17.18 | all-reduce | flops 512 | bytes 4096 | tf_op jit(solution)/shard_map/psum | solution.py:87
  719.3 28.6 %psum.130 = f32[256]{0:T(256)S(1)} all-reduce(f32[256]{0:T(256)S(1)} %broadcast_select_fusion.7), channel_id=1, replica_groups=mesh['prow'=16,'pcol'=16] {'prow'}, use_global_device_ids=true, to_apply=%region_18.19 | all-reduce | flops 256 | bytes 2048 | tf_op jit(solution)/shard_map/psum | solution.py:13
  749.4 30.9 %all-reduce.1 = f32[2048]{0:T(1024)S(1)} all-reduce(f32[2048]{0:T(1024)S(1)} %multiply_add_fusion), channel_id=2, replica_groups=mesh['prow'=16,'pcol'=16] {'pcol'}, use_global_device_ids=true, to_apply=%region_19.20.clone | all-reduce | flops 2048 | bytes 16384
  (291 shorter events, 44.0 us)
Async XLA Ops:
  0.6 314.4 %copy-start = (bf16[2048,256]{1,0:T(8,128)(2,1)S(1)}, bf16[2048,256]{1,0:T(8,128)(2,1)}, u32[]{:S(2)}) copy-start(bf16[2048,256]{1,0:T(8,128)(2,1)} %param.13) | copy-start | bytes 3145732
  56.9 226.4 %copy-start.3 = (f32[2048]{0:T(1024)S(1)}, f32[2048]{0:T(1024)}, u32[]{:S(2)}) copy-start(f32[2048]{0:T(1024)} %param.12) | copy-start | bytes 24580
  56.9 226.4 %copy-start.1 = (bf16[256,512]{1,0:T(8,128)(2,1)S(1)}, bf16[256,512]{1,0:T(8,128)(2,1)}, u32[]{:S(2)}) copy-start(bf16[256,512]{1,0:T(8,128)(2,1)} %param.15) | copy-start | bytes 786436
  56.9 259.1 %copy-start.2 = (f32[4,8]{1,0:T(4,128)S(1)}, f32[4,8]{1,0:T(4,128)}, u32[]{:S(2)}) copy-start(f32[4,8]{1,0:T(4,128)} %param.14) | copy-start | bytes 388
  242.6 537.7 %copy-start.4 = (u32[256]{0:T(256)S(1)}, u32[256]{0:T(256)}, u32[]{:S(2)}) copy-start(u32[256]{0:T(256)} %constant.330) | copy-start | bytes 3076
where the time goes:
time: 794 us; the launch traced here: 782 us
  blocking collectives  571 us (72%)
  matrix products  125 us (16%)
  other arithmetic  69.6 us (9%)
  between operations  8.26 us (1%)
    psum x8, blocking collectives, from_root(): return lax.psum(kept, axis)  236 us
    psum x7, blocking collectives, body(): diag_rows = base_tile - lax.psum(pending_tile, 'pcol')  214 us
    dot_general x16, matrix products, column_block(): jnp.dot(block, entries, precision=lax.Precision.HIGHEST, preferred_elemen...  115 us
    unnamed x2, blocking collectives  81.2 us
    mul x16, other arithmetic, scramble(): lax.shift_right_logical(mixed, jnp.int32(8)).astype(jnp.float32)  52.1 us
    psum x1, blocking collectives, body(): baseline = rhs - lax.psum(partial_rows, 'pcol')  40.7 us

commit v1 on v0

v1 whole, which is shorter than its diff:
```python
import functools

import jax
import jax.numpy as jnp
from jax import lax
from jax.experimental import pallas as pl
from jax.experimental.pallas import tpu as pltpu
from jax.sharding import PartitionSpec as P

NB = 512
KB = 8
RT_DEV = 4
CT_DEV = 25
GRID = 16
ROWS = RT_DEV * NB
LANES = 128
GROUPS = NB // LANES
STRIP = 32
UNIT = 2.0 ** -40

VMEM = pl.BlockSpec(memory_space=pltpu.VMEM)
SMEM = pl.BlockSpec(memory_space=pltpu.SMEM)
BIG = 48 * 1024 * 1024


def shift_right(value, amount):
    return lax.shift_right_logical(value, jnp.full_like(value, amount))


def signed_hash(mixed):
    mixed = mixed ^ shift_right(mixed, 15)
    mixed = mixed * jnp.int32(747796405)
    mixed = mixed ^ shift_right(mixed, 13)
    mixed = mixed * jnp.int32(1274126177)
    return (mixed ^ jnp.int32(-2147483648)) ^ shift_right(mixed, 16)


def hash_kernel(first_row, rows, with_sum, seeds, v, acc_out, *sum_out):
    slot = lax.axis_index("prow") * RT_DEV
    bias = jnp.sum(v[...], axis=0, keepdims=True) * jnp.float32(-127.5)

    def strip(number, carry):
        row = first_row + number * STRIP
        tile = row // NB
        inner = row % NB
        t = (inner + lax.broadcasted_iota(jnp.int32, (STRIP, LANES), 0)) * jnp.int32(NB)
        u = lax.broadcasted_iota(jnp.int32, (STRIP, LANES), 1)
        base = [(t + u + jnp.int32(LANES * g)) * jnp.int32(1103515245) for g in range(GROUPS)]
        accs = [jnp.zeros((STRIP, LANES), jnp.float32) for _ in range(GROUPS)]
        accs[0] = accs[0] + bias
        for j in range(CT_DEV):
            seed = seeds[slot + tile, j]
            for g in range(GROUPS):
                entries = jnp.broadcast_to(v[pl.ds(GROUPS * j + g, 1), :], (STRIP, LANES))
                accs[g] = accs[g] + signed_hash(base[g] + seed).astype(jnp.float32) * entries
        total = (accs[0] + accs[1]) + (accs[2] + accs[3])
        acc_out[pl.ds(pl.multiple_of(number * STRIP, STRIP), STRIP), :] = total
        return carry

    lax.fori_loop(0, rows // STRIP, strip, 0)
    if with_sum:
        sum_out[0][...] = jnp.sum(acc_out[...].T, axis=0, keepdims=True)


def hash_rows(seeds, v, first_row, rows, with_sum=False):
    shapes = [jax.ShapeDtypeStruct((rows, LANES), jnp.float32)]
    if with_sum:
        shapes.append(jax.ShapeDtypeStruct((1, rows), jnp.float32))
    work = rows * CT_DEV * NB
    return pl.pallas_call(
        functools.partial(hash_kernel, first_row, rows, with_sum),
        out_shape=shapes,
        in_specs=[SMEM, VMEM],
        out_specs=[VMEM] * len(shapes),
        cost_estimate=pl.CostEstimate(flops=work * 14, bytes_accessed=rows * LANES * 4, transcendentals=0),
        name=f"hash_{first_row}",
    )(seeds, v)


def step_kernel(k, residual, *refs):
    if k == 0:
        inv, tiles, total_out, solved_out = refs
    else:
        same, other, solved_in, inv, tiles, total_out, solved_out = refs
    col = lax.axis_index("pcol")
    mine = col // 2 == k

    @pl.when(mine)
    def _():
        s = residual[...]
        if k > 0:
            running = same[...] + other[...]
            s = s - running[k:k + 1, :]
        y = jnp.sum(inv[...].astype(jnp.float32) * s, axis=1, keepdims=True)
        eye = lax.broadcasted_iota(jnp.int32, (256, 256), 0) == lax.broadcasted_iota(jnp.int32, (256, 256), 1)
        solved_out[...] = jnp.sum(jnp.where(eye, y, 0.0), axis=0, keepdims=True)
        if k < KB - 1:
            rows = [jnp.zeros((1, NB), jnp.float32)] * (k + 1)
            for kk in range(k + 1, KB):
                part = jnp.zeros((16, NB), jnp.float32)
                for j in range(GRID):
                    part = part + tiles[j, kk - 1] * y[16 * j:16 * j + 16]
                rows.append(jnp.sum(part, axis=0, keepdims=True))
            update = jnp.concatenate(rows, axis=0)
            if k > 0:
                update = update + jnp.where(col % 2 == 0, running, 0.0)
            total_out[...] = update

    @pl.when(jnp.logical_not(mine))
    def _():
        if k > 0:
            solved_out[...] = solved_in[...]
        else:
            solved_out[...] = jnp.zeros_like(solved_out)
        if k < KB - 1:
            total_out[...] = jnp.zeros_like(total_out)


def step(k, residual, running, solved, inv, tiles):
    args = (residual,) if k == 0 else (residual, running[0], running[1], solved)
    return pl.pallas_call(
        functools.partial(step_kernel, k),
        out_shape=[jax.ShapeDtypeStruct((KB, NB), jnp.float32), jax.ShapeDtypeStruct((1, 256), jnp.float32)],
        in_specs=[VMEM] * (len(args) + 2),
        out_specs=[VMEM] * 2,
        compiler_params=pltpu.CompilerParams(vmem_limit_bytes=BIG),
        name=f"step_{k}",
    )(*args, inv, tiles)


def last_kernel(count, factor, solved, panel, *refs):
    accs, out = refs[:count], refs[count]
    y = solved[...]
    row = 0
    for acc in accs:
        rows = acc.shape[0]
        for at in range(0, rows, LANES):
            part = panel[row + at:row + at + LANES, :].astype(jnp.float32) * y
            part = (part[:, :LANES] + part[:, LANES:]) * factor[(row + at) // NB]
            part = part + acc[at:at + LANES, :] * jnp.float32(UNIT)
            out[(row + at) // LANES, :] = jnp.sum(part.T, axis=0)
        row += rows


def last(factor, solved, panel, accs):
    return pl.pallas_call(
        functools.partial(last_kernel, len(accs)),
        out_shape=jax.ShapeDtypeStruct((GRID, LANES), jnp.float32),
        in_specs=[SMEM] + [VMEM] * (2 + len(accs)),
        out_specs=VMEM,
        compiler_params=pltpu.CompilerParams(vmem_limit_bytes=BIG),
        name="last",
    )(factor, solved, panel, *accs)


def to_all(value, axis):
    return lax.all_to_all(jnp.broadcast_to(value[None], (GRID,) + value.shape), axis, 0, 0, tiled=True)


def after(value, *others):
    return lax.optimization_barrier((value,) + others)[0]


def body(seeds, tile_owner, vector, rhs, panel, tile_scales, inverses):
    row_index = lax.axis_index("prow")
    col_index = lax.axis_index("pcol")
    anchor = tile_owner[0]
    block = col_index // 2
    first_tile = jnp.mod(row_index - anchor, GRID)
    my_tiles = jnp.arange(RT_DEV, dtype=jnp.int32) * GRID + first_tile
    scales = lax.dynamic_slice_in_dim(tile_scales, block, 1, 1)[:, 0]
    factor = jnp.where(my_tiles > block, scales, jnp.float32(0.0))

    v = to_all(vector, "prow").reshape(CT_DEV * GROUPS, LANES)
    scaled = (panel[:NB].astype(jnp.float32) * factor[0]).T.reshape(GRID, GRID, NB)
    spread = lax.all_to_all(scaled, "prow", 0, 0, tiled=True)
    own = lax.dynamic_slice_in_dim(jnp.concatenate([spread, spread]), anchor + 1, KB - 1, 0)
    tiles = to_all(own, "prow")

    acc0, sum0 = hash_rows(seeds, v, 0, NB, True)
    entries = jnp.where(first_tile == col_index, v.reshape(CT_DEV, NB)[:RT_DEV].reshape(ROWS), 0.0)
    given = jnp.where(col_index == 0, rhs, 0.0) - entries

    part = given[:NB] - sum0[0] * jnp.float32(UNIT)
    gathered = to_all(part, "prow")
    acc1 = hash_rows(seeds, after(v, part), NB, 384)[0]
    blocks = lax.dynamic_slice_in_dim(jnp.concatenate([gathered, gathered]), anchor, KB, 0)
    blocks = after(jnp.repeat(blocks, 2, axis=0), acc1)
    parts = lax.all_to_all(blocks, "pcol", 0, 0, tiled=True)
    acc2 = hash_rows(seeds, after(v, blocks), NB + 384, 384)[0]
    residual = after(jnp.sum(parts, axis=0, keepdims=True), acc2)

    accs = [acc0, acc1, acc2]
    running, solved = None, None
    row = NB + 768
    for k in range(KB):
        total, solved = step(k, residual, running, solved, inverses, tiles)
        if k == KB - 1:
            break
        same = lax.ppermute(total, "pcol", [(2 * k + h, 2 * k + 2 + h) for h in range(2)])
        other = lax.ppermute(total, "pcol", [(2 * k + h, 2 * k + 3 - h) for h in range(2)])
        if row < ROWS:
            accs.append(hash_rows(seeds, after(v, total), row, 128)[0])
            row += 128
            same = after(same, accs[-1])
        running = (same, other)

    sums = given.reshape(GRID, LANES) - last(factor, solved, panel, accs)
    updated = jnp.sum(lax.all_to_all(sums, "pcol", 0, 0, tiled=True), axis=0)
    return (solved.reshape(256), updated)


def solution(mesh):
    placed = (
        P(None, "pcol"),
        P(),
        P(("pcol", "prow")),
        P("prow"),
        P("prow", "pcol"),
        P("prow", None),
        P("pcol", None),
    )
    return jax.shard_map(
        body,
        mesh=mesh,
        in_specs=placed,
        out_specs=(P("pcol"), P(("prow", "pcol"))),
        check_vma=False,
    )
```

time: 794 us -> 216 us (0.27); the launches traced: 782 us -> 214 us
  blocking collectives: 571 us -> 11.7 us
  matrix products: 125 us -> 0 us
  Pallas kernels: 0 us -> 81.1 us
  other arithmetic: 69.6 us -> 2.37 us
  waiting for transfers between devices: 0 us -> 56.6 us
  starting transfers between devices: 0 us -> 51.2 us
    psum x16 -> x0, blocking collectives: 490 us -> none  [the longest x8 236 us: from_root(): return lax.psum(kept, axis)]
    dot_general x32 -> x0, matrix products: 125 us -> none  [the longest x16 115 us: column_block(): jnp.dot(block, entries, precision=lax.Precision.HIGHEST, preferred_elemen...]
    unnamed x2 -> x0, blocking collectives: 81.2 us -> none
    pallas_call x0 -> x18, Pallas kernels: none -> 81.1 us  [the longest x9 62.7 us: hash_rows(): pl.pallas_call(functools.partial(hash_kernel, first_row, rows, with_sum),...]
    all_to_all x0 -> x5, waiting for transfers between devices: none -> 56.5 us  [the longest x3 49.2 us: to_all(): lax.all_to_all(jnp.broadcast_to(value[None], (GRID,) + value.shape), axis...]
    mul x65 -> x2, other arithmetic: 55.3 us -> 1.55 us  [the longest x1 0.88 us: body(): panel[:NB].astype(jnp.float32) * factor[0]]
    all_to_all x0 -> x5, starting transfers between devices: none -> 38.8 us  [the longest x3 20 us: to_all(): lax.all_to_all(jnp.broadcast_to(value[None], (GRID,) + value.shape), axis...]
    ppermute x0 -> x14, starting transfers between devices: none -> 12.4 us  [the longest x7 6.71 us: body(): lax.ppermute(total, 'pcol', [(2 * k + h, 2 * k + 3 - h) for h in range(2)])]
  transfers between devices with their start and end apart: 0 -> 19, of which waited for: 0 -> 3; matrix products, arithmetic and copies ran while one was open for 0% -> 2% of each run, Pallas kernels for 0% -> 23%
where the time goes in v1:
time: 216 us; the launch traced here: 214 us
  Pallas kernels  81.1 us (38%)
  waiting for transfers between devices  56.6 us (26%)
  starting transfers between devices  51.2 us (24%)
  blocking collectives  11.7 us (5%)
  local copies, waits for them, and re-layouts  9.16 us (4%)
  other arithmetic  2.37 us (1%)
    pallas_call x9, Pallas kernels, hash_rows(): pl.pallas_call(functools.partial(hash_kernel, first_row, rows, with_sum),...  62.7 us
    all_to_all x3, waiting for transfers between devices, to_all(): lax.all_to_all(jnp.broadcast_to(value[None], (GRID,) + value.shape), axis...  49.2 us
    all_to_all x3, starting transfers between devices, to_all(): lax.all_to_all(jnp.broadcast_to(value[None], (GRID,) + value.shape), axis...  20 us
    pallas_call x8, Pallas kernels, step(): pl.pallas_call(functools.partial(step_kernel, k), out_shape=[jax.ShapeDty...  17.5 us
    all_to_all x1, starting transfers between devices, body(): parts = lax.all_to_all(blocks, 'pcol', 0, 0, tiled=True)  11.9 us
    all_to_all x1, blocking collectives, body(): updated = jnp.sum(lax.all_to_all(sums, 'pcol', 0, 0, tiled=True), axis=0)  11.7 us
    all_to_all x1, waiting for transfers between devices, body(): parts = lax.all_to_all(blocks, 'pcol', 0, 0, tiled=True)  7.34 us
    all_to_all x1, starting transfers between devices, body(): spread = lax.all_to_all(scaled, 'prow', 0, 0, tiled=True)  6.97 us
  transfers between devices with their start and end apart: 19, of which 3 were waited for; matrix products, arithmetic and copies ran while one was open for 2% of the time, Pallas kernels for 23%

profile of v1, /device:TPU:29, one launch (start us, length us, event | category | flops | bytes accessed | tf_op | source)
XLA Modules:
  0.0 214.1 jit_solution(12137485874081553907)
XLA Ops:
  0.7 1.3 broadcast_in_dim.36
  2.0 6.6 %all-to-all-start = ((f32[16,1,800]{2,1,0:T(1,128)}), f32[16,1,800]{2,1,0:T(1,128)S(1)}, u32[]{:S(2)}, u32[]{:S(2)}) async-start(f32[16,1,800]{2,1,0:T(1,128)} %broadcast_in_dim.36), calls=%async_computation | async-start | bytes 114688 | tf_op jit(solution)/shard_map/all_to_all | solution.py:157
  9.4 1.0 slice.18
  10.6 1.4 copy.40.seeds
  12.2 0.7 reshape.44.v
  12.9 13.4 %hash_0.1 = (f32[512,128]{1,0:T(8,128)}, f32[1,512]{1,0:T(1,128)}) custom-call(s32[64,25]{1,0:T(8,128)} %copy.40.seeds, f32[100,128]{1,0:T(8,128)} %reshape.44.v), custom_call_target="tpu_custom_call" | custom-call | flops 91750400 | bytes 262144 | tf_op jit(solution)/shard_map/hash_0/pallas_call | solution.py:70
  26.4 0.7 broadcast_multiply_fusion
  27.7 6.7 %all-to-all-start.1 = ((f32[16,1,512]{2,1,0:T(1,128)}), f32[16,1,512]{2,1,0:T(1,128)S(1)}, u32[]{:S(2)}, u32[]{:S(2)}) async-start(f32[16,1,512]{2,1,0:T(1,128)} %broadcast_in_dim.38), calls=%async_computation.1 | async-start | bytes 65536 | tf_op jit(solution)/shard_map/all_to_all | solution.py:157
  34.4 0.9 convert_multiply_fusion
  35.2 2.1 %all-to-all-done.1 = f32[16,1,512]{2,1,0:T(1,128)S(1)} async-done(((f32[16,1,512]{2,1,0:T(1,128)}), f32[16,1,512]{2,1,0:T(1,128)S(1)}, u32[]{:S(2)}, u32[]{:S(2)}) %all-to-all-start.1) | async-done | bytes 32800 | tf_op jit(solution)/shard_map/all_to_all | solution.py:157
  37.4 7.0 %all-to-all-start.3 = ((f32[16,16,512]{2,1,0:T(8,128)}), f32[16,16,512]{2,1,0:T(8,128)S(1)}, u32[]{:S(2)}, u32[]{:S(2)}) async-start(f32[16,16,512]{2,1,0:T(8,128)} %bitcast.5), calls=%async_computation.3 | async-start | bytes 1048576 | tf_op jit(solution)/shard_map/all_to_all | solution.py:176
  44.5 10.5 %hash_512.1.refs_1_ = f32[384,128]{1,0:T(8,128)} custom-call(s32[64,25]{1,0:T(8,128)} %copy.40.seeds, f32[100,128]{1,0:T(8,128)} %reshape.44.v), custom_call_target="tpu_custom_call" | custom-call | flops 68812800 | bytes 196608 | tf_op jit(solution)/shard_map/hash_512/pallas_call | solution.py:70
  55.8 11.9 %all-to-all-start.2 = ((f32[16,1,512]{2,1,0:T(1,128)}), f32[16,1,512]{2,1,0:T(1,128)S(1)}, u32[]{:S(2)}, u32[]{:S(2)}) async-start(f32[16,1,512]{2,1,0:T(1,128)} %all_to_all.31), calls=%async_computation.2 | async-start | bytes 65536 | tf_op jit(solution)/shard_map/all_to_all | solution.py:189
  67.7 7.3 %all-to-all-done.2 = f32[16,1,512]{2,1,0:T(1,128)S(1)} async-done(((f32[16,1,512]{2,1,0:T(1,128)}), f32[16,1,512]{2,1,0:T(1,128)S(1)}, u32[]{:S(2)}, u32[]{:S(2)}) %all-to-all-start.2) | async-done | bytes 32800 | tf_op jit(solution)/shard_map/all_to_all | solution.py:189
  75.0 2.3 %broadcast_in_dim.42 = f32[16,7,16,512]{3,2,1,0:T(8,128)} broadcast(f32[7,16,512]{2,1,0:T(8,128)S(1)} %fusion), dimensions={1,2,3} | broadcast | bytes 3899392 | tf_op jit(solution)/shard_map/broadcast_in_dim | solution.py:157
  77.3 6.8 %all-to-all-start.4 = ((f32[16,7,16,512]{3,2,1,0:T(8,128)}), f32[16,7,16,512]{3,2,1,0:T(8,128)}, u32[]{:S(2)}, u32[]{:S(2)}) async-start(f32[16,7,16,512]{3,2,1,0:T(8,128)} %broadcast_in_dim.42), calls=%async_computation.4 | async-start | bytes 7340032 | tf_op jit(solution)/shard_map/all_to_all | solution.py:157
  84.1 10.5 %hash_896.1.refs_2_ = f32[384,128]{1,0:T(8,128)} custom-call(s32[64,25]{1,0:T(8,128)} %copy.40.seeds, f32[100,128]{1,0:T(8,128)} %reshape.44.v), custom_call_target="tpu_custom_call" | custom-call | flops 68812800 | bytes 196608 | tf_op jit(solution)/shard_map/hash_896/pallas_call | solution.py:70
  94.7 47.1 %all-to-all-done.4.refs_1_.refs_4_ = f32[16,7,16,512]{3,2,1,0:T(8,128)} async-done(((f32[16,7,16,512]{3,2,1,0:T(8,128)}), f32[16,7,16,512]{3,2,1,0:T(8,128)}, u32[]{:S(2)}, u32[]{:S(2)}) %all-to-all-start.4) | async-done | bytes 3670048 | tf_op jit(solution)/shard_map/all_to_all | solution.py:157
  141.7 2.4 %step_0.1 = (f32[8,512]{1,0:T(8,128)S(1)}, f32[1,256]{1,0:T(1,128)S(1)}) custom-call(f32[1,512]{1,0:T(1,128)S(1)} %bitcast.21, bf16[256,512]{1,0:T(8,128)(2,1)S(1)} %copy-done.1, f32[16,7,16,512]{3,2,1,0:T(8,128)} %all-to-all-done.4.refs_1_.refs_4_), custom_call_target="tpu_custom_call" | custom-call | tf_op jit(solution)/shard_map/step_0/pallas_call | solution.py:121
  144.2 1.8 collective-permute-start
  146.0 2.7 %collective-permute-start.1 = (f32[8,512]{1,0:T(8,128)S(1)}, f32[8,512]{1,0:T(8,128)S(1)}, u32[]{:S(2)}, u32[]{:S(2)}) collective-permute-start(f32[8,512]{1,0:T(8,128)S(1)} %get-tuple-element.40), channel_id=1, source_target_pairs={{0,3},{1,2},{16,19},{17,18},{32,35},{33,34},{48,51},{49,50},{64,67... | collective-permute-start | bytes 49160 | tf_op jit(solution)/shard_map/ppermute | solution.py:201
  148.7 4.7 %hash_1280.1.refs_3_ = f32[128,128]{1,0:T(8,128)} custom-call(s32[64,25]{1,0:T(8,128)} %copy.40.seeds, f32[100,128]{1,0:T(8,128)} %reshape.44.v), custom_call_target="tpu_custom_call" | custom-call | flops 22937600 | bytes 65536 | tf_op jit(solution)/shard_map/hash_1280/pallas_call | solution.py:70
  153.4 2.0 step_1.1
  155.4 0.7 collective-permute-start.2
  156.1 0.7 collective-permute-start.3
  156.8 4.7 %hash_1408.1.refs_4_ = f32[128,128]{1,0:T(8,128)} custom-call(s32[64,25]{1,0:T(8,128)} %copy.40.seeds, f32[100,128]{1,0:T(8,128)} %reshape.44.v), custom_call_target="tpu_custom_call" | custom-call | flops 22937600 | bytes 65536 | tf_op jit(solution)/shard_map/hash_1408/pallas_call | solution.py:70
  161.5 2.0 step_2.1
  163.5 0.7 collective-permute-start.4
  164.2 0.7 collective-permute-start.5
  164.9 4.7 %hash_1536.1.refs_5_ = f32[128,128]{1,0:T(8,128)} custom-call(s32[64,25]{1,0:T(8,128)} %copy.40.seeds, f32[100,128]{1,0:T(8,128)} %reshape.44.v), custom_call_target="tpu_custom_call" | custom-call | flops 22937600 | bytes 65536 | tf_op jit(solution)/shard_map/hash_1536/pallas_call | solution.py:70
  169.6 2.0 step_3.1
  171.6 0.7 collective-permute-start.6
  172.3 0.7 collective-permute-start.7
  172.9 4.7 %hash_1664.1.refs_6_ = f32[128,128]{1,0:T(8,128)} custom-call(s32[64,25]{1,0:T(8,128)} %copy.40.seeds, f32[100,128]{1,0:T(8,128)} %reshape.44.v), custom_call_target="tpu_custom_call" | custom-call | flops 22937600 | bytes 65536 | tf_op jit(solution)/shard_map/hash_1664/pallas_call | solution.py:70
  177.7 2.0 step_4.1
  179.7 0.7 collective-permute-start.8
  180.4 0.7 collective-permute-start.9
  181.0 4.7 %hash_1792.1.refs_7_ = f32[128,128]{1,0:T(8,128)} custom-call(s32[64,25]{1,0:T(8,128)} %copy.40.seeds, f32[100,128]{1,0:T(8,128)} %reshape.44.v), custom_call_target="tpu_custom_call" | custom-call | flops 22937600 | bytes 65536 | tf_op jit(solution)/shard_map/hash_1792/pallas_call | solution.py:70
  185.7 2.0 step_5.1
  187.8 0.7 collective-permute-start.10
  188.4 0.7 collective-permute-start.11
  189.1 4.7 %hash_1920.1.refs_8_ = f32[128,128]{1,0:T(8,128)} custom-call(s32[64,25]{1,0:T(8,128)} %copy.40.seeds, f32[100,128]{1,0:T(8,128)} %reshape.44.v), custom_call_target="tpu_custom_call" | custom-call | flops 22937600 | bytes 65536 | tf_op jit(solution)/shard_map/hash_1920/pallas_call | solution.py:70
  193.9 2.2 %step_6.1 = (f32[8,512]{1,0:T(8,128)S(1)}, f32[1,256]{1,0:T(1,128)S(1)}) custom-call(f32[1,512]{1,0:T(1,128)S(1)} %bitcast.27, f32[8,512]{1,0:T(8,128)S(1)} %collective-permute-done.10.refs_0_, f32[8,512]{1,0:T(8,128)S(1)} %collective-permute-done.11.refs_1_, f32[1,256]{1,0:T(1,128)S(1)} %get-tuple-element.63.refs_2_, bf16[256,512]{1,0:T(8,128)(2,1)S(1)} %copy-done.1, ...), custom_call_target="tpu_custom_call" | custom-call | tf_op jit(solution)/shard_map/step_6/pallas_call | solution.py:121
  196.8 0.7 collective-permute-start.13
  197.4 2.6 %step_7.1 = (f32[8,512]{1,0:T(8,128)}, f32[1,256]{1,0:T(1,128)}) custom-call(f32[1,512]{1,0:T(1,128)S(1)} %bitcast.28, f32[8,512]{1,0:T(8,128)S(1)} %collective-permute-done.12.refs_0_, f32[8,512]{1,0:T(8,128)S(1)} %collective-permute-done.13.refs_1_, f32[1,256]{1,0:T(1,128)S(1)} %get-tuple-element.65.refs_2_, bf16[256,512]{1,0:T(8,128)(2,1)S(1)} %copy-done.1, ...), custom_call_target="tpu_custom_call" | custom-call | tf_op jit(solution)/shard_map/step_7/pallas_call | solution.py:121
  200.2 0.7 copy-done.12
  200.8 0.9 last.1
  201.8 11.7 %all_to_all.43 = f32[16,1,128]{2,1,0:T(1,128)S(1)} all-to-all(f32[16,1,128]{2,1,0:T(1,128)S(1)} %bitcast.33), channel_id=1, replica_groups=mesh['prow'=16,'pcol'=16] {'pcol'}, dimensions={0} | all-to-all | bytes 16384 | tf_op jit(solution)/shard_map/all_to_all | solution.py:209
  (63 shorter events, 3.3 us)
Async XLA Ops:
  0.6 8.6 %copy-start = (f32[4,8]{1,0:T(4,128)S(1)}, f32[4,8]{1,0:T(4,128)}, u32[]{:S(2)}) copy-start(f32[4,8]{1,0:T(4,128)} %param.12) | copy-start | bytes 388
  0.6 43.7 %copy-start.13 = (s32[64]{0:T(128)S(1)}, s32[64]{0:T(128)}, u32[]{:S(2)}) copy-start(s32[64]{0:T(128)} %param.8) | copy-start | bytes 772
  2.0 10.0 %all-to-all-start = ((f32[16,1,800]{2,1,0:T(1,128)}), f32[16,1,800]{2,1,0:T(1,128)S(1)}, u32[]{:S(2)}, u32[]{:S(2)}) async-start(f32[16,1,800]{2,1,0:T(1,128)} %broadcast_in_dim.36), calls=%async_computation | async-start | bytes 114688 | tf_op jit(solution)/shard_map/all_to_all | solution.py:157
  27.7 9.7 %all-to-all-start.1 = ((f32[16,1,512]{2,1,0:T(1,128)}), f32[16,1,512]{2,1,0:T(1,128)S(1)}, u32[]{:S(2)}, u32[]{:S(2)}) async-start(f32[16,1,512]{2,1,0:T(1,128)} %broadcast_in_dim.38), calls=%async_computation.1 | async-start | bytes 65536 | tf_op jit(solution)/shard_map/all_to_all | solution.py:157
  37.4 18.4 %all-to-all-start.3 = ((f32[16,16,512]{2,1,0:T(8,128)}), f32[16,16,512]{2,1,0:T(8,128)S(1)}, u32[]{:S(2)}, u32[]{:S(2)}) async-start(f32[16,16,512]{2,1,0:T(8,128)} %bitcast.5), calls=%async_computation.3 | async-start | bytes 1048576 | tf_op jit(solution)/shard_map/all_to_all | solution.py:176
  55.8 19.2 %all-to-all-start.2 = ((f32[16,1,512]{2,1,0:T(1,128)}), f32[16,1,512]{2,1,0:T(1,128)S(1)}, u32[]{:S(2)}, u32[]{:S(2)}) async-start(f32[16,1,512]{2,1,0:T(1,128)} %all_to_all.31), calls=%async_computation.2 | async-start | bytes 65536 | tf_op jit(solution)/shard_map/all_to_all | solution.py:189
  77.3 64.4 %copy-start.1 = (bf16[256,512]{1,0:T(8,128)(2,1)S(1)}, bf16[256,512]{1,0:T(8,128)(2,1)}, u32[]{:S(2)}) copy-start(bf16[256,512]{1,0:T(8,128)(2,1)} %refs_3_.13) | copy-start | bytes 786436
  77.3 64.4 %all-to-all-start.4 = ((f32[16,7,16,512]{3,2,1,0:T(8,128)}), f32[16,7,16,512]{3,2,1,0:T(8,128)}, u32[]{:S(2)}, u32[]{:S(2)}) async-start(f32[16,7,16,512]{3,2,1,0:T(8,128)} %broadcast_in_dim.42), calls=%async_computation.4 | async-start | bytes 7340032 | tf_op jit(solution)/shard_map/all_to_all | solution.py:157
  144.2 9.2 %collective-permute-start = (f32[8,512]{1,0:T(8,128)S(1)}, f32[8,512]{1,0:T(8,128)S(1)}, u32[]{:S(2)}, u32[]{:S(2)}) collective-permute-start(f32[8,512]{1,0:T(8,128)S(1)} %get-tuple-element.40), channel_id=1, source_target_pairs={{0,2},{1,3},{16,18},{17,19},{32,34},{33,35},{48,50},{49,51},{64,66... | collective-permute-start | bytes 49160 | tf_op jit(solution)/shard_map/ppermute | solution.py:200
  146.0 7.5 %collective-permute-start.1 = (f32[8,512]{1,0:T(8,128)S(1)}, f32[8,512]{1,0:T(8,128)S(1)}, u32[]{:S(2)}, u32[]{:S(2)}) collective-permute-start(f32[8,512]{1,0:T(8,128)S(1)} %get-tuple-element.40), channel_id=1, source_target_pairs={{0,3},{1,2},{16,19},{17,18},{32,35},{33,34},{48,51},{49,50},{64,67... | collective-permute-start | bytes 49160 | tf_op jit(solution)/shard_map/ppermute | solution.py:201
  155.4 6.0 %collective-permute-start.2 = (f32[8,512]{1,0:T(8,128)S(1)}, f32[8,512]{1,0:T(8,128)S(1)}, u32[]{:S(2)}, u32[]{:S(2)}) collective-permute-start(f32[8,512]{1,0:T(8,128)S(1)} %get-tuple-element.44), channel_id=1, source_target_pairs={{2,4},{3,5},{18,20},{19,21},{34,36},{35,37},{50,52},{51,53},{66,68... | collective-permute-start | bytes 49160 | tf_op jit(solution)/shard_map/ppermute | solution.py:200
  156.1 5.4 %collective-permute-start.3 = (f32[8,512]{1,0:T(8,128)S(1)}, f32[8,512]{1,0:T(8,128)S(1)}, u32[]{:S(2)}, u32[]{:S(2)}) collective-permute-start(f32[8,512]{1,0:T(8,128)S(1)} %get-tuple-element.44), channel_id=1, source_target_pairs={{2,5},{3,4},{18,21},{19,20},{34,37},{35,36},{50,53},{51,52},{66,69... | collective-permute-start | bytes 49160 | tf_op jit(solution)/shard_map/ppermute | solution.py:201
  163.5 6.0 %collective-permute-start.4 = (f32[8,512]{1,0:T(8,128)S(1)}, f32[8,512]{1,0:T(8,128)S(1)}, u32[]{:S(2)}, u32[]{:S(2)}) collective-permute-start(f32[8,512]{1,0:T(8,128)S(1)} %get-tuple-element.48), channel_id=1, source_target_pairs={{4,6},{5,7},{20,22},{21,23},{36,38},{37,39},{52,54},{53,55},{68,70... | collective-permute-start | bytes 49160 | tf_op jit(solution)/shard_map/ppermute | solution.py:200
  164.2 5.4 %collective-permute-start.5 = (f32[8,512]{1,0:T(8,128)S(1)}, f32[8,512]{1,0:T(8,128)S(1)}, u32[]{:S(2)}, u32[]{:S(2)}) collective-permute-start(f32[8,512]{1,0:T(8,128)S(1)} %get-tuple-element.48), channel_id=1, source_target_pairs={{4,7},{5,6},{20,23},{21,22},{36,39},{37,38},{52,55},{53,54},{68,71... | collective-permute-start | bytes 49160 | tf_op jit(solution)/shard_map/ppermute | solution.py:201
  171.6 6.0 %collective-permute-start.6 = (f32[8,512]{1,0:T(8,128)S(1)}, f32[8,512]{1,0:T(8,128)S(1)}, u32[]{:S(2)}, u32[]{:S(2)}) collective-permute-start(f32[8,512]{1,0:T(8,128)S(1)} %get-tuple-element.52), channel_id=1, source_target_pairs={{6,8},{7,9},{22,24},{23,25},{38,40},{39,41},{54,56},{55,57},{70,72... | collective-permute-start | bytes 49160 | tf_op jit(solution)/shard_map/ppermute | solution.py:200
  172.3 5.4 %collective-permute-start.7 = (f32[8,512]{1,0:T(8,128)S(1)}, f32[8,512]{1,0:T(8,128)S(1)}, u32[]{:S(2)}, u32[]{:S(2)}) collective-permute-start(f32[8,512]{1,0:T(8,128)S(1)} %get-tuple-element.52), channel_id=1, source_target_pairs={{6,9},{7,8},{22,25},{23,24},{38,41},{39,40},{54,57},{55,56},{70,73... | collective-permute-start | bytes 49160 | tf_op jit(solution)/shard_map/ppermute | solution.py:201
  179.7 6.0 %collective-permute-start.8 = (f32[8,512]{1,0:T(8,128)S(1)}, f32[8,512]{1,0:T(8,128)S(1)}, u32[]{:S(2)}, u32[]{:S(2)}) collective-permute-start(f32[8,512]{1,0:T(8,128)S(1)} %get-tuple-element.56), channel_id=1, source_target_pairs={{8,10},{9,11},{24,26},{25,27},{40,42},{41,43},{56,58},{57,59},{72,... | collective-permute-start | bytes 49160 | tf_op jit(solution)/shard_map/ppermute | solution.py:200
  180.4 5.4 %collective-permute-start.9 = (f32[8,512]{1,0:T(8,128)S(1)}, f32[8,512]{1,0:T(8,128)S(1)}, u32[]{:S(2)}, u32[]{:S(2)}) collective-permute-start(f32[8,512]{1,0:T(8,128)S(1)} %get-tuple-element.56), channel_id=1, source_target_pairs={{8,11},{9,10},{24,27},{25,26},{40,43},{41,42},{56,59},{57,58},{72,... | collective-permute-start | bytes 49160 | tf_op jit(solution)/shard_map/ppermute | solution.py:201
  187.8 6.0 %collective-permute-start.10 = (f32[8,512]{1,0:T(8,128)S(1)}, f32[8,512]{1,0:T(8,128)S(1)}, u32[]{:S(2)}, u32[]{:S(2)}) collective-permute-start(f32[8,512]{1,0:T(8,128)S(1)} %get-tuple-element.60), channel_id=1, source_target_pairs={{10,12},{11,13},{26,28},{27,29},{42,44},{43,45},{58,60},{59,61},{7... | collective-permute-start | bytes 49160 | tf_op jit(solution)/shard_map/ppermute | solution.py:200
  188.4 5.4 %collective-permute-start.11 = (f32[8,512]{1,0:T(8,128)S(1)}, f32[8,512]{1,0:T(8,128)S(1)}, u32[]{:S(2)}, u32[]{:S(2)}) collective-permute-start(f32[8,512]{1,0:T(8,128)S(1)} %get-tuple-element.60), channel_id=1, source_target_pairs={{10,13},{11,12},{26,29},{27,28},{42,45},{43,44},{58,61},{59,60},{7... | collective-permute-start | bytes 49160 | tf_op jit(solution)/shard_map/ppermute | solution.py:201
  193.8 6.3 %copy-start.2 = (bf16[2048,256]{1,0:T(8,128)(2,1)S(1)}, bf16[2048,256]{1,0:T(8,128)(2,1)}, u32[]{:S(2)}) copy-start(bf16[2048,256]{1,0:T(8,128)(2,1)} %panel.1) | copy-start | bytes 3145732
  193.8 6.3 %copy-start.3 = (f32[384,128]{1,0:T(8,128)S(1)}, f32[384,128]{1,0:T(8,128)}, u32[]{:S(2)}) copy-start(f32[384,128]{1,0:T(8,128)} %hash_512.1.refs_1_) | copy-start | bytes 589828
  193.8 6.3 %copy-start.4 = (f32[384,128]{1,0:T(8,128)S(1)}, f32[384,128]{1,0:T(8,128)}, u32[]{:S(2)}) copy-start(f32[384,128]{1,0:T(8,128)} %hash_896.1.refs_2_) | copy-start | bytes 589828
  193.8 6.2 %copy-start.5 = (f32[512,128]{1,0:T(8,128)S(1)}, f32[512,128]{1,0:T(8,128)}, u32[]{:S(2)}) copy-start(f32[512,128]{1,0:T(8,128)} %get-tuple-element.67.refs_0_) | copy-start | bytes 786436
  193.9 6.2 %copy-start.6 = (f32[128,128]{1,0:T(8,128)S(1)}, f32[128,128]{1,0:T(8,128)}, u32[]{:S(2)}) copy-start(f32[128,128]{1,0:T(8,128)} %hash_1280.1.refs_3_) | copy-start | bytes 196612
  193.9 6.2 %copy-start.7 = (f32[128,128]{1,0:T(8,128)S(1)}, f32[128,128]{1,0:T(8,128)}, u32[]{:S(2)}) copy-start(f32[128,128]{1,0:T(8,128)} %hash_1408.1.refs_4_) | copy-start | bytes 196612
  193.9 6.2 %copy-start.8 = (f32[128,128]{1,0:T(8,128)S(1)}, f32[128,128]{1,0:T(8,128)}, u32[]{:S(2)}) copy-start(f32[128,128]{1,0:T(8,128)} %hash_1536.1.refs_5_) | copy-start | bytes 196612
  193.9 6.2 %copy-start.9 = (f32[128,128]{1,0:T(8,128)S(1)}, f32[128,128]{1,0:T(8,128)}, u32[]{:S(2)}) copy-start(f32[128,128]{1,0:T(8,128)} %hash_1664.1.refs_6_) | copy-start | bytes 196612
  193.9 6.2 %copy-start.10 = (f32[128,128]{1,0:T(8,128)S(1)}, f32[128,128]{1,0:T(8,128)}, u32[]{:S(2)}) copy-start(f32[128,128]{1,0:T(8,128)} %hash_1792.1.refs_7_) | copy-start | bytes 196612
  193.9 6.2 %copy-start.11 = (f32[128,128]{1,0:T(8,128)S(1)}, f32[128,128]{1,0:T(8,128)}, u32[]{:S(2)}) copy-start(f32[128,128]{1,0:T(8,128)} %hash_1920.1.refs_8_) | copy-start | bytes 196612
  196.1 1.3 collective-permute-start.12
  196.8 0.7 collective-permute-start.13
  200.2 0.7 copy-start.12

commit v2 on v1

v2 whole, which is shorter than its diff:
```python
import functools

import jax
import jax.numpy as jnp
from jax import lax
from jax.experimental import pallas as pl
from jax.experimental.pallas import tpu as pltpu
from jax.sharding import PartitionSpec as P

NB = 512
KB = 8
RT_DEV = 4
CT_DEV = 25
GRID = 16
ROWS = RT_DEV * NB
LANES = 128
GROUPS = NB // LANES
STRIP = 32
UNIT = 2.0 ** -40
NEAR = 4
PIECE = 256
WIDE = 64
WINDOW = 7
AHEAD = 2
GAPS = (1, 3, 4, 5)
BIAS = -127.5

VMEM = pl.BlockSpec(memory_space=pltpu.VMEM)
SMEM = pl.BlockSpec(memory_space=pltpu.SMEM)
LIMIT = pltpu.CompilerParams(vmem_limit_bytes=10 * 1024 * 1024)


def shift_right(value, amount):
    return lax.shift_right_logical(value, jnp.full_like(value, amount))


def signed_hash(mixed):
    mixed = mixed ^ shift_right(mixed, 15)
    mixed = mixed * jnp.int32(747796405)
    mixed = mixed ^ shift_right(mixed, 13)
    mixed = mixed * jnp.int32(1274126177)
    return (mixed ^ jnp.int32(-2147483648)) ^ shift_right(mixed, 16)


def weighted(bases, seed, entries, sums):
    return [
        total + signed_hash(base + seed).astype(jnp.float32) * entry
        for base, entry, total in zip(bases, entries, sums)
    ]


def first_kernel(owner, seeds, window, rhs, vector, out, sums):
    row_index, col_index = lax.axis_index("prow"), lax.axis_index("pcol")
    anchor = owner[0]
    my_tile = (row_index - anchor + GRID) & (GRID - 1)
    group = (row_index * 25) >> 2
    bias = jnp.broadcast_to(jnp.sum(window[...], axis=0, keepdims=True) * jnp.float32(BIAS), (WIDE, LANES))
    u = lax.broadcasted_iota(jnp.int32, (WIDE, LANES), 1)
    t = lax.broadcasted_iota(jnp.int32, (WIDE, LANES), 0)

    def tile(k, carry):
        slot = ((anchor + k) & (GRID - 1)) * RT_DEV
        shifts = [
            seeds[slot, (group + i) >> 2] + (((group + i) & 3) * LANES) * jnp.int32(1103515245)
            for i in range(WINDOW)
        ]

        def strip(number, inner):
            base = ((number * WIDE + t) * NB + u) * jnp.int32(1103515245)
            totals = [bias, jnp.zeros((WIDE, LANES), jnp.float32)]
            for i in range(WINDOW):
                entries = jnp.broadcast_to(window[i:i + 1, :], (WIDE, LANES))
                totals[i % 2] = weighted([base], shifts[i], [entries], [totals[i % 2]])[0]
            sums[pl.ds(pl.multiple_of(number * WIDE, WIDE), WIDE), :] = totals[0] + totals[1]
            return inner

        lax.fori_loop(0, NB // WIDE, strip, 0)
        value = jnp.sum(sums[...].T, axis=0, keepdims=True) * jnp.float32(-UNIT)
        value = value + jnp.where((col_index == 0) & (k == my_tile), rhs[...], 0.0)
        value = value - jnp.where((row_index == 0) & (col_index == k), vector[...], 0.0)
        out[pl.ds(2 * k, 2), :, :] = jnp.broadcast_to(value[None], (2, 1, NB))
        return carry

    lax.fori_loop(0, KB, tile, 0)


def first_rows(tile_owner, seeds, window, rhs, vector):
    return pl.pallas_call(
        first_kernel,
        out_shape=jax.ShapeDtypeStruct((GRID, 1, NB), jnp.float32),
        in_specs=[SMEM, SMEM, VMEM, VMEM, VMEM],
        out_specs=VMEM,
        scratch_shapes=[pltpu.VMEM((NB, LANES), jnp.float32)],
        cost_estimate=pl.CostEstimate(flops=KB * NB * 1600, bytes_accessed=GRID * NB * 4, transcendentals=0),
        compiler_params=LIMIT,
        name="first_rows",
    )(tile_owner, seeds, window, rhs, vector)


def hash_kernel(tile, start, with_sum, seeds, meta, v, *outs):
    acc_out = outs[0]
    bias = jnp.sum(jnp.sum(v[...], axis=0), axis=0, keepdims=True) * jnp.float32(BIAS)
    begin = meta[0] if with_sum else start

    def strip(number, carry):
        inner = begin + number * STRIP
        t = (inner + lax.broadcasted_iota(jnp.int32, (STRIP, LANES), 0)) * jnp.int32(NB)
        u = lax.broadcasted_iota(jnp.int32, (STRIP, LANES), 1)
        bases = [(t + u + jnp.int32(LANES * g)) * jnp.int32(1103515245) for g in range(GROUPS)]
        sums = [jnp.broadcast_to(bias, (STRIP, LANES))] + [jnp.zeros((STRIP, LANES), jnp.float32)] * (GROUPS - 1)
        for j in range(CT_DEV):
            entries = [jnp.broadcast_to(v[j, g:g + 1, :], (STRIP, LANES)) for g in range(GROUPS)]
            sums = weighted(bases, seeds[tile, j], entries, sums)
        total = (sums[0] + sums[1]) + (sums[2] + sums[3])
        acc_out[pl.ds(pl.multiple_of(number * STRIP, STRIP), STRIP), :] = total
        return carry

    lax.fori_loop(0, PIECE // STRIP, strip, 0)
    if with_sum:
        outs[1][...] = jnp.sum(acc_out[...].T, axis=0, keepdims=True)


def hash_rows(seeds, meta, v, tile, start, with_sum=False):
    shapes = [jax.ShapeDtypeStruct((PIECE, LANES), jnp.float32)]
    if with_sum:
        shapes.append(jax.ShapeDtypeStruct((1, PIECE), jnp.float32))
    return pl.pallas_call(
        functools.partial(hash_kernel, tile, start, with_sum),
        out_shape=shapes,
        in_specs=[SMEM, SMEM, VMEM],
        out_specs=[VMEM] * len(shapes),
        cost_estimate=pl.CostEstimate(
            flops=PIECE * CT_DEV * NB * 2, bytes_accessed=PIECE * LANES * 4, transcendentals=0
        ),
        compiler_params=LIMIT,
        name=f"hash_{tile}_{start}",
    )(seeds, meta, v)


def step_kernel(k, residual, *refs):
    refs = list(refs)
    same, other, solved_in = [refs.pop(0) for _ in range(3)] if k > 0 else [None] * 3
    inv = refs.pop(0)
    near, far = refs[:4], refs[4:8]
    total_out, solved_out, spread_y = refs[8:]
    col = lax.axis_index("pcol")
    me = lax.axis_index("prow")
    mine = col // 2 == k

    @pl.when(mine)
    def _():
        s = residual[...]
        if k > 0:
            running = same[...] + other[...]
            s = s - running[k:k + 1, :]
        y = jnp.sum(inv[...].astype(jnp.float32) * s, axis=1, keepdims=True)
        if k < KB - 1:
            spread_y[...] = jnp.broadcast_to(y, (256, LANES)).reshape(GRID, 16, LANES)
            rows = [jnp.zeros((1, NB), jnp.float32)] * (k + 1)
            for kk in range(k, KB - 1):
                part = jnp.zeros((16, NB), jnp.float32)
                for m in range(4):
                    for i in range(4):
                        if kk < NEAR:
                            tile, source = near[m][i, kk], me ^ (4 * m + i)
                        else:
                            tile, source = far[m][i, kk - NEAR], me ^ (4 * i + m)
                        part = part + tile * jnp.concatenate([spread_y[source]] * GROUPS, axis=1)
                rows.append(jnp.sum(part, axis=0, keepdims=True))
            update = jnp.concatenate(rows, axis=0)
            if k > 0:
                update = update + jnp.where(col % 2 == 0, running, 0.0)
            total_out[...] = update
        eye = lax.broadcasted_iota(jnp.int32, (256, 256), 0) == lax.broadcasted_iota(jnp.int32, (256, 256), 1)
        solved_out[...] = jnp.sum(jnp.where(eye, y, 0.0), axis=0, keepdims=True)

    @pl.when(jnp.logical_not(mine))
    def _():
        if k > 0:
            solved_out[...] = solved_in[...]
        else:
            solved_out[...] = jnp.zeros_like(solved_out)
        if k < KB - 1:
            total_out[...] = jnp.zeros_like(total_out)


def step(k, residual, running, solved, inv, tiles):
    args = (residual,) if k == 0 else (residual, running[0], running[1], solved)
    return pl.pallas_call(
        functools.partial(step_kernel, k),
        out_shape=[jax.ShapeDtypeStruct((KB, NB), jnp.float32), jax.ShapeDtypeStruct((1, 256), jnp.float32)],
        in_specs=[VMEM] * (len(args) + 9),
        out_specs=[VMEM] * 2,
        scratch_shapes=[pltpu.VMEM((GRID, 16, LANES), jnp.float32)],
        compiler_params=LIMIT,
        name=f"step_{k}",
    )(*args, inv, *tiles)


def last_kernel(factor, owner, rhs, v, residual, own_sum, their_sum, solved, panel, *refs):
    accs, out = refs[:-1], refs[-1]
    row_index, col_index = lax.axis_index("prow"), lax.axis_index("pcol")
    my_tile = (row_index - owner[0] + GRID) & (GRID - 1)
    early = my_tile < KB
    y = solved[...]
    for at in range(0, ROWS, LANES):
        n = at // LANES
        part = panel[at:at + LANES, :].astype(jnp.float32) * y
        part = (part[:, :LANES] + part[:, LANES:]) * factor[at // NB]
        if at >= NB:
            piece, row = divmod(at - NB, PIECE)
            part = part + accs[piece][row:row + LANES, :] * jnp.float32(UNIT)
        total = jnp.sum(part.T, axis=0, keepdims=True)
        given = jnp.where(col_index == 0, rhs[n:n + 1, :], 0.0)
        given = given - jnp.where(my_tile == col_index, v[n // GROUPS, n % GROUPS:n % GROUPS + 1, :], 0.0)
        if at < NB:
            held = own_sum if at < PIECE else their_sum
            given = given - held[:, at % PIECE:at % PIECE + LANES] * jnp.float32(UNIT)
            known = jnp.where(col_index == 2 * my_tile, residual[:, at:at + LANES], 0.0)
            given = jnp.where(early, known, given)
        out[n:n + 1, :] = given - total


def last(factor, owner, rhs, v, residual, own_sum, their_sum, solved, panel, accs):
    return pl.pallas_call(
        last_kernel,
        out_shape=jax.ShapeDtypeStruct((GRID, LANES), jnp.float32),
        in_specs=[SMEM] * 2 + [VMEM] * (7 + len(accs)),
        out_specs=VMEM,
        compiler_params=LIMIT,
        name="last",
    )(factor, owner, rhs, v, residual, own_sum, their_sum, solved, panel, *accs)


def to_all(value, axis):
    return lax.all_to_all(jnp.broadcast_to(value[None], (GRID,) + value.shape), axis, 0, 0, tiled=True)


def exchange(value, mask):
    return lax.ppermute(value, "prow", [(i, i ^ mask) for i in range(GRID)])


def after(value, *others):
    return lax.optimization_barrier((value,) + others)[0]


def body(seeds, tile_owner, vector, rhs, panel, tile_scales, inverses):
    row_index = lax.axis_index("prow")
    col_index = lax.axis_index("pcol")
    anchor = tile_owner[0]
    block = col_index // 2
    first_tile = jnp.mod(row_index - anchor, GRID)
    my_tiles = jnp.arange(RT_DEV, dtype=jnp.int32) * GRID + first_tile
    scales = lax.dynamic_slice_in_dim(tile_scales, block, 1, 1)[:, 0]
    factor = jnp.where(my_tiles > block, scales, jnp.float32(0.0))

    scaled = (panel[:NB].astype(jnp.float32) * factor[0]).T.reshape(GRID, 16, NB)
    padded = jnp.pad(vector, (0, 2 * NB - vector.shape[0])).reshape(1, 2, NB)
    sent = jnp.concatenate([scaled, jnp.broadcast_to(padded, (GRID, 2, NB))], axis=1)
    came = lax.all_to_all(sent, "prow", 0, 0, tiled=True)

    edge = jnp.zeros((96,), jnp.float32)
    window = lax.dynamic_slice_in_dim(
        jnp.concatenate([edge, vector, edge]), 96 - 32 * jnp.mod(row_index, 4), WINDOW * LANES, 0
    ).reshape(WINDOW, LANES)
    parts = first_rows(
        tile_owner, seeds, window, rhs[:NB].reshape(1, NB), vector[:NB].reshape(1, NB)
    )

    early = first_tile < KB
    shared = jnp.where(early, jnp.mod(row_index + KB, GRID), row_index) * RT_DEV
    seed_rows = jnp.concatenate([
        lax.dynamic_slice_in_dim(seeds, row_index * RT_DEV + 1, RT_DEV - 1, 0),
        lax.dynamic_slice_in_dim(seeds, shared, 1, 0),
    ])
    meta = jnp.where(early, PIECE, 0).reshape(1)

    own = lax.dynamic_slice_in_dim(jnp.concatenate([came, came])[:, :16], anchor + 1, KB - 1, 0)
    v = came[:, 16:].reshape(GRID, 2 * NB)[:, :vector.shape[0]].reshape(CT_DEV, GROUPS, LANES)
    near, far, parts, v = lax.optimization_barrier((own[:NEAR], own[NEAR:], parts, v))
    near = jnp.stack([near] + [exchange(near, m) for m in (1, 2, 3)])
    far = jnp.stack([far] + [exchange(far, m) for m in (4, 8, 12)])
    accs = []
    _, own_sum = hash_rows(seed_rows, meta, v, RT_DEV - 1, 0, True)
    their_sum = exchange(own_sum, KB)
    part = jnp.sum(lax.all_to_all(parts, "pcol", 0, 0, tiled=True), axis=0)
    near, far, part, own_sum = lax.optimization_barrier((near, far, part, own_sum))
    tiles = [near] + [exchange(near, m) for m in (4, 8, 12)] + [far] + [exchange(far, m) for m in (1, 2, 3)]
    came = to_all(part, "prow")
    here = after(v, part)
    for n in range(AHEAD):
        accs.append(hash_rows(seed_rows, meta, here, *divmod(n * PIECE, NB))[0])
        here = after(v, accs[-1])
    residual = after(jnp.sum(came, axis=0), accs[-1])

    running, solved = None, None
    for k in range(KB):
        total, solved = step(k, residual, running, solved, inverses, tiles)
        if k == KB - 1:
            break
        same = lax.ppermute(total, "pcol", [(2 * k + h, 2 * k + 2 + h) for h in range(2)])
        other = lax.ppermute(total, "pcol", [(2 * k + h, 2 * k + 3 - h) for h in range(2)])
        if k in GAPS:
            accs.append(hash_rows(seed_rows, meta, after(v, total), *divmod(len(accs) * PIECE, NB))[0])
            same = after(same, accs[-1])
        running = (same, other)

    sums = last(
        factor, tile_owner, rhs.reshape(GRID, LANES), v, residual, own_sum, their_sum, solved, panel, accs
    )
    updated = jnp.sum(lax.all_to_all(sums, "pcol", 0, 0, tiled=True), axis=0)
    return (solved.reshape(256), updated)


def solution(mesh):
    placed = (
        P(None, "pcol"),
        P(),
        P(("pcol", "prow")),
        P("prow"),
        P("prow", "pcol"),
        P("prow", None),
        P("pcol", None),
    )
    return jax.shard_map(
        body,
        mesh=mesh,
        in_specs=placed,
        out_specs=(P("pcol"), P(("prow", "pcol"))),
        check_vma=False,
    )
```

time: 216 us -> 157 us (0.73)
  waiting for transfers between devices: 56.6 us -> 9.65 us
  Pallas kernels: 81.1 us -> 65 us
  blocking collectives: 11.7 us -> 16.1 us
    all_to_all x3 -> x1, waiting for transfers between devices: 49.2 us -> 0.01 us  [to_all(): lax.all_to_all(jnp.broadcast_to(value[None], (GRID,) + value.shape), axis...]
    ppermute x0 -> x13, starting transfers between devices: none -> 12.2 us  [exchange(): return lax.ppermute(value, 'prow', [(i, i ^ mask) for i in range(GRID)])]
    all_to_all x3 -> x1, starting transfers between devices: 20 us -> 8.47 us  [to_all(): lax.all_to_all(jnp.broadcast_to(value[None], (GRID,) + value.shape), axis...]
    ppermute x0 -> x13, waiting for transfers between devices: none -> 8.77 us  [exchange(): return lax.ppermute(value, 'prow', [(i, i ^ mask) for i in range(GRID)])]
    pallas_call x8, Pallas kernels: 17.5 us -> 9.15 us  [step(): pl.pallas_call(functools.partial(step_kernel, k), out_shape=[jax.ShapeDty...]
    pallas_call x10 -> x9, Pallas kernels: 63.6 us -> 55.8 us  [the longest x7 44.9 us: hash_rows(): pl.pallas_call(functools.partial(hash_kernel, tile, start, with_sum), out...]
    all_to_all x2, waiting for transfers between devices: 7.34 us -> 0.01 us  [the longest x1 0.01 us: body(): part = jnp.sum(lax.all_to_all(parts, 'pcol', 0, 0, tiled=True), axis=0)]
    all_to_all x1, blocking collectives: 11.7 us -> 16.1 us  [body(): updated = jnp.sum(lax.all_to_all(sums, 'pcol', 0, 0, tiled=True), axis=0)]
  transfers between devices with their start and end apart: 19 -> 30, of which waited for: 3 -> 3; matrix products, arithmetic and copies ran while one was open for 2% -> 2% of each run, Pallas kernels for 23% -> 36%
where the time goes in v2:
time: 157 us; the launch traced here: 155 us
  Pallas kernels  65 us (41%)
  starting transfers between devices  52.4 us (33%)
  blocking collectives  16.1 us (10%)
  waiting for transfers between devices  9.65 us (6%)
  local copies, waits for them, and re-layouts  7.22 us (5%)
  other arithmetic  3.63 us (2%)
    pallas_call x7, Pallas kernels, hash_rows(): pl.pallas_call(functools.partial(hash_kernel, tile, start, with_sum), out...  44.9 us
    all_to_all x1, blocking collectives, body(): updated = jnp.sum(lax.all_to_all(sums, 'pcol', 0, 0, tiled=True), axis=0)  16.1 us
    ppermute x13, starting transfers between devices, exchange(): return lax.ppermute(value, 'prow', [(i, i ^ mask) for i in range(GRID)])  12.2 us
    all_to_all x1, starting transfers between devices, body(): part = jnp.sum(lax.all_to_all(parts, 'pcol', 0, 0, tiled=True), axis=0)  11.1 us
    pallas_call x1, Pallas kernels, first_rows(): pl.pallas_call(first_kernel, out_shape=jax.ShapeDtypeStruct((GRID, 1, NB)...  10 us
    pallas_call x8, Pallas kernels, step(): pl.pallas_call(functools.partial(step_kernel, k), out_shape=[jax.ShapeDty...  9.15 us
    ppermute x13, waiting for transfers between devices, exchange(): return lax.ppermute(value, 'prow', [(i, i ^ mask) for i in range(GRID)])  8.77 us
    all_to_all x1, starting transfers between devices, to_all(): lax.all_to_all(jnp.broadcast_to(value[None], (GRID,) + value.shape), axis...  8.47 us
  transfers between devices with their start and end apart: 30, of which 3 were waited for; matrix products, arithmetic and copies ran while one was open for 2% of the time, Pallas kernels for 36%

profile of v2, /device:TPU:29, one launch (start us, length us, event | category | flops | bytes accessed | tf_op | source)
XLA Modules:
  0.0 155.4 jit_solution(11896510009952501105)
XLA Ops:
  1.6 1.0 multiply_bitcast_fusion
  3.4 1.0 pad_maximum_fusion
  4.3 6.6 %all-to-all-start = ((f32[16,18,512]{2,1,0:T(8,128)}), f32[16,18,512]{2,1,0:T(8,128)S(1)}, u32[]{:S(2)}, u32[]{:S(2)}) async-start(f32[16,18,512]{2,1,0:T(8,128)} %pad_maximum_fusion), calls=%async_computation | async-start | bytes 1572864 | tf_op jit(solution)/shard_map/all_to_all | solution.py:260
  11.8 0.7 slice.36
  12.6 10.0 %first_rows.1 = f32[16,1,512]{2,1,0:T(1,128)} custom-call(s32[64]{0:T(128)S(1)} %copy-done.11, s32[64,25]{1,0:T(8,128)S(1)} %copy.24.seeds, f32[7,128]{1,0:T(8,128)S(1)} %dynamic-slice_bitcast_fusion.window, f32[1,512]{1,0:T(1,128)S(1)} %bitcast.42, f32[1,512]{1,0:T(1,128)S(1)} %bitcast.41), custom_call_target="tpu_custom_call" | custom-call | flops 6553600 | bytes 32768 | tf_op jit(solution)/shard_map/first_rows/pallas_call | solution.py:88
  22.9 1.0 collective-permute-start.3
  24.5 1.2 collective-permute-start.5
  26.5 11.1 %all-to-all-start.1 = ((f32[16,1,512]{2,1,0:T(1,128)}), f32[16,1,512]{2,1,0:T(1,128)S(1)}, u32[]{:S(2)}, u32[]{:S(2)}) async-start(f32[16,1,512]{2,1,0:T(1,128)} %first_rows.1), calls=%async_computation.1 | async-start | bytes 65536 | tf_op jit(solution)/shard_map/all_to_all | solution.py:286
  37.7 3.1 %collective-permute-start.1 = (f32[4,16,512]{2,1,0:T(8,128)S(1)}, f32[4,16,512]{2,1,0:T(8,128)S(1)}, u32[]{:S(2)}, u32[]{:S(2)}) collective-permute-start(f32[4,16,512]{2,1,0:T(8,128)S(1)} %slice.40), channel_id=1, source_target_pairs={{0,32},{16,48},{32,0},{48,16},{64,96},{80,112},{96,64},{112,80},{1... | collective-permute-start | bytes 393224 | tf_op jit(solution)/shard_map/ppermute | solution.py:240
  40.8 7.0 %hash_3_0.1 = (f32[256,128]{1,0:T(8,128)}, f32[1,256]{1,0:T(1,128)S(1)}) custom-call(s32[4,25]{1,0:T(4,128)S(1)} %pad_add_fusion.seeds, s32[1]{0:T(128)} %bitcast.16.meta, f32[25,4,128]{2,1,0:T(4,128)S(1)} %reshape.45.v), custom_call_target="tpu_custom_call" | custom-call | flops 6553600 | bytes 131072 | tf_op jit(solution)/shard_map/hash_3_0/pallas_call | solution.py:127
  48.6 2.2 %collective-permute-start.6 = (f32[4,4,16,512]{3,2,1,0:T(8,128)S(1)}, f32[4,4,16,512]{3,2,1,0:T(8,128)S(1)}, u32[]{:S(2)}, u32[]{:S(2)}) collective-permute-start(f32[4,4,16,512]{3,2,1,0:T(8,128)S(1)} %pad_maximum_fusion.1.refs_1_.refs_4_), channel_id=1, source_target_pairs={{0,64},{16,80},{32,96},{48,112},{64,0},{80,16},{96,32},{112,48},{1... | collective-permute-start | bytes 1572872 | tf_op jit(solution)/shard_map/ppermute | solution.py:240
  51.3 0.7 collective-permute-start.8
  52.1 1.6 %collective-permute-start.11 = (f32[4,3,16,512]{3,2,1,0:T(8,128)S(1)}, f32[4,3,16,512]{3,2,1,0:T(8,128)S(1)}, u32[]{:S(2)}, u32[]{:S(2)}) collective-permute-start(f32[4,3,16,512]{3,2,1,0:T(8,128)S(1)} %pad_maximum_fusion.2.refs_5_.refs_8_), channel_id=1, source_target_pairs={{0,48},{16,32},{32,16},{48,0},{64,112},{80,96},{96,80},{112,64},{1... | collective-permute-start | bytes 1179656 | tf_op jit(solution)/shard_map/ppermute | solution.py:240
  53.6 6.8 %collective-permute-done.10.refs_7_.refs_10_ = f32[4,3,16,512]{3,2,1,0:T(8,128)S(1)} collective-permute-done((f32[4,3,16,512]{3,2,1,0:T(8,128)S(1)}, f32[4,3,16,512]{3,2,1,0:T(8,128)S(1)}, u32[]{:S(2)}, u32[]{:S(2)}) %collective-permute-start.10) | collective-permute-done | bytes 393248 | tf_op jit(solution)/shard_map/ppermute | solution.py:240
  61.1 8.5 %all-to-all-start.2 = ((f32[16,1,512]{2,1,0:T(1,128)}), f32[16,1,512]{2,1,0:T(1,128)}, u32[]{:S(2)}, u32[]{:S(2)}) async-start(f32[16,1,512]{2,1,0:T(1,128)} %broadcast_in_dim.27), calls=%async_computation.2 | async-start | bytes 65536 | tf_op jit(solution)/shard_map/all_to_all | solution.py:236
  69.6 0.8 copy-done.3
  70.4 6.3 %hash_0_0.1.refs_0_ = f32[256,128]{1,0:T(8,128)S(1)} custom-call(s32[4,25]{1,0:T(4,128)S(1)} %pad_add_fusion.seeds, s32[1]{0:T(128)} %bitcast.16.meta, f32[25,4,128]{2,1,0:T(4,128)S(1)} %copy-done.3), custom_call_target="tpu_custom_call" | custom-call | flops 6553600 | bytes 131072 | tf_op jit(solution)/shard_map/hash_0_0/pallas_call | solution.py:127
  76.7 0.7 copy-done.6
  77.4 6.3 %hash_0_256.1.refs_1_ = f32[256,128]{1,0:T(8,128)S(1)} custom-call(s32[4,25]{1,0:T(4,128)S(1)} %pad_add_fusion.seeds, s32[1]{0:T(128)} %bitcast.16.meta, f32[25,4,128]{2,1,0:T(4,128)S(1)} %copy-done.3), custom_call_target="tpu_custom_call" | custom-call | flops 6553600 | bytes 131072 | tf_op jit(solution)/shard_map/hash_0_256/pallas_call | solution.py:127
  84.4 0.8 reduce_sum.33
  85.2 1.4 step_0.1
  86.6 2.5 %collective-permute-start.12 = (f32[8,512]{1,0:T(8,128)S(1)}, f32[8,512]{1,0:T(8,128)S(1)}, u32[]{:S(2)}, u32[]{:S(2)}) collective-permute-start(f32[8,512]{1,0:T(8,128)S(1)} %get-tuple-element.48), channel_id=1, source_target_pairs={{0,2},{1,3},{16,18},{17,19},{32,34},{33,35},{48,50},{49,51},{64,66... | collective-permute-start | bytes 49160 | tf_op jit(solution)/shard_map/ppermute | solution.py:301
  89.2 3.6 %collective-permute-start.13 = (f32[8,512]{1,0:T(8,128)S(1)}, f32[8,512]{1,0:T(8,128)S(1)}, u32[]{:S(2)}, u32[]{:S(2)}) collective-permute-start(f32[8,512]{1,0:T(8,128)S(1)} %get-tuple-element.48), channel_id=1, source_target_pairs={{0,3},{1,2},{16,19},{17,18},{32,35},{33,34},{48,51},{49,50},{64,67... | collective-permute-start | bytes 49160 | tf_op jit(solution)/shard_map/ppermute | solution.py:302
  92.8 0.8 collective-permute-done.13.refs_1_
  93.6 1.0 step_1.1
  94.6 0.7 collective-permute-start.14
  95.3 0.7 collective-permute-start.15
  96.0 6.3 %hash_1_0.1.refs_2_ = f32[256,128]{1,0:T(8,128)S(1)} custom-call(s32[4,25]{1,0:T(4,128)S(1)} %pad_add_fusion.seeds, s32[1]{0:T(128)} %bitcast.16.meta, f32[25,4,128]{2,1,0:T(4,128)S(1)} %copy-done.4), custom_call_target="tpu_custom_call" | custom-call | flops 6553600 | bytes 131072 | tf_op jit(solution)/shard_map/hash_1_0/pallas_call | solution.py:127
  102.3 1.0 step_2.1
  103.3 0.7 collective-permute-start.16
  104.0 0.7 collective-permute-start.17
  104.6 1.0 step_3.1
  105.7 0.7 collective-permute-start.18
  106.3 0.7 collective-permute-start.19
  107.0 6.3 %hash_1_256.1.refs_3_ = f32[256,128]{1,0:T(8,128)S(1)} custom-call(s32[4,25]{1,0:T(4,128)S(1)} %pad_add_fusion.seeds, s32[1]{0:T(128)} %bitcast.16.meta, f32[25,4,128]{2,1,0:T(4,128)S(1)} %copy-done.4), custom_call_target="tpu_custom_call" | custom-call | flops 6553600 | bytes 131072 | tf_op jit(solution)/shard_map/hash_1_256/pallas_call | solution.py:127
  113.3 1.0 step_4.1
  115.0 0.7 collective-permute-start.21
  115.7 6.3 %hash_2_0.1.refs_4_ = f32[256,128]{1,0:T(8,128)S(1)} custom-call(s32[4,25]{1,0:T(4,128)S(1)} %pad_add_fusion.seeds, s32[1]{0:T(128)} %bitcast.16.meta, f32[25,4,128]{2,1,0:T(4,128)S(1)} %copy-done.4), custom_call_target="tpu_custom_call" | custom-call | flops 6553600 | bytes 131072 | tf_op jit(solution)/shard_map/hash_2_0/pallas_call | solution.py:127
  122.0 1.0 step_5.1
  123.7 0.7 collective-permute-start.23
  124.3 6.3 %hash_2_256.1.refs_5_ = f32[256,128]{1,0:T(8,128)S(1)} custom-call(s32[4,25]{1,0:T(4,128)S(1)} %pad_add_fusion.seeds, s32[1]{0:T(128)} %bitcast.16.meta, f32[25,4,128]{2,1,0:T(4,128)S(1)} %copy-done.4), custom_call_target="tpu_custom_call" | custom-call | flops 6553600 | bytes 131072 | tf_op jit(solution)/shard_map/hash_2_256/pallas_call | solution.py:127
  130.7 1.0 step_6.1
  131.7 0.8 collective-permute-start.24
  132.5 0.7 collective-permute-start.25
  133.6 1.7 %step_7.1 = (f32[8,512]{1,0:T(8,128)}, f32[1,256]{1,0:T(1,128)}) custom-call(f32[1,512]{1,0:T(1,128)S(1)} %bitcast.37, f32[8,512]{1,0:T(8,128)S(1)} %collective-permute-done.24.refs_0_, f32[8,512]{1,0:T(8,128)S(1)} %collective-permute-done.25.refs_1_, f32[1,256]{1,0:T(1,128)S(1)} %get-tuple-element.69.refs_2_, bf16[256,512]{1,0:T(8,128)(2,1)S(1)} %copy-done.1, ...), custom_call_target="tpu_custom_call" | custom-call | tf_op jit(solution)/shard_map/step_7/pallas_call | solution.py:189
  135.3 1.9 %collective-permute-done.26.their_sum = f32[1,256]{1,0:T(1,128)S(1)} collective-permute-done((f32[1,256]{1,0:T(1,128)S(1)}, f32[1,256]{1,0:T(1,128)S(1)}, u32[]{:S(2)}, u32[]{:S(2)}) %collective-permute-start.26) | collective-permute-done | bytes 1056 | tf_op jit(solution)/shard_map/ppermute | solution.py:240
  137.9 0.9 last.1
  138.8 16.1 %all_to_all.24 = f32[16,1,128]{2,1,0:T(1,128)S(1)} all-to-all(f32[16,1,128]{2,1,0:T(1,128)S(1)} %bitcast.39), channel_id=1, replica_groups=mesh['prow'=16,'pcol'=16] {'pcol'}, dimensions={0} | all-to-all | bytes 16384 | tf_op jit(solution)/shard_map/all_to_all | solution.py:311
  (96 shorter events, 9.7 us)
Async XLA Ops:
  0.6 0.8 copy-start
  0.6 0.7 copy-start.11
  2.6 0.7 copy-start.16
  4.3 18.3 %all-to-all-start = ((f32[16,18,512]{2,1,0:T(8,128)}), f32[16,18,512]{2,1,0:T(8,128)S(1)}, u32[]{:S(2)}, u32[]{:S(2)}) async-start(f32[16,18,512]{2,1,0:T(8,128)} %pad_maximum_fusion), calls=%async_computation | async-start | bytes 1572864 | tf_op jit(solution)/shard_map/all_to_all | solution.py:260
  11.0 0.7 copy-start.17
  22.9 24.8 %copy-start.2 = (f32[25,4,128]{2,1,0:T(4,128)}, f32[25,4,128]{2,1,0:T(4,128)S(1)}, u32[]{:S(2)}) copy-start(f32[25,4,128]{2,1,0:T(4,128)S(1)} %reshape.45.v) | copy-start | bytes 153604
  22.9 14.7 %collective-permute-start.3 = (f32[3,16,512]{2,1,0:T(8,128)S(1)}, f32[3,16,512]{2,1,0:T(8,128)S(1)}, u32[]{:S(2)}, u32[]{:S(2)}) collective-permute-start(f32[3,16,512]{2,1,0:T(8,128)S(1)} %slice.41), channel_id=1, source_target_pairs={{0,64},{16,80},{32,96},{48,112},{64,0},{80,16},{96,32},{112,48},{1... | collective-permute-start | bytes 294920 | tf_op jit(solution)/shard_map/ppermute | solution.py:240
  23.9 24.5 %collective-permute-start.4 = (f32[3,16,512]{2,1,0:T(8,128)S(1)}, f32[3,16,512]{2,1,0:T(8,128)S(1)}, u32[]{:S(2)}, u32[]{:S(2)}) collective-permute-start(f32[3,16,512]{2,1,0:T(8,128)S(1)} %slice.41), channel_id=1, source_target_pairs={{0,128},{16,144},{32,160},{48,176},{64,192},{80,208},{96,224},{112... | collective-permute-start | bytes 294920 | tf_op jit(solution)/shard_map/ppermute | solution.py:240
  24.5 23.9 %collective-permute-start.5 = (f32[3,16,512]{2,1,0:T(8,128)S(1)}, f32[3,16,512]{2,1,0:T(8,128)S(1)}, u32[]{:S(2)}, u32[]{:S(2)}) collective-permute-start(f32[3,16,512]{2,1,0:T(8,128)S(1)} %slice.41), channel_id=1, source_target_pairs={{0,192},{16,208},{32,224},{48,240},{64,128},{80,144},{96,160},{112... | collective-permute-start | bytes 294920 | tf_op jit(solution)/shard_map/ppermute | solution.py:240
  25.7 22.7 %collective-permute-start.2 = (f32[4,16,512]{2,1,0:T(8,128)S(1)}, f32[4,16,512]{2,1,0:T(8,128)S(1)}, u32[]{:S(2)}, u32[]{:S(2)}) collective-permute-start(f32[4,16,512]{2,1,0:T(8,128)S(1)} %slice.40), channel_id=1, source_target_pairs={{0,48},{16,32},{32,16},{48,0},{64,112},{80,96},{96,80},{112,64},{1... | collective-permute-start | bytes 393224 | tf_op jit(solution)/shard_map/ppermute | solution.py:240
  26.0 22.5 %collective-permute-start = (f32[4,16,512]{2,1,0:T(8,128)S(1)}, f32[4,16,512]{2,1,0:T(8,128)S(1)}, u32[]{:S(2)}, u32[]{:S(2)}) collective-permute-start(f32[4,16,512]{2,1,0:T(8,128)S(1)} %slice.40), channel_id=1, source_target_pairs={{0,16},{16,0},{32,48},{48,32},{64,80},{80,64},{96,112},{112,96},{1... | collective-permute-start | bytes 393224 | tf_op jit(solution)/shard_map/ppermute | solution.py:240
  26.5 21.8 %all-to-all-start.1 = ((f32[16,1,512]{2,1,0:T(1,128)}), f32[16,1,512]{2,1,0:T(1,128)S(1)}, u32[]{:S(2)}, u32[]{:S(2)}) async-start(f32[16,1,512]{2,1,0:T(1,128)} %first_rows.1), calls=%async_computation.1 | async-start | bytes 65536 | tf_op jit(solution)/shard_map/all_to_all | solution.py:286
  37.7 10.8 %collective-permute-start.1 = (f32[4,16,512]{2,1,0:T(8,128)S(1)}, f32[4,16,512]{2,1,0:T(8,128)S(1)}, u32[]{:S(2)}, u32[]{:S(2)}) collective-permute-start(f32[4,16,512]{2,1,0:T(8,128)S(1)} %slice.40), channel_id=1, source_target_pairs={{0,32},{16,48},{32,0},{48,16},{64,96},{80,112},{96,64},{112,80},{1... | collective-permute-start | bytes 393224 | tf_op jit(solution)/shard_map/ppermute | solution.py:240
  47.8 0.6 copy-start.13
  48.5 36.7 %copy-start.1 = (bf16[256,512]{1,0:T(8,128)(2,1)S(1)}, bf16[256,512]{1,0:T(8,128)(2,1)}, u32[]{:S(2)}) copy-start(bf16[256,512]{1,0:T(8,128)(2,1)} %refs_3_.13) | copy-start | bytes 786436
  48.5 12.0 %collective-permute-start.10 = (f32[4,3,16,512]{3,2,1,0:T(8,128)S(1)}, f32[4,3,16,512]{3,2,1,0:T(8,128)S(1)}, u32[]{:S(2)}, u32[]{:S(2)}) collective-permute-start(f32[4,3,16,512]{3,2,1,0:T(8,128)S(1)} %pad_maximum_fusion.2.refs_5_.refs_8_), channel_id=1, source_target_pairs={{0,32},{16,48},{32,0},{48,16},{64,96},{80,112},{96,64},{112,80},{1... | collective-permute-start | bytes 1179656 | tf_op jit(solution)/shard_map/ppermute | solution.py:240
  48.6 36.6 %collective-permute-start.6 = (f32[4,4,16,512]{3,2,1,0:T(8,128)S(1)}, f32[4,4,16,512]{3,2,1,0:T(8,128)S(1)}, u32[]{:S(2)}, u32[]{:S(2)}) collective-permute-start(f32[4,4,16,512]{3,2,1,0:T(8,128)S(1)} %pad_maximum_fusion.1.refs_1_.refs_4_), channel_id=1, source_target_pairs={{0,64},{16,80},{32,96},{48,112},{64,0},{80,16},{96,32},{112,48},{1... | collective-permute-start | bytes 1572872 | tf_op jit(solution)/shard_map/ppermute | solution.py:240
  50.8 34.4 %collective-permute-start.7 = (f32[4,4,16,512]{3,2,1,0:T(8,128)S(1)}, f32[4,4,16,512]{3,2,1,0:T(8,128)S(1)}, u32[]{:S(2)}, u32[]{:S(2)}) collective-permute-start(f32[4,4,16,512]{3,2,1,0:T(8,128)S(1)} %pad_maximum_fusion.1.refs_1_.refs_4_), channel_id=1, source_target_pairs={{0,128},{16,144},{32,160},{48,176},{64,192},{80,208},{96,224},{112... | collective-permute-start | bytes 1572872 | tf_op jit(solution)/shard_map/ppermute | solution.py:240
  51.3 33.9 %collective-permute-start.8 = (f32[4,4,16,512]{3,2,1,0:T(8,128)S(1)}, f32[4,4,16,512]{3,2,1,0:T(8,128)S(1)}, u32[]{:S(2)}, u32[]{:S(2)}) collective-permute-start(f32[4,4,16,512]{3,2,1,0:T(8,128)S(1)} %pad_maximum_fusion.1.refs_1_.refs_4_), channel_id=1, source_target_pairs={{0,192},{16,208},{32,224},{48,240},{64,128},{80,144},{96,160},{112... | collective-permute-start | bytes 1572872 | tf_op jit(solution)/shard_map/ppermute | solution.py:240
  52.1 33.1 %collective-permute-start.11 = (f32[4,3,16,512]{3,2,1,0:T(8,128)S(1)}, f32[4,3,16,512]{3,2,1,0:T(8,128)S(1)}, u32[]{:S(2)}, u32[]{:S(2)}) collective-permute-start(f32[4,3,16,512]{3,2,1,0:T(8,128)S(1)} %pad_maximum_fusion.2.refs_5_.refs_8_), channel_id=1, source_target_pairs={{0,48},{16,32},{32,16},{48,0},{64,112},{80,96},{96,80},{112,64},{1... | collective-permute-start | bytes 1179656 | tf_op jit(solution)/shard_map/ppermute | solution.py:240
  60.5 24.7 %collective-permute-start.9 = (f32[4,3,16,512]{3,2,1,0:T(8,128)S(1)}, f32[4,3,16,512]{3,2,1,0:T(8,128)}, u32[]{:S(2)}, u32[]{:S(2)}) collective-permute-start(f32[4,3,16,512]{3,2,1,0:T(8,128)S(1)} %pad_maximum_fusion.2.refs_5_.refs_8_), channel_id=1, source_target_pairs={{0,16},{16,0},{32,48},{48,32},{64,80},{80,64},{96,112},{112,96},{1... | collective-permute-start | bytes 1179656 | tf_op jit(solution)/shard_map/ppermute | solution.py:240
  61.1 23.2 %all-to-all-start.2 = ((f32[16,1,512]{2,1,0:T(1,128)}), f32[16,1,512]{2,1,0:T(1,128)}, u32[]{:S(2)}, u32[]{:S(2)}) async-start(f32[16,1,512]{2,1,0:T(1,128)} %broadcast_in_dim.27), calls=%async_computation.2 | async-start | bytes 65536 | tf_op jit(solution)/shard_map/all_to_all | solution.py:236
  69.6 0.8 copy-start.3
  76.7 0.7 copy-start.6
  83.7 0.7 copy-start.8
  86.6 6.1 %collective-permute-start.12 = (f32[8,512]{1,0:T(8,128)S(1)}, f32[8,512]{1,0:T(8,128)S(1)}, u32[]{:S(2)}, u32[]{:S(2)}) collective-permute-start(f32[8,512]{1,0:T(8,128)S(1)} %get-tuple-element.48), channel_id=1, source_target_pairs={{0,2},{1,3},{16,18},{17,19},{32,34},{33,35},{48,50},{49,51},{64,66... | collective-permute-start | bytes 49160 | tf_op jit(solution)/shard_map/ppermute | solution.py:301
  89.2 4.4 %collective-permute-start.13 = (f32[8,512]{1,0:T(8,128)S(1)}, f32[8,512]{1,0:T(8,128)S(1)}, u32[]{:S(2)}, u32[]{:S(2)}) collective-permute-start(f32[8,512]{1,0:T(8,128)S(1)} %get-tuple-element.48), channel_id=1, source_target_pairs={{0,3},{1,2},{16,19},{17,18},{32,35},{33,34},{48,51},{49,50},{64,67... | collective-permute-start | bytes 49160 | tf_op jit(solution)/shard_map/ppermute | solution.py:302
  93.6 2.3 %copy-start.4 = (f32[25,4,128]{2,1,0:T(4,128)S(1)}, f32[25,4,128]{2,1,0:T(4,128)}, u32[]{:S(2)}) copy-start(f32[25,4,128]{2,1,0:T(4,128)} %copy-done.2) | copy-start | bytes 153604
  94.6 7.7 %collective-permute-start.14 = (f32[8,512]{1,0:T(8,128)S(1)}, f32[8,512]{1,0:T(8,128)S(1)}, u32[]{:S(2)}, u32[]{:S(2)}) collective-permute-start(f32[8,512]{1,0:T(8,128)S(1)} %get-tuple-element.50), channel_id=1, source_target_pairs={{2,4},{3,5},{18,20},{19,21},{34,36},{35,37},{50,52},{51,53},{66,68... | collective-permute-start | bytes 49160 | tf_op jit(solution)/shard_map/ppermute | solution.py:301
  95.3 7.0 %collective-permute-start.15 = (f32[8,512]{1,0:T(8,128)S(1)}, f32[8,512]{1,0:T(8,128)S(1)}, u32[]{:S(2)}, u32[]{:S(2)}) collective-permute-start(f32[8,512]{1,0:T(8,128)S(1)} %get-tuple-element.50), channel_id=1, source_target_pairs={{2,5},{3,4},{18,21},{19,20},{34,37},{35,36},{50,53},{51,52},{66,69... | collective-permute-start | bytes 49160 | tf_op jit(solution)/shard_map/ppermute | solution.py:302
  103.3 1.3 collective-permute-start.16
  104.0 0.7 collective-permute-start.17
  105.7 7.7 %collective-permute-start.18 = (f32[8,512]{1,0:T(8,128)S(1)}, f32[8,512]{1,0:T(8,128)S(1)}, u32[]{:S(2)}, u32[]{:S(2)}) collective-permute-start(f32[8,512]{1,0:T(8,128)S(1)} %get-tuple-element.56), channel_id=1, source_target_pairs={{6,8},{7,9},{22,24},{23,25},{38,40},{39,41},{54,56},{55,57},{70,72... | collective-permute-start | bytes 49160 | tf_op jit(solution)/shard_map/ppermute | solution.py:301
  106.3 7.0 %collective-permute-start.19 = (f32[8,512]{1,0:T(8,128)S(1)}, f32[8,512]{1,0:T(8,128)S(1)}, u32[]{:S(2)}, u32[]{:S(2)}) collective-permute-start(f32[8,512]{1,0:T(8,128)S(1)} %get-tuple-element.56), channel_id=1, source_target_pairs={{6,9},{7,8},{22,25},{23,24},{38,41},{39,40},{54,57},{55,56},{70,73... | collective-permute-start | bytes 49160 | tf_op jit(solution)/shard_map/ppermute | solution.py:302
  114.3 7.7 %collective-permute-start.20 = (f32[8,512]{1,0:T(8,128)S(1)}, f32[8,512]{1,0:T(8,128)S(1)}, u32[]{:S(2)}, u32[]{:S(2)}) collective-permute-start(f32[8,512]{1,0:T(8,128)S(1)} %get-tuple-element.60), channel_id=1, source_target_pairs={{8,10},{9,11},{24,26},{25,27},{40,42},{41,43},{56,58},{57,59},{72,... | collective-permute-start | bytes 49160 | tf_op jit(solution)/shard_map/ppermute | solution.py:301
  115.0 7.0 %collective-permute-start.21 = (f32[8,512]{1,0:T(8,128)S(1)}, f32[8,512]{1,0:T(8,128)S(1)}, u32[]{:S(2)}, u32[]{:S(2)}) collective-permute-start(f32[8,512]{1,0:T(8,128)S(1)} %get-tuple-element.60), channel_id=1, source_target_pairs={{8,11},{9,10},{24,27},{25,26},{40,43},{41,42},{56,59},{57,58},{72,... | collective-permute-start | bytes 49160 | tf_op jit(solution)/shard_map/ppermute | solution.py:302
  123.0 7.7 %collective-permute-start.22 = (f32[8,512]{1,0:T(8,128)S(1)}, f32[8,512]{1,0:T(8,128)S(1)}, u32[]{:S(2)}, u32[]{:S(2)}) collective-permute-start(f32[8,512]{1,0:T(8,128)S(1)} %get-tuple-element.64), channel_id=1, source_target_pairs={{10,12},{11,13},{26,28},{27,29},{42,44},{43,45},{58,60},{59,61},{7... | collective-permute-start | bytes 49160 | tf_op jit(solution)/shard_map/ppermute | solution.py:301
  123.7 7.0 %collective-permute-start.23 = (f32[8,512]{1,0:T(8,128)S(1)}, f32[8,512]{1,0:T(8,128)S(1)}, u32[]{:S(2)}, u32[]{:S(2)}) collective-permute-start(f32[8,512]{1,0:T(8,128)S(1)} %get-tuple-element.64), channel_id=1, source_target_pairs={{10,13},{11,12},{26,29},{27,28},{42,45},{43,44},{58,61},{59,60},{7... | collective-permute-start | bytes 49160 | tf_op jit(solution)/shard_map/ppermute | solution.py:302
  131.7 1.5 copy-start.14
  131.7 1.8 %collective-permute-start.24 = (f32[8,512]{1,0:T(8,128)S(1)}, f32[8,512]{1,0:T(8,128)S(1)}, u32[]{:S(2)}, u32[]{:S(2)}) collective-permute-start(f32[8,512]{1,0:T(8,128)S(1)} %get-tuple-element.68), channel_id=1, source_target_pairs={{12,14},{13,15},{28,30},{29,31},{44,46},{45,47},{60,62},{61,63},{7... | collective-permute-start | bytes 49160 | tf_op jit(solution)/shard_map/ppermute | solution.py:301
  132.5 1.1 collective-permute-start.25
  133.2 4.0 %collective-permute-start.26 = (f32[1,256]{1,0:T(1,128)S(1)}, f32[1,256]{1,0:T(1,128)S(1)}, u32[]{:S(2)}, u32[]{:S(2)}) collective-permute-start(f32[1,256]{1,0:T(1,128)S(1)} %copy-done.14), channel_id=1, source_target_pairs={{0,128},{16,144},{32,160},{48,176},{64,192},{80,208},{96,224},{112... | collective-permute-start | bytes 3080 | tf_op jit(solution)/shard_map/ppermute | solution.py:240
  133.5 3.6 %copy-start.5 = (bf16[2048,256]{1,0:T(8,128)(2,1)S(1)}, bf16[2048,256]{1,0:T(8,128)(2,1)}, u32[]{:S(2)}) copy-start(bf16[2048,256]{1,0:T(8,128)(2,1)} %panel.1) | copy-start | bytes 3145732
  133.5 3.6 %copy-start.7 = (f32[256,128]{1,0:T(8,128)S(1)}, f32[256,128]{1,0:T(8,128)}, u32[]{:S(2)}) copy-start(f32[256,128]{1,0:T(8,128)} %copy-done.6) | copy-start | bytes 393220
  133.6 3.6 %copy-start.9 = (f32[256,128]{1,0:T(8,128)S(1)}, f32[256,128]{1,0:T(8,128)}, u32[]{:S(2)}) copy-start(f32[256,128]{1,0:T(8,128)} %copy-done.8) | copy-start | bytes 393220
  133.6 3.6 %copy-start.10 = (f32[2048]{0:T(1024)S(1)}, f32[2048]{0:T(1024)}, u32[]{:S(2)}) copy-start(f32[2048]{0:T(1024)} %param.10) | copy-start | bytes 24580
  137.2 0.7 copy-start.12
  137.2 0.7 copy-start.15

commit v3 on v2

--- a/solution.py
+++ b/solution.py
@@ -22,12 +22,13 @@
 WIDE = 64
 WINDOW = 7
 AHEAD = 2
-GAPS = (1, 3, 4, 5)
+GAPS = (1, 2, 3, 4)
 BIAS = -127.5
 
 VMEM = pl.BlockSpec(memory_space=pltpu.VMEM)
+ANY = pl.BlockSpec(memory_space=pl.ANY)
 SMEM = pl.BlockSpec(memory_space=pltpu.SMEM)
-LIMIT = pltpu.CompilerParams(vmem_limit_bytes=10 * 1024 * 1024)
+LIMIT = pltpu.CompilerParams(vmem_limit_bytes=6 * 1024 * 1024)
 
 
 def shift_right(value, amount):
@@ -97,10 +98,9 @@
     )(tile_owner, seeds, window, rhs, vector)
 
 
-def hash_kernel(tile, start, with_sum, seeds, meta, v, *outs):
-    acc_out = outs[0]
+def hash_kernel(row, tile, start, seeds, meta, v, table, _, out, held):
     bias = jnp.sum(jnp.sum(v[...], axis=0), axis=0, keepdims=True) * jnp.float32(BIAS)
-    begin = meta[0] if with_sum else start
+    begin = meta[0] if start is None else start
 
     def strip(number, carry):
         inner = begin + number * STRIP
@@ -112,29 +112,28 @@
             entries = [jnp.broadcast_to(v[j, g:g + 1, :], (STRIP, LANES)) for g in range(GROUPS)]
             sums = weighted(bases, seeds[tile, j], entries, sums)
         total = (sums[0] + sums[1]) + (sums[2] + sums[3])
-        acc_out[pl.ds(pl.multiple_of(number * STRIP, STRIP), STRIP), :] = total
+        held[pl.ds(pl.multiple_of(number * STRIP, STRIP), STRIP), :] = total
         return carry
 
     lax.fori_loop(0, PIECE // STRIP, strip, 0)
-    if with_sum:
-        outs[1][...] = jnp.sum(acc_out[...].T, axis=0, keepdims=True)
-
-
-def hash_rows(seeds, meta, v, tile, start, with_sum=False):
-    shapes = [jax.ShapeDtypeStruct((PIECE, LANES), jnp.float32)]
-    if with_sum:
-        shapes.append(jax.ShapeDtypeStruct((1, PIECE), jnp.float32))
+    out[...] = table[...]
+    out[row:row + 1, :] = jnp.sum(held[...].T, axis=0, keepdims=True) * jnp.float32(UNIT)
+
+
+def hash_rows(seeds, meta, v, table, token, row):
+    tile, start = divmod((row - 1) * PIECE, NB) if row > 0 else (RT_DEV - 1, None)
     return pl.pallas_call(
-        functools.partial(hash_kernel, tile, start, with_sum),
-        out_shape=shapes,
-        in_specs=[SMEM, SMEM, VMEM],
-        out_specs=[VMEM] * len(shapes),
+        functools.partial(hash_kernel, row, tile, start),
+        out_shape=jax.ShapeDtypeStruct((KB, PIECE), jnp.float32),
+        in_specs=[SMEM, SMEM, VMEM, VMEM, ANY],
+        out_specs=VMEM,
+        scratch_shapes=[pltpu.VMEM((PIECE, LANES), jnp.float32)],
         cost_estimate=pl.CostEstimate(
             flops=PIECE * CT_DEV * NB * 2, bytes_accessed=PIECE * LANES * 4, transcendentals=0
         ),
         compiler_params=LIMIT,
-        name=f"hash_{tile}_{start}",
-    )(seeds, meta, v)
+        name=f"hash_{row}",
+    )(seeds, meta, v, table, token)
 
 
 def step_kernel(k, residual, *refs):
@@ -142,13 +141,16 @@
     same, other, solved_in = [refs.pop(0) for _ in range(3)] if k > 0 else [None] * 3
     inv = refs.pop(0)
     near, far = refs[:4], refs[4:8]
-    total_out, solved_out, spread_y = refs[8:]
+    _, total_out, solved_out, spread_y, held, sem = refs[8:]
     col = lax.axis_index("pcol")
     me = lax.axis_index("prow")
     mine = col // 2 == k
 
     @pl.when(mine)
     def _():
+        if k < KB - 1:
+            fetch = pltpu.make_async_copy(far[3].at[:, max(k - NEAR, 0):], held, sem)
+            fetch.start()
         s = residual[...]
         if k > 0:
             running = same[...] + other[...]
@@ -158,13 +160,17 @@
             spread_y[...] = jnp.broadcast_to(y, (256, LANES)).reshape(GRID, 16, LANES)
             rows = [jnp.zeros((1, NB), jnp.float32)] * (k + 1)
             for kk in range(k, KB - 1):
+                if kk == max(k, NEAR):
+                    fetch.wait()
                 part = jnp.zeros((16, NB), jnp.float32)
                 for m in range(4):
                     for i in range(4):
                         if kk < NEAR:
                             tile, source = near[m][i, kk], me ^ (4 * m + i)
+                        elif m < 3:
+                            tile, source = far[m][i, kk - NEAR], me ^ (4 * i + m)
                         else:
-                            tile, source = far[m][i, kk - NEAR], me ^ (4 * i + m)
+                            tile, source = held[i, kk - max(k, NEAR)], me ^ (4 * i + m)
                         part = part + tile * jnp.concatenate([spread_y[source]] * GROUPS, axis=1)
                 rows.append(jnp.sum(part, axis=0, keepdims=True))
             update = jnp.concatenate(rows, axis=0)
@@ -184,52 +190,54 @@
             total_out[...] = jnp.zeros_like(total_out)
 
 
-def step(k, residual, running, solved, inv, tiles):
+def step(k, residual, running, solved, inv, tiles, token):
     args = (residual,) if k == 0 else (residual, running[0], running[1], solved)
     return pl.pallas_call(
         functools.partial(step_kernel, k),
         out_shape=[jax.ShapeDtypeStruct((KB, NB), jnp.float32), jax.ShapeDtypeStruct((1, 256), jnp.float32)],
-        in_specs=[VMEM] * (len(args) + 9),
+        in_specs=[VMEM] * (len(args) + 8) + [ANY, VMEM],
         out_specs=[VMEM] * 2,
-        scratch_shapes=[pltpu.VMEM((GRID, 16, LANES), jnp.float32)],
+        scratch_shapes=[
+            pltpu.VMEM((GRID, 16, LANES), jnp.float32),
+            pltpu.VMEM((4, min(KB - 1 - NEAR, max(KB - 1 - k, 1)), 16, NB), jnp.float32),
+            pltpu.SemaphoreType.DMA,
+        ],
         compiler_params=LIMIT,
         name=f"step_{k}",
-    )(*args, inv, *tiles)
-
-
-def last_kernel(factor, owner, rhs, v, residual, own_sum, their_sum, solved, panel, *refs):
-    accs, out = refs[:-1], refs[-1]
+    )(*args, inv, *tiles, token)
+
+
+def last_kernel(factor, owner, rhs, v, residual, theirs, solved, panel, table, out):
     row_index, col_index = lax.axis_index("prow"), lax.axis_index("pcol")
     my_tile = (row_index - owner[0] + GRID) & (GRID - 1)
-    early = my_tile < KB
     y = solved[...]
     for at in range(0, ROWS, LANES):
         n = at // LANES
         part = panel[at:at + LANES, :].astype(jnp.float32) * y
         part = (part[:, :LANES] + part[:, LANES:]) * factor[at // NB]
-        if at >= NB:
-            piece, row = divmod(at - NB, PIECE)
-            part = part + accs[piece][row:row + LANES, :] * jnp.float32(UNIT)
         total = jnp.sum(part.T, axis=0, keepdims=True)
         given = jnp.where(col_index == 0, rhs[n:n + 1, :], 0.0)
         given = given - jnp.where(my_tile == col_index, v[n // GROUPS, n % GROUPS:n % GROUPS + 1, :], 0.0)
         if at < NB:
-            held = own_sum if at < PIECE else their_sum
-            given = given - held[:, at % PIECE:at % PIECE + LANES] * jnp.float32(UNIT)
+            shared = table[0:1, at:at + LANES] if at < PIECE else theirs[:, at - PIECE:at - PIECE + LANES]
+            given = given - shared
             known = jnp.where(col_index == 2 * my_tile, residual[:, at:at + LANES], 0.0)
-            given = jnp.where(early, known, given)
+            given = jnp.where(my_tile < KB, known, given)
+        else:
+            piece, row = divmod(at - NB, PIECE)
+            given = given - table[piece + 1:piece + 2, row:row + LANES]
         out[n:n + 1, :] = given - total
 
 
-def last(factor, owner, rhs, v, residual, own_sum, their_sum, solved, panel, accs):
+def last(factor, owner, rhs, v, residual, theirs, solved, panel, table):
     return pl.pallas_call(
         last_kernel,
         out_shape=jax.ShapeDtypeStruct((GRID, LANES), jnp.float32),
-        in_specs=[SMEM] * 2 + [VMEM] * (7 + len(accs)),
+        in_specs=[SMEM] * 2 + [VMEM] * 7,
         out_specs=VMEM,
         compiler_params=LIMIT,
         name="last",
-    )(factor, owner, rhs, v, residual, own_sum, their_sum, solved, panel, *accs)
+    )(factor, owner, rhs, v, residual, theirs, solved, panel, table)
 
 
 def to_all(value, axis):
@@ -238,10 +246,6 @@
 
 def exchange(value, mask):
     return lax.ppermute(value, "prow", [(i, i ^ mask) for i in range(GRID)])
-
-
-def after(value, *others):
-    return lax.optimization_barrier((value,) + others)[0]
 
 
 def body(seeds, tile_owner, vector, rhs, panel, tile_scales, inverses):
@@ -280,34 +284,34 @@
     near, far, parts, v = lax.optimization_barrier((own[:NEAR], own[NEAR:], parts, v))
     near = jnp.stack([near] + [exchange(near, m) for m in (1, 2, 3)])
     far = jnp.stack([far] + [exchange(far, m) for m in (4, 8, 12)])
-    accs = []
-    _, own_sum = hash_rows(seed_rows, meta, v, RT_DEV - 1, 0, True)
-    their_sum = exchange(own_sum, KB)
+    table = hash_rows(seed_rows, meta, v, jnp.zeros((KB, PIECE), jnp.float32), parts, 0)
     part = jnp.sum(lax.all_to_all(parts, "pcol", 0, 0, tiled=True), axis=0)
-    near, far, part, own_sum = lax.optimization_barrier((near, far, part, own_sum))
-    tiles = [near] + [exchange(near, m) for m in (4, 8, 12)] + [far] + [exchange(far, m) for m in (1, 2, 3)]
-    came = to_all(part, "prow")
-    here = after(v, part)
-    for n in range(AHEAD):
-        accs.append(hash_rows(seed_rows, meta, here, *divmod(n * PIECE, NB))[0])
-        here = after(v, accs[-1])
-    residual = after(jnp.sum(came, axis=0), accs[-1])
+    near, far, part, table = lax.optimization_barrier((near, far, part, table))
+    first, second = exchange(far, 1), exchange(far, 2)
+    across = [exchange(near, m) for m in (4, 8, 12)]
+    far, first = lax.optimization_barrier((far, first))
+    tiles = [near] + across + [far, first, second, exchange(far, 3)]
+    came = to_all(jnp.concatenate([part, jnp.pad(table[:1], ((0, 0), (0, PIECE)))]), "prow")
+    row = 1
+    for _ in range(AHEAD):
+        table = hash_rows(seed_rows, meta, v, table, part, row)
+        row += 1
+    residual = jnp.sum(came[:, :1], axis=0)
+    theirs = lax.dynamic_slice_in_dim(came, jnp.mod(row_index + KB, GRID), 1, 0)[0, 1:, :PIECE]
 
     running, solved = None, None
     for k in range(KB):
-        total, solved = step(k, residual, running, solved, inverses, tiles)
+        total, solved = step(k, residual, running, solved, inverses, tiles, table)
         if k == KB - 1:
             break
         same = lax.ppermute(total, "pcol", [(2 * k + h, 2 * k + 2 + h) for h in range(2)])
         other = lax.ppermute(total, "pcol", [(2 * k + h, 2 * k + 3 - h) for h in range(2)])
         if k in GAPS:
-            accs.append(hash_rows(seed_rows, meta, after(v, total), *divmod(len(accs) * PIECE, NB))[0])
-            same = after(same, accs[-1])
+            table = hash_rows(seed_rows, meta, v, table, total, row)
+            row += 1
         running = (same, other)
 
-    sums = last(
-        factor, tile_owner, rhs.reshape(GRID, LANES), v, residual, own_sum, their_sum, solved, panel, accs
-    )
+    sums = last(factor, tile_owner, rhs.reshape(GRID, LANES), v, residual, theirs, solved, panel, table)
     updated = jnp.sum(lax.all_to_all(sums, "pcol", 0, 0, tiled=True), axis=0)
     return (solved.reshape(256), updated)
 

time: 157 us -> 152 us (0.968)
  Pallas kernels: 65 us -> 59.4 us
  waiting for transfers between devices: 9.65 us -> 5.69 us
  blocking collectives: 16.1 us -> 18 us
    pallas_call x8, Pallas kernels: 9.15 us -> 3.5 us  [step(): pl.pallas_call(functools.partial(step_kernel, k), out_shape=[jax.ShapeDty...]
    ppermute x13 -> x12, waiting for transfers between devices: 8.77 us -> 4.8 us  [exchange(): return lax.ppermute(value, 'prow', [(i, i ^ mask) for i in range(GRID)])]
    all_to_all x1, starting transfers between devices: 8.47 us -> 6.37 us  [to_all(): lax.all_to_all(jnp.broadcast_to(value[None], (GRID,) + value.shape), axis...]
    ppermute x7, starting transfers between devices: 7.56 us -> 9.55 us  [body(): lax.ppermute(total, 'pcol', [(2 * k + h, 2 * k + 3 - h) for h in range(2)])]
    all_to_all x1, blocking collectives: 16.1 us -> 18 us  [body(): updated = jnp.sum(lax.all_to_all(sums, 'pcol', 0, 0, tiled=True), axis=0)]
    ppermute x13 -> x12, starting transfers between devices: 12.2 us -> 13.5 us  [exchange(): return lax.ppermute(value, 'prow', [(i, i ^ mask) for i in range(GRID)])]
    unnamed x38 -> x44, local copies, waits for them, and re-layouts: 5.26 us -> 5.41 us
  transfers between devices with their start and end apart: 30 -> 29, of which waited for: 3 -> 2; matrix products, arithmetic and copies ran while one was open for 2% -> 3% of each run, Pallas kernels for 36% -> 37%
where the time goes in v3:
time: 152 us; the launch traced here: 150 us
  Pallas kernels  59.4 us (39%)
  starting transfers between devices  52.9 us (35%)
  blocking collectives  18 us (12%)
  local copies, waits for them, and re-layouts  8.1 us (5%)
  waiting for transfers between devices  5.69 us (4%)
  other arithmetic  4.29 us (3%)
    pallas_call x7, Pallas kernels, hash_rows(): pl.pallas_call(functools.partial(hash_kernel, row, tile, start), out_shap...  45 us
    all_to_all x1, blocking collectives, body(): updated = jnp.sum(lax.all_to_all(sums, 'pcol', 0, 0, tiled=True), axis=0)  18 us
    ppermute x12, starting transfers between devices, exchange(): return lax.ppermute(value, 'prow', [(i, i ^ mask) for i in range(GRID)])  13.5 us
    all_to_all x1, starting transfers between devices, body(): part = jnp.sum(lax.all_to_all(parts, 'pcol', 0, 0, tiled=True), axis=0)  11.1 us
    pallas_call x1, Pallas kernels, first_rows(): pl.pallas_call(first_kernel, out_shape=jax.ShapeDtypeStruct((GRID, 1, NB)...  10 us
    ppermute x7, starting transfers between devices, body(): lax.ppermute(total, 'pcol', [(2 * k + h, 2 * k + 3 - h) for h in range(2)])  9.55 us
    all_to_all x1, starting transfers between devices, body(): came = lax.all_to_all(sent, 'prow', 0, 0, tiled=True)  6.55 us
    all_to_all x1, starting transfers between devices, to_all(): lax.all_to_all(jnp.broadcast_to(value[None], (GRID,) + value.shape), axis...  6.37 us
  transfers between devices with their start and end apart: 29, of which 2 were waited for; matrix products, arithmetic and copies ran while one was open for 3% of the time, Pallas kernels for 37%

profile of v3, /device:TPU:29, one launch (start us, length us, event | category | flops | bytes accessed | tf_op | source)
XLA Modules:
  0.0 149.9 jit_solution(9743919392806539415)
XLA Ops:
  1.4 0.7 copy-done.19
  2.8 1.0 multiply_bitcast_fusion
  4.0 1.0 pad_maximum_fusion
  5.0 6.6 %all-to-all-start = ((f32[16,18,512]{2,1,0:T(8,128)}), f32[16,18,512]{2,1,0:T(8,128)S(1)}, u32[]{:S(2)}, u32[]{:S(2)}) async-start(f32[16,18,512]{2,1,0:T(8,128)} %pad_maximum_fusion), calls=%async_computation | async-start | bytes 1572864 | tf_op jit(solution)/shard_map/all_to_all | solution.py:264
  11.7 0.7 slice.45
  12.6 10.0 %first_rows.1._ = f32[16,1,512]{2,1,0:T(1,128)} custom-call(s32[64]{0:T(128)S(1)} %copy-done.14, s32[64,25]{1,0:T(8,128)S(1)} %copy.24.seeds, f32[7,128]{1,0:T(8,128)S(1)} %dynamic-slice_bitcast_fusion.window, f32[1,512]{1,0:T(1,128)S(1)} %bitcast.46, f32[1,512]{1,0:T(1,128)S(1)} %bitcast.45), custom_call_target="tpu_custom_call" | custom-call | flops 6553600 | bytes 32768 | tf_op jit(solution)/shard_map/first_rows/pallas_call | solution.py:89
  23.3 2.4 %collective-permute-start.4 = (f32[3,16,512]{2,1,0:T(8,128)S(1)}, f32[3,16,512]{2,1,0:T(8,128)S(1)}, u32[]{:S(2)}, u32[]{:S(2)}) collective-permute-start(f32[3,16,512]{2,1,0:T(8,128)S(1)} %slice.53), channel_id=1, source_target_pairs={{0,128},{16,144},{32,160},{48,176},{64,192},{80,208},{96,224},{112... | collective-permute-start | bytes 294920 | tf_op jit(solution)/shard_map/ppermute | solution.py:248
  26.6 2.1 %collective-permute-start.1 = (f32[4,16,512]{2,1,0:T(8,128)S(1)}, f32[4,16,512]{2,1,0:T(8,128)S(1)}, u32[]{:S(2)}, u32[]{:S(2)}) collective-permute-start(f32[4,16,512]{2,1,0:T(8,128)S(1)} %slice.52), channel_id=1, source_target_pairs={{0,32},{16,48},{32,0},{48,16},{64,96},{80,112},{96,64},{112,80},{1... | collective-permute-start | bytes 393224 | tf_op jit(solution)/shard_map/ppermute | solution.py:248
  28.7 11.1 %all-to-all-start.1 = ((f32[16,1,512]{2,1,0:T(1,128)}), f32[16,1,512]{2,1,0:T(1,128)S(1)}, u32[]{:S(2)}, u32[]{:S(2)}) async-start(f32[16,1,512]{2,1,0:T(1,128)} %first_rows.1._), calls=%async_computation.1 | async-start | bytes 65536 | tf_op jit(solution)/shard_map/all_to_all | solution.py:288
  39.8 1.0 collective-permute-start
  40.8 6.4 %hash_0.1.table = f32[8,256]{1,0:T(8,128)S(1)} custom-call(s32[4,25]{1,0:T(4,128)S(1)} %pad_add_fusion.seeds, s32[1]{0:T(128)} %bitcast.16.meta, f32[25,4,128]{2,1,0:T(4,128)S(1)} %reshape.43.v, f32[8,256]{1,0:T(8,128)S(1)} %broadcast_in_dim.27.table, f32[16,1,512]{2,1,0:T(1,128)} %first_rows.1._), custom_call_target="tpu_custom_call" | custom-call | flops 6553600 | bytes 131072 | tf_op jit(solution)/shard_map/hash_0/pallas_call | solution.py:125
  48.0 0.9 collective-permute-start.9
  49.2 2.4 %collective-permute-start.7 = (f32[4,4,16,512]{3,2,1,0:T(8,128)S(1)}, f32[4,4,16,512]{3,2,1,0:T(8,128)S(1)}, u32[]{:S(2)}, u32[]{:S(2)}) collective-permute-start(f32[4,4,16,512]{3,2,1,0:T(8,128)S(1)} %pad_maximum_fusion.1.refs_1_.refs_4_), channel_id=1, source_target_pairs={{0,128},{16,144},{32,160},{48,176},{64,192},{80,208},{96,224},{112... | collective-permute-start | bytes 1572872 | tf_op jit(solution)/shard_map/ppermute | solution.py:248
  52.2 1.5 %collective-permute-start.10 = (f32[4,3,16,512]{3,2,1,0:T(8,128)S(1)}, f32[4,3,16,512]{3,2,1,0:T(8,128)S(1)}, u32[]{:S(2)}, u32[]{:S(2)}) collective-permute-start(f32[4,3,16,512]{3,2,1,0:T(8,128)S(1)} %pad_maximum_fusion.2.refs_5_.refs_8_), channel_id=1, source_target_pairs={{0,32},{16,48},{32,0},{48,16},{64,96},{80,112},{96,64},{112,80},{1... | collective-permute-start | bytes 1179656 | tf_op jit(solution)/shard_map/ppermute | solution.py:248
  53.7 4.8 %collective-permute-done.9.refs_6_.refs_9_ = f32[4,3,16,512]{3,2,1,0:T(8,128)S(1)} collective-permute-done((f32[4,3,16,512]{3,2,1,0:T(8,128)S(1)}, f32[4,3,16,512]{3,2,1,0:T(8,128)S(1)}, u32[]{:S(2)}, u32[]{:S(2)}) %collective-permute-start.9) | collective-permute-done | bytes 393248 | tf_op jit(solution)/shard_map/ppermute | solution.py:248
  58.5 1.1 collective-permute-start.11
  60.3 6.4 %all-to-all-start.2 = ((f32[16,2,512]{2,1,0:T(2,128)}), f32[16,2,512]{2,1,0:T(2,128)}, u32[]{:S(2)}, u32[]{:S(2)}) async-start(f32[16,2,512]{2,1,0:T(2,128)} %broadcast_in_dim.28), calls=%async_computation.2 | async-start | bytes 131072 | tf_op jit(solution)/shard_map/all_to_all | solution.py:244
  66.6 0.8 copy-done.3
  67.4 0.7 copy-done.10
  68.1 6.4 %hash_1.1.table = f32[8,256]{1,0:T(8,128)S(1)} custom-call(s32[4,25]{1,0:T(4,128)S(1)} %pad_add_fusion.seeds, s32[1]{0:T(128)} %bitcast.16.meta, f32[25,4,128]{2,1,0:T(4,128)S(1)} %copy-done.3, f32[8,256]{1,0:T(8,128)S(1)} %hash_0.1.table, f32[1,512]{1,0:T(1,128)S(1)} %bitcast.42), custom_call_target="tpu_custom_call" | custom-call | flops 6553600 | bytes 131072 | tf_op jit(solution)/shard_map/hash_1/pallas_call | solution.py:125
  74.5 6.4 %hash_2.1.refs_9_.refs_12_.table = f32[8,256]{1,0:T(8,128)S(1)} custom-call(s32[4,25]{1,0:T(4,128)S(1)} %pad_add_fusion.seeds, s32[1]{0:T(128)} %bitcast.16.meta, f32[25,4,128]{2,1,0:T(4,128)S(1)} %copy-done.3, f32[8,256]{1,0:T(8,128)S(1)} %hash_1.1.table, f32[1,512]{1,0:T(1,128)S(1)} %bitcast.43), custom_call_target="tpu_custom_call" | custom-call | flops 6553600 | bytes 131072 | tf_op jit(solution)/shard_map/hash_2/pallas_call | solution.py:125
  81.0 0.9 slice_reduce_fusion
  81.9 1.3 step_0.1
  83.3 5.0 %collective-permute-start.13 = (f32[8,512]{1,0:T(8,128)S(1)}, f32[8,512]{1,0:T(8,128)S(1)}, u32[]{:S(2)}, u32[]{:S(2)}) collective-permute-start(f32[8,512]{1,0:T(8,128)S(1)} %get-tuple-element.37), channel_id=1, source_target_pairs={{0,3},{1,2},{16,19},{17,18},{32,35},{33,34},{48,51},{49,50},{64,67... | collective-permute-start | bytes 49160 | tf_op jit(solution)/shard_map/ppermute | solution.py:308
  88.3 1.3 collective-permute-start.12
  89.6 0.8 collective-permute-done.12.refs_0_
  90.5 0.7 collective-permute-start.15
  91.1 0.7 collective-permute-start.14
  91.8 6.4 %hash_3.1.refs_12_.table = f32[8,256]{1,0:T(8,128)S(1)} custom-call(s32[4,25]{1,0:T(4,128)S(1)} %copy-done.8, s32[1]{0:T(128)} %bitcast.16.meta, f32[25,4,128]{2,1,0:T(4,128)S(1)} %copy-done.4, f32[8,256]{1,0:T(8,128)S(1)} %hash_2.1.refs_9_.refs_12_.table, f32[8,512]{1,0:T(8,128)S(1)} %get-tuple-element.39._), custom_call_target="tpu_custom_call" | custom-call | flops 6553600 | bytes 131072 | tf_op jit(solution)/shard_map/hash_3/pallas_call | solution.py:125
  98.3 0.7 collective-permute-start.17
  99.0 0.7 collective-permute-start.16
  99.7 6.4 %hash_4.1.refs_12_.table = f32[8,256]{1,0:T(8,128)S(1)} custom-call(s32[4,25]{1,0:T(4,128)S(1)} %copy-done.8, s32[1]{0:T(128)} %bitcast.16.meta, f32[25,4,128]{2,1,0:T(4,128)S(1)} %copy-done.4, f32[8,256]{1,0:T(8,128)S(1)} %hash_3.1.refs_12_.table, f32[8,512]{1,0:T(8,128)S(1)} %get-tuple-element.41._), custom_call_target="tpu_custom_call" | custom-call | flops 6553600 | bytes 131072 | tf_op jit(solution)/shard_map/hash_4/pallas_call | solution.py:125
  106.2 0.7 collective-permute-start.19
  106.8 0.7 collective-permute-start.18
  107.5 6.4 %hash_5.1.refs_12_.table = f32[8,256]{1,0:T(8,128)S(1)} custom-call(s32[4,25]{1,0:T(4,128)S(1)} %copy-done.8, s32[1]{0:T(128)} %bitcast.16.meta, f32[25,4,128]{2,1,0:T(4,128)S(1)} %copy-done.4, f32[8,256]{1,0:T(8,128)S(1)} %hash_4.1.refs_12_.table, f32[8,512]{1,0:T(8,128)S(1)} %get-tuple-element.43._), custom_call_target="tpu_custom_call" | custom-call | flops 6553600 | bytes 131072 | tf_op jit(solution)/shard_map/hash_5/pallas_call | solution.py:125
  114.0 0.7 collective-permute-start.21
  114.7 0.7 collective-permute-start.20
  115.3 6.4 %hash_6.1.refs_12_.table = f32[8,256]{1,0:T(8,128)S(1)} custom-call(s32[4,25]{1,0:T(4,128)S(1)} %copy-done.8, s32[1]{0:T(128)} %bitcast.16.meta, f32[25,4,128]{2,1,0:T(4,128)S(1)} %copy-done.4, f32[8,256]{1,0:T(8,128)S(1)} %hash_5.1.refs_12_.table, f32[8,512]{1,0:T(8,128)S(1)} %get-tuple-element.45._), custom_call_target="tpu_custom_call" | custom-call | flops 6553600 | bytes 131072 | tf_op jit(solution)/shard_map/hash_6/pallas_call | solution.py:125
  121.8 0.7 step_5.1
  123.0 1.2 collective-permute-start.23
  124.3 1.2 collective-permute-start.22
  125.5 0.7 copy-done.18
  126.2 0.7 step_6.1
  127.0 0.7 collective-permute-start.25
  127.6 0.7 collective-permute-start.24
  128.3 0.7 fusion.2.theirs
  130.5 0.9 last.1
  131.4 18.0 %all_to_all.24 = f32[16,1,128]{2,1,0:T(1,128)S(1)} all-to-all(f32[16,1,128]{2,1,0:T(1,128)S(1)} %bitcast.40), channel_id=1, replica_groups=mesh['prow'=16,'pcol'=16] {'pcol'}, dimensions={0} | all-to-all | bytes 16384 | tf_op jit(solution)/shard_map/all_to_all | solution.py:315
  (104 shorter events, 8.2 us)
Async XLA Ops:
  0.6 1.4 copy-start
  0.7 0.7 copy-start.14
  1.4 0.7 copy-start.19
  5.0 17.7 %all-to-all-start = ((f32[16,18,512]{2,1,0:T(8,128)}), f32[16,18,512]{2,1,0:T(8,128)S(1)}, u32[]{:S(2)}, u32[]{:S(2)}) async-start(f32[16,18,512]{2,1,0:T(8,128)} %pad_maximum_fusion), calls=%async_computation | async-start | bytes 1572864 | tf_op jit(solution)/shard_map/all_to_all | solution.py:264
  11.6 0.8 copy-start.20
  22.9 24.3 %copy-start.2 = (f32[25,4,128]{2,1,0:T(4,128)}, f32[25,4,128]{2,1,0:T(4,128)S(1)}, u32[]{:S(2)}) copy-start(f32[25,4,128]{2,1,0:T(4,128)S(1)} %reshape.43.v) | copy-start | bytes 153604
  22.9 16.8 %collective-permute-start.5 = (f32[3,16,512]{2,1,0:T(8,128)S(1)}, f32[3,16,512]{2,1,0:T(8,128)S(1)}, u32[]{:S(2)}, u32[]{:S(2)}) collective-permute-start(f32[3,16,512]{2,1,0:T(8,128)S(1)} %slice.53), channel_id=1, source_target_pairs={{0,192},{16,208},{32,224},{48,240},{64,128},{80,144},{96,160},{112... | collective-permute-start | bytes 294920 | tf_op jit(solution)/shard_map/ppermute | solution.py:248
  23.3 24.6 %collective-permute-start.4 = (f32[3,16,512]{2,1,0:T(8,128)S(1)}, f32[3,16,512]{2,1,0:T(8,128)S(1)}, u32[]{:S(2)}, u32[]{:S(2)}) collective-permute-start(f32[3,16,512]{2,1,0:T(8,128)S(1)} %slice.53), channel_id=1, source_target_pairs={{0,128},{16,144},{32,160},{48,176},{64,192},{80,208},{96,224},{112... | collective-permute-start | bytes 294920 | tf_op jit(solution)/shard_map/ppermute | solution.py:248
  25.7 22.2 %collective-permute-start.3 = (f32[3,16,512]{2,1,0:T(8,128)S(1)}, f32[3,16,512]{2,1,0:T(8,128)S(1)}, u32[]{:S(2)}, u32[]{:S(2)}) collective-permute-start(f32[3,16,512]{2,1,0:T(8,128)S(1)} %slice.53), channel_id=1, source_target_pairs={{0,64},{16,80},{32,96},{48,112},{64,0},{80,16},{96,32},{112,48},{1... | collective-permute-start | bytes 294920 | tf_op jit(solution)/shard_map/ppermute | solution.py:248
  26.3 21.6 %collective-permute-start.2 = (f32[4,16,512]{2,1,0:T(8,128)S(1)}, f32[4,16,512]{2,1,0:T(8,128)S(1)}, u32[]{:S(2)}, u32[]{:S(2)}) collective-permute-start(f32[4,16,512]{2,1,0:T(8,128)S(1)} %slice.52), channel_id=1, source_target_pairs={{0,48},{16,32},{32,16},{48,0},{64,112},{80,96},{96,80},{112,64},{1... | collective-permute-start | bytes 393224 | tf_op jit(solution)/shard_map/ppermute | solution.py:248
  26.6 21.4 %collective-permute-start.1 = (f32[4,16,512]{2,1,0:T(8,128)S(1)}, f32[4,16,512]{2,1,0:T(8,128)S(1)}, u32[]{:S(2)}, u32[]{:S(2)}) collective-permute-start(f32[4,16,512]{2,1,0:T(8,128)S(1)} %slice.52), channel_id=1, source_target_pairs={{0,32},{16,48},{32,0},{48,16},{64,96},{80,112},{96,64},{112,80},{1... | collective-permute-start | bytes 393224 | tf_op jit(solution)/shard_map/ppermute | solution.py:248
  28.7 18.6 %all-to-all-start.1 = ((f32[16,1,512]{2,1,0:T(1,128)}), f32[16,1,512]{2,1,0:T(1,128)S(1)}, u32[]{:S(2)}, u32[]{:S(2)}) async-start(f32[16,1,512]{2,1,0:T(1,128)} %first_rows.1._), calls=%async_computation.1 | async-start | bytes 65536 | tf_op jit(solution)/shard_map/all_to_all | solution.py:288
  39.8 8.2 %collective-permute-start = (f32[4,16,512]{2,1,0:T(8,128)S(1)}, f32[4,16,512]{2,1,0:T(8,128)S(1)}, u32[]{:S(2)}, u32[]{:S(2)}) collective-permute-start(f32[4,16,512]{2,1,0:T(8,128)S(1)} %slice.52), channel_id=1, source_target_pairs={{0,16},{16,0},{32,48},{48,32},{64,80},{80,64},{96,112},{112,96},{1... | collective-permute-start | bytes 393224 | tf_op jit(solution)/shard_map/ppermute | solution.py:248
  40.8 33.8 %copy-start.7 = (s32[4,25]{1,0:T(4,128)}, s32[4,25]{1,0:T(4,128)S(1)}, u32[]{:S(2)}) copy-start(s32[4,25]{1,0:T(4,128)S(1)} %pad_add_fusion.seeds) | copy-start | bytes 1204
  48.0 11.6 %copy-start.9 = (f32[512]{0:T(512)S(1)}, f32[512]{0:T(512)}, u32[]{:S(2)}) copy-start(f32[512]{0:T(512)} %reduce_sum.31) | copy-start | bytes 6148
  48.0 33.9 %copy-start.1 = (bf16[256,512]{1,0:T(8,128)(2,1)S(1)}, bf16[256,512]{1,0:T(8,128)(2,1)}, u32[]{:S(2)}) copy-start(bf16[256,512]{1,0:T(8,128)(2,1)} %refs_3_.13) | copy-start | bytes 786436
  48.0 10.4 %collective-permute-start.9 = (f32[4,3,16,512]{3,2,1,0:T(8,128)S(1)}, f32[4,3,16,512]{3,2,1,0:T(8,128)S(1)}, u32[]{:S(2)}, u32[]{:S(2)}) collective-permute-start(f32[4,3,16,512]{3,2,1,0:T(8,128)S(1)} %pad_maximum_fusion.2.refs_5_.refs_8_), channel_id=1, source_target_pairs={{0,16},{16,0},{32,48},{48,32},{64,80},{80,64},{96,112},{112,96},{1... | collective-permute-start | bytes 1179656 | tf_op jit(solution)/shard_map/ppermute | solution.py:248
  48.9 33.0 %collective-permute-start.8 = (f32[4,4,16,512]{3,2,1,0:T(8,128)S(1)}, f32[4,4,16,512]{3,2,1,0:T(8,128)S(1)}, u32[]{:S(2)}, u32[]{:S(2)}) collective-permute-start(f32[4,4,16,512]{3,2,1,0:T(8,128)S(1)} %pad_maximum_fusion.1.refs_1_.refs_4_), channel_id=1, source_target_pairs={{0,192},{16,208},{32,224},{48,240},{64,128},{80,144},{96,160},{112... | collective-permute-start | bytes 1572872 | tf_op jit(solution)/shard_map/ppermute | solution.py:248
  49.2 32.7 %collective-permute-start.7 = (f32[4,4,16,512]{3,2,1,0:T(8,128)S(1)}, f32[4,4,16,512]{3,2,1,0:T(8,128)S(1)}, u32[]{:S(2)}, u32[]{:S(2)}) collective-permute-start(f32[4,4,16,512]{3,2,1,0:T(8,128)S(1)} %pad_maximum_fusion.1.refs_1_.refs_4_), channel_id=1, source_target_pairs={{0,128},{16,144},{32,160},{48,176},{64,192},{80,208},{96,224},{112... | collective-permute-start | bytes 1572872 | tf_op jit(solution)/shard_map/ppermute | solution.py:248
  51.6 30.3 %collective-permute-start.6 = (f32[4,4,16,512]{3,2,1,0:T(8,128)S(1)}, f32[4,4,16,512]{3,2,1,0:T(8,128)S(1)}, u32[]{:S(2)}, u32[]{:S(2)}) collective-permute-start(f32[4,4,16,512]{3,2,1,0:T(8,128)S(1)} %pad_maximum_fusion.1.refs_1_.refs_4_), channel_id=1, source_target_pairs={{0,64},{16,80},{32,96},{48,112},{64,0},{80,16},{96,32},{112,48},{1... | collective-permute-start | bytes 1572872 | tf_op jit(solution)/shard_map/ppermute | solution.py:248
  52.2 29.7 %collective-permute-start.10 = (f32[4,3,16,512]{3,2,1,0:T(8,128)S(1)}, f32[4,3,16,512]{3,2,1,0:T(8,128)S(1)}, u32[]{:S(2)}, u32[]{:S(2)}) collective-permute-start(f32[4,3,16,512]{3,2,1,0:T(8,128)S(1)} %pad_maximum_fusion.2.refs_5_.refs_8_), channel_id=1, source_target_pairs={{0,32},{16,48},{32,0},{48,16},{64,96},{80,112},{96,64},{112,80},{1... | collective-permute-start | bytes 1179656 | tf_op jit(solution)/shard_map/ppermute | solution.py:248
  58.5 23.4 %collective-permute-start.11 = (f32[4,3,16,512]{3,2,1,0:T(8,128)S(1)}, f32[4,3,16,512]{3,2,1,0:T(8,128)}, u32[]{:S(2)}, u32[]{:S(2)}) collective-permute-start(f32[4,3,16,512]{3,2,1,0:T(8,128)S(1)} %pad_maximum_fusion.2.refs_5_.refs_8_), channel_id=1, source_target_pairs={{0,48},{16,32},{32,16},{48,0},{64,112},{80,96},{96,80},{112,64},{1... | collective-permute-start | bytes 1179656 | tf_op jit(solution)/shard_map/ppermute | solution.py:248
  60.3 20.7 %all-to-all-start.2 = ((f32[16,2,512]{2,1,0:T(2,128)}), f32[16,2,512]{2,1,0:T(2,128)}, u32[]{:S(2)}, u32[]{:S(2)}) async-start(f32[16,2,512]{2,1,0:T(2,128)} %broadcast_in_dim.28), calls=%async_computation.2 | async-start | bytes 131072 | tf_op jit(solution)/shard_map/all_to_all | solution.py:244
  66.6 0.8 copy-start.3
  67.4 0.7 copy-start.10
  83.3 6.3 %collective-permute-start.13 = (f32[8,512]{1,0:T(8,128)S(1)}, f32[8,512]{1,0:T(8,128)S(1)}, u32[]{:S(2)}, u32[]{:S(2)}) collective-permute-start(f32[8,512]{1,0:T(8,128)S(1)} %get-tuple-element.37), channel_id=1, source_target_pairs={{0,3},{1,2},{16,19},{17,18},{32,35},{33,34},{48,51},{49,50},{64,67... | collective-permute-start | bytes 49160 | tf_op jit(solution)/shard_map/ppermute | solution.py:308
  88.3 2.1 %collective-permute-start.12 = (f32[8,512]{1,0:T(8,128)S(1)}, f32[8,512]{1,0:T(8,128)S(1)}, u32[]{:S(2)}, u32[]{:S(2)}) collective-permute-start(f32[8,512]{1,0:T(8,128)S(1)} %get-tuple-element.37), channel_id=1, source_target_pairs={{0,2},{1,3},{16,18},{17,19},{32,34},{33,35},{48,50},{49,51},{64,66... | collective-permute-start | bytes 49160 | tf_op jit(solution)/shard_map/ppermute | solution.py:307
  90.4 1.4 copy-start.4
  90.4 1.4 copy-start.8
  90.5 7.8 %collective-permute-start.15 = (f32[8,512]{1,0:T(8,128)S(1)}, f32[8,512]{1,0:T(8,128)S(1)}, u32[]{:S(2)}, u32[]{:S(2)}) collective-permute-start(f32[8,512]{1,0:T(8,128)S(1)} %get-tuple-element.39._), channel_id=1, source_target_pairs={{2,5},{3,4},{18,21},{19,20},{34,37},{35,36},{50,53},{51,52},{66,69... | collective-permute-start | bytes 49160 | tf_op jit(solution)/shard_map/ppermute | solution.py:308
  91.1 7.1 %collective-permute-start.14 = (f32[8,512]{1,0:T(8,128)S(1)}, f32[8,512]{1,0:T(8,128)S(1)}, u32[]{:S(2)}, u32[]{:S(2)}) collective-permute-start(f32[8,512]{1,0:T(8,128)S(1)} %get-tuple-element.39._), channel_id=1, source_target_pairs={{2,4},{3,5},{18,20},{19,21},{34,36},{35,37},{50,52},{51,53},{66,68... | collective-permute-start | bytes 49160 | tf_op jit(solution)/shard_map/ppermute | solution.py:307
  98.3 7.8 %collective-permute-start.17 = (f32[8,512]{1,0:T(8,128)S(1)}, f32[8,512]{1,0:T(8,128)S(1)}, u32[]{:S(2)}, u32[]{:S(2)}) collective-permute-start(f32[8,512]{1,0:T(8,128)S(1)} %get-tuple-element.41._), channel_id=1, source_target_pairs={{4,7},{5,6},{20,23},{21,22},{36,39},{37,38},{52,55},{53,54},{68,71... | collective-permute-start | bytes 49160 | tf_op jit(solution)/shard_map/ppermute | solution.py:308
  99.0 7.1 %collective-permute-start.16 = (f32[8,512]{1,0:T(8,128)S(1)}, f32[8,512]{1,0:T(8,128)S(1)}, u32[]{:S(2)}, u32[]{:S(2)}) collective-permute-start(f32[8,512]{1,0:T(8,128)S(1)} %get-tuple-element.41._), channel_id=1, source_target_pairs={{4,6},{5,7},{20,22},{21,23},{36,38},{37,39},{52,54},{53,55},{68,70... | collective-permute-start | bytes 49160 | tf_op jit(solution)/shard_map/ppermute | solution.py:307
  106.2 7.8 %collective-permute-start.19 = (f32[8,512]{1,0:T(8,128)S(1)}, f32[8,512]{1,0:T(8,128)S(1)}, u32[]{:S(2)}, u32[]{:S(2)}) collective-permute-start(f32[8,512]{1,0:T(8,128)S(1)} %get-tuple-element.43._), channel_id=1, source_target_pairs={{6,9},{7,8},{22,25},{23,24},{38,41},{39,40},{54,57},{55,56},{70,73... | collective-permute-start | bytes 49160 | tf_op jit(solution)/shard_map/ppermute | solution.py:308
  106.8 7.1 %collective-permute-start.18 = (f32[8,512]{1,0:T(8,128)S(1)}, f32[8,512]{1,0:T(8,128)S(1)}, u32[]{:S(2)}, u32[]{:S(2)}) collective-permute-start(f32[8,512]{1,0:T(8,128)S(1)} %get-tuple-element.43._), channel_id=1, source_target_pairs={{6,8},{7,9},{22,24},{23,25},{38,40},{39,41},{54,56},{55,57},{70,72... | collective-permute-start | bytes 49160 | tf_op jit(solution)/shard_map/ppermute | solution.py:307
  114.0 7.8 %collective-permute-start.21 = (f32[8,512]{1,0:T(8,128)S(1)}, f32[8,512]{1,0:T(8,128)S(1)}, u32[]{:S(2)}, u32[]{:S(2)}) collective-permute-start(f32[8,512]{1,0:T(8,128)S(1)} %get-tuple-element.45._), channel_id=1, source_target_pairs={{8,11},{9,10},{24,27},{25,26},{40,43},{41,42},{56,59},{57,58},{72,... | collective-permute-start | bytes 49160 | tf_op jit(solution)/shard_map/ppermute | solution.py:308
  114.7 7.1 %collective-permute-start.20 = (f32[8,512]{1,0:T(8,128)S(1)}, f32[8,512]{1,0:T(8,128)S(1)}, u32[]{:S(2)}, u32[]{:S(2)}) collective-permute-start(f32[8,512]{1,0:T(8,128)S(1)} %get-tuple-element.45._), channel_id=1, source_target_pairs={{8,10},{9,11},{24,26},{25,27},{40,42},{41,43},{56,58},{57,59},{72,... | collective-permute-start | bytes 49160 | tf_op jit(solution)/shard_map/ppermute | solution.py:307
  123.0 2.5 %collective-permute-start.23 = (f32[8,512]{1,0:T(8,128)}, f32[8,512]{1,0:T(8,128)}, u32[]{:S(2)}, u32[]{:S(2)}) collective-permute-start(f32[8,512]{1,0:T(8,128)} %get-tuple-element.47), channel_id=1, source_target_pairs={{10,13},{11,12},{26,29},{27,28},{42,45},{43,44},{58,61},{59,60},{7... | collective-permute-start | bytes 49160 | tf_op jit(solution)/shard_map/ppermute | solution.py:308
  124.3 1.3 collective-permute-start.22
  125.5 0.7 copy-start.18
  127.0 2.0 %collective-permute-start.25 = (f32[8,512]{1,0:T(8,128)S(1)}, f32[8,512]{1,0:T(8,128)S(1)}, u32[]{:S(2)}, u32[]{:S(2)}) collective-permute-start(f32[8,512]{1,0:T(8,128)S(1)} %get-tuple-element.49), channel_id=1, source_target_pairs={{12,15},{13,14},{28,31},{29,30},{44,47},{45,46},{60,63},{61,62},{7... | collective-permute-start | bytes 49160 | tf_op jit(solution)/shard_map/ppermute | solution.py:308
  127.6 1.4 collective-permute-start.24
  129.0 0.8 copy-start.5
  129.0 1.3 copy-start.6
  129.0 1.2 copy-start.11
  129.7 0.8 copy-start.16
  129.7 0.8 copy-start.13
  129.7 0.8 copy-start.15
  (2 other events, 1.0 us)

commit v4 on v3

--- a/solution.py
+++ b/solution.py
@@ -22,7 +22,7 @@
 WIDE = 64
 WINDOW = 7
 AHEAD = 2
-GAPS = (1, 2, 3, 4)
+GAPS = (1, 2, 3, 5)
 BIAS = -127.5
 
 VMEM = pl.BlockSpec(memory_space=pltpu.VMEM)
@@ -136,22 +136,25 @@
     )(seeds, meta, v, table, token)
 
 
-def step_kernel(k, residual, *refs):
+def step_kernel(k, came, *refs):
     refs = list(refs)
-    same, other, solved_in = [refs.pop(0) for _ in range(3)] if k > 0 else [None] * 3
-    inv = refs.pop(0)
-    near, far = refs[:4], refs[4:8]
-    _, total_out, solved_out, spread_y, held, sem = refs[8:]
+    same, other = [refs.pop(0) for _ in range(2)] if k > 0 else [None] * 2
+    inv, table = refs.pop(0), refs.pop(0)
+    near = [refs.pop(0) for _ in range(4)] if k < NEAR else None
+    far = [refs.pop(0) for _ in range(4)] if k < KB - 1 else None
+    total_out = refs.pop(0) if k < KB - 1 else None
+    table_out, spread_y, held, sem = refs
     col = lax.axis_index("pcol")
     me = lax.axis_index("prow")
     mine = col // 2 == k
+    table_out[...] = table[...]
 
     @pl.when(mine)
     def _():
-        if k < KB - 1:
-            fetch = pltpu.make_async_copy(far[3].at[:, max(k - NEAR, 0):], held, sem)
+        if k < NEAR:
+            fetch = pltpu.make_async_copy(near[1].at[:, k:], held, sem)
             fetch.start()
-        s = residual[...]
+        s = jnp.sum(came[:, :1, :], axis=0)
         if k > 0:
             running = same[...] + other[...]
             s = s - running[k:k + 1, :]
@@ -159,18 +162,17 @@
         if k < KB - 1:
             spread_y[...] = jnp.broadcast_to(y, (256, LANES)).reshape(GRID, 16, LANES)
             rows = [jnp.zeros((1, NB), jnp.float32)] * (k + 1)
+            if k < NEAR:
+                fetch.wait()
             for kk in range(k, KB - 1):
-                if kk == max(k, NEAR):
-                    fetch.wait()
                 part = jnp.zeros((16, NB), jnp.float32)
                 for m in range(4):
                     for i in range(4):
                         if kk < NEAR:
-                            tile, source = near[m][i, kk], me ^ (4 * m + i)
-                        elif m < 3:
+                            tile = held[i, kk - k] if m == 1 else near[m][i, kk]
+                            source = me ^ (4 * m + i)
+                        else:
                             tile, source = far[m][i, kk - NEAR], me ^ (4 * i + m)
-                        else:
-                            tile, source = held[i, kk - max(k, NEAR)], me ^ (4 * i + m)
                         part = part + tile * jnp.concatenate([spread_y[source]] * GROUPS, axis=1)
                 rows.append(jnp.sum(part, axis=0, keepdims=True))
             update = jnp.concatenate(rows, axis=0)
@@ -178,39 +180,46 @@
                 update = update + jnp.where(col % 2 == 0, running, 0.0)
             total_out[...] = update
         eye = lax.broadcasted_iota(jnp.int32, (256, 256), 0) == lax.broadcasted_iota(jnp.int32, (256, 256), 1)
-        solved_out[...] = jnp.sum(jnp.where(eye, y, 0.0), axis=0, keepdims=True)
-
-    @pl.when(jnp.logical_not(mine))
-    def _():
-        if k > 0:
-            solved_out[...] = solved_in[...]
-        else:
-            solved_out[...] = jnp.zeros_like(solved_out)
-        if k < KB - 1:
+        table_out[KB - 1:KB, :] = jnp.sum(jnp.where(eye, y, 0.0), axis=0, keepdims=True)
+
+    if k < KB - 1:
+        @pl.when(jnp.logical_not(mine))
+        def _():
             total_out[...] = jnp.zeros_like(total_out)
 
 
-def step(k, residual, running, solved, inv, tiles, token):
-    args = (residual,) if k == 0 else (residual, running[0], running[1], solved)
+def step(k, came, running, inv, table, tiles):
+    args = [came, *running, inv, table]
+    shapes = [jax.ShapeDtypeStruct((KB, PIECE), jnp.float32)]
+    in_specs = [VMEM] * len(args)
+    if k < NEAR:
+        args += tiles[:4]
+        in_specs += [VMEM, ANY, VMEM, VMEM]
+    if k < KB - 1:
+        args += tiles[4:]
+        in_specs += [VMEM] * 4
+        shapes = [jax.ShapeDtypeStruct((KB, NB), jnp.float32)] + shapes
     return pl.pallas_call(
         functools.partial(step_kernel, k),
-        out_shape=[jax.ShapeDtypeStruct((KB, NB), jnp.float32), jax.ShapeDtypeStruct((1, 256), jnp.float32)],
-        in_specs=[VMEM] * (len(args) + 8) + [ANY, VMEM],
-        out_specs=[VMEM] * 2,
+        out_shape=shapes,
+        in_specs=in_specs,
+        out_specs=[VMEM] * len(shapes),
         scratch_shapes=[
             pltpu.VMEM((GRID, 16, LANES), jnp.float32),
-            pltpu.VMEM((4, min(KB - 1 - NEAR, max(KB - 1 - k, 1)), 16, NB), jnp.float32),
+            pltpu.VMEM((4, max(NEAR - k, 1), 16, NB), jnp.float32),
             pltpu.SemaphoreType.DMA,
         ],
         compiler_params=LIMIT,
         name=f"step_{k}",
-    )(*args, inv, *tiles, token)
-
-
-def last_kernel(factor, owner, rhs, v, residual, theirs, solved, panel, table, out):
+    )(*args)
+
+
+def last_kernel(factor, owner, rhs, v, came, panel, table, out):
     row_index, col_index = lax.axis_index("prow"), lax.axis_index("pcol")
     my_tile = (row_index - owner[0] + GRID) & (GRID - 1)
-    y = solved[...]
+    y = table[KB - 1:KB, :]
+    residual = jnp.sum(came[:, :1, :], axis=0)
+    theirs = came[(row_index + KB) & (GRID - 1), 1:, :]
     for at in range(0, ROWS, LANES):
         n = at // LANES
         part = panel[at:at + LANES, :].astype(jnp.float32) * y
@@ -229,15 +238,15 @@
         out[n:n + 1, :] = given - total
 
 
-def last(factor, owner, rhs, v, residual, theirs, solved, panel, table):
+def last(factor, owner, rhs, v, came, panel, table):
     return pl.pallas_call(
         last_kernel,
         out_shape=jax.ShapeDtypeStruct((GRID, LANES), jnp.float32),
-        in_specs=[SMEM] * 2 + [VMEM] * 7,
+        in_specs=[SMEM] * 2 + [VMEM] * 5,
         out_specs=VMEM,
         compiler_params=LIMIT,
         name="last",
-    )(factor, owner, rhs, v, residual, theirs, solved, panel, table)
+    )(factor, owner, rhs, v, came, panel, table)
 
 
 def to_all(value, axis):
@@ -296,24 +305,21 @@
     for _ in range(AHEAD):
         table = hash_rows(seed_rows, meta, v, table, part, row)
         row += 1
-    residual = jnp.sum(came[:, :1], axis=0)
-    theirs = lax.dynamic_slice_in_dim(came, jnp.mod(row_index + KB, GRID), 1, 0)[0, 1:, :PIECE]
-
-    running, solved = None, None
-    for k in range(KB):
-        total, solved = step(k, residual, running, solved, inverses, tiles, table)
-        if k == KB - 1:
-            break
+
+    running = ()
+    for k in range(KB - 1):
+        total, table = step(k, came, running, inverses, table, tiles)
         same = lax.ppermute(total, "pcol", [(2 * k + h, 2 * k + 2 + h) for h in range(2)])
         other = lax.ppermute(total, "pcol", [(2 * k + h, 2 * k + 3 - h) for h in range(2)])
         if k in GAPS:
             table = hash_rows(seed_rows, meta, v, table, total, row)
             row += 1
         running = (same, other)
-
-    sums = last(factor, tile_owner, rhs.reshape(GRID, LANES), v, residual, theirs, solved, panel, table)
+    table = step(KB - 1, came, running, inverses, table, tiles)[0]
+
+    sums = last(factor, tile_owner, rhs.reshape(GRID, LANES), v, came, panel, table)
     updated = jnp.sum(lax.all_to_all(sums, "pcol", 0, 0, tiled=True), axis=0)
-    return (solved.reshape(256), updated)
+    return (table[KB - 1], updated)
 
 
 def solution(mesh):

time: 152 us -> 143 us (0.941)
  blocking collectives: 18 us -> 0 us
  starting transfers between devices: 52.9 us -> 61.3 us
  waiting for transfers between devices: 5.69 us -> 12.1 us
  local copies, waits for them, and re-layouts: 8.1 us -> 5.12 us
    all_to_all x1 -> x0, blocking collectives: 18 us -> none  [body(): updated = jnp.sum(lax.all_to_all(sums, 'pcol', 0, 0, tiled=True), axis=0)]
    all_to_all x0 -> x1, starting transfers between devices: none -> 9.61 us  [body(): updated = jnp.sum(lax.all_to_all(sums, 'pcol', 0, 0, tiled=True), axis=0)]
    all_to_all x0 -> x1, waiting for transfers between devices: none -> 6.46 us  [body(): updated = jnp.sum(lax.all_to_all(sums, 'pcol', 0, 0, tiled=True), axis=0)]
    unnamed x44 -> x22, local copies, waits for them, and re-layouts: 5.41 us -> 3.25 us
    pallas_call x8, Pallas kernels: 3.5 us -> 1.84 us  [step(): pl.pallas_call(functools.partial(step_kernel, k), out_shape=shapes, in_sp...]
  transfers between devices with their start and end apart: 29 -> 30, of which waited for: 2 -> 3; matrix products, arithmetic and copies ran while one was open for 3% -> 1% of each run, Pallas kernels for 37% -> 39%
where the time goes in v4:
time: 143 us; the launch traced here: 141 us
  starting transfers between devices  61.3 us (43%)
  Pallas kernels  58.4 us (41%)
  waiting for transfers between devices  12.1 us (8%)
  local copies, waits for them, and re-layouts  5.12 us (4%)
  other arithmetic  2.84 us (2%)
  between operations  1.46 us (1%)
    pallas_call x7, Pallas kernels, hash_rows(): pl.pallas_call(functools.partial(hash_kernel, row, tile, start), out_shap...  45 us
    ppermute x12, starting transfers between devices, exchange(): return lax.ppermute(value, 'prow', [(i, i ^ mask) for i in range(GRID)])  13.5 us
    all_to_all x1, starting transfers between devices, body(): part = jnp.sum(lax.all_to_all(parts, 'pcol', 0, 0, tiled=True), axis=0)  11.1 us
    pallas_call x1, Pallas kernels, first_rows(): pl.pallas_call(first_kernel, out_shape=jax.ShapeDtypeStruct((GRID, 1, NB)...  10 us
    all_to_all x1, starting transfers between devices, body(): updated = jnp.sum(lax.all_to_all(sums, 'pcol', 0, 0, tiled=True), axis=0)  9.61 us
    ppermute x7, starting transfers between devices, body(): lax.ppermute(total, 'pcol', [(2 * k + h, 2 * k + 3 - h) for h in range(2)])  8.82 us
    all_to_all x1, starting transfers between devices, body(): came = lax.all_to_all(sent, 'prow', 0, 0, tiled=True)  6.55 us
    all_to_all x1, waiting for transfers between devices, body(): updated = jnp.sum(lax.all_to_all(sums, 'pcol', 0, 0, tiled=True), axis=0)  6.46 us
  transfers between devices with their start and end apart: 30, of which 3 were waited for; matrix products, arithmetic and copies ran while one was open for 1% of the time, Pallas kernels for 39%

profile of v4, /device:TPU:29, one launch (start us, length us, event | category | flops | bytes accessed | tf_op | source)
XLA Modules:
  0.0 141.2 jit_solution(15009400643442382225)
XLA Ops:
  0.7 0.6 copy-done.6
  1.4 0.7 copy-done.8
  2.8 1.0 multiply_bitcast_fusion
  4.0 1.0 pad_maximum_fusion
  5.0 6.6 %all-to-all-start = ((f32[16,18,512]{2,1,0:T(8,128)}), f32[16,18,512]{2,1,0:T(8,128)S(1)}, u32[]{:S(2)}, u32[]{:S(2)}) async-start(f32[16,18,512]{2,1,0:T(8,128)} %pad_maximum_fusion), calls=%async_computation | async-start | bytes 1572864 | tf_op jit(solution)/shard_map/all_to_all | solution.py:273
  11.8 0.6 copy-done.3
  12.6 10.0 %first_rows.1._ = f32[16,1,512]{2,1,0:T(1,128)} custom-call(s32[64]{0:T(128)S(1)} %copy-done.6, s32[64,25]{1,0:T(8,128)S(1)} %copy.14.seeds, f32[7,128]{1,0:T(8,128)S(1)} %dynamic-slice_bitcast_fusion.window, f32[1,512]{1,0:T(1,128)S(1)} %bitcast.33, f32[1,512]{1,0:T(1,128)S(1)} %bitcast.32), custom_call_target="tpu_custom_call" | custom-call | flops 6553600 | bytes 32768 | tf_op jit(solution)/shard_map/first_rows/pallas_call | solution.py:89
  23.3 2.4 %collective-permute-start.4 = (f32[3,16,512]{2,1,0:T(8,128)S(1)}, f32[3,16,512]{2,1,0:T(8,128)S(1)}, u32[]{:S(2)}, u32[]{:S(2)}) collective-permute-start(f32[3,16,512]{2,1,0:T(8,128)S(1)} %slice.49), channel_id=1, source_target_pairs={{0,128},{16,144},{32,160},{48,176},{64,192},{80,208},{96,224},{112... | collective-permute-start | bytes 294920 | tf_op jit(solution)/shard_map/ppermute | solution.py:257
  25.7 0.6 collective-permute-start.3
  26.6 2.1 %collective-permute-start.1 = (f32[4,16,512]{2,1,0:T(8,128)S(1)}, f32[4,16,512]{2,1,0:T(8,128)S(1)}, u32[]{:S(2)}, u32[]{:S(2)}) collective-permute-start(f32[4,16,512]{2,1,0:T(8,128)S(1)} %slice.48), channel_id=1, source_target_pairs={{0,32},{16,48},{32,0},{48,16},{64,96},{80,112},{96,64},{112,80},{1... | collective-permute-start | bytes 393224 | tf_op jit(solution)/shard_map/ppermute | solution.py:257
  28.7 11.1 %all-to-all-start.1 = ((f32[16,1,512]{2,1,0:T(1,128)}), f32[16,1,512]{2,1,0:T(1,128)S(1)}, u32[]{:S(2)}, u32[]{:S(2)}) async-start(f32[16,1,512]{2,1,0:T(1,128)} %first_rows.1._), calls=%async_computation.1 | async-start | bytes 65536 | tf_op jit(solution)/shard_map/all_to_all | solution.py:297
  39.8 1.0 collective-permute-start
  40.8 6.4 %hash_0.1.table = f32[8,256]{1,0:T(8,128)S(1)} custom-call(s32[4,25]{1,0:T(4,128)S(1)} %pad_add_fusion.seeds, s32[1]{0:T(128)} %bitcast.16.meta, f32[25,4,128]{2,1,0:T(4,128)S(1)} %reshape.39.v, f32[8,256]{1,0:T(8,128)S(1)} %broadcast_in_dim.27.table, f32[16,1,512]{2,1,0:T(1,128)} %first_rows.1._), custom_call_target="tpu_custom_call" | custom-call | flops 6553600 | bytes 131072 | tf_op jit(solution)/shard_map/hash_0/pallas_call | solution.py:125
  47.4 0.9 collective-permute-start.9
  48.6 2.4 %collective-permute-start.7 = (f32[4,4,16,512]{3,2,1,0:T(8,128)S(1)}, f32[4,4,16,512]{3,2,1,0:T(8,128)S(1)}, u32[]{:S(2)}, u32[]{:S(2)}) collective-permute-start(f32[4,4,16,512]{3,2,1,0:T(8,128)S(1)} %pad_maximum_fusion.1.refs_2_.refs_4_), channel_id=1, source_target_pairs={{0,128},{16,144},{32,160},{48,176},{64,192},{80,208},{96,224},{112... | collective-permute-start | bytes 1572872 | tf_op jit(solution)/shard_map/ppermute | solution.py:257
  51.0 0.6 collective-permute-start.6
  51.6 1.5 %collective-permute-start.10 = (f32[4,3,16,512]{3,2,1,0:T(8,128)S(1)}, f32[4,3,16,512]{3,2,1,0:T(8,128)S(1)}, u32[]{:S(2)}, u32[]{:S(2)}) collective-permute-start(f32[4,3,16,512]{3,2,1,0:T(8,128)S(1)} %pad_maximum_fusion.2.refs_6_.refs_8_.refs_4_), channel_id=1, source_target_pairs={{0,32},{16,48},{32,0},{48,16},{64,96},{80,112},{96,64},{112,80},{1... | collective-permute-start | bytes 1179656 | tf_op jit(solution)/shard_map/ppermute | solution.py:257
  53.1 4.7 %collective-permute-done.9.refs_7_.refs_9_.refs_5_ = f32[4,3,16,512]{3,2,1,0:T(8,128)S(1)} collective-permute-done((f32[4,3,16,512]{3,2,1,0:T(8,128)S(1)}, f32[4,3,16,512]{3,2,1,0:T(8,128)S(1)}, u32[]{:S(2)}, u32[]{:S(2)}) %collective-permute-start.9) | collective-permute-done | bytes 393248 | tf_op jit(solution)/shard_map/ppermute | solution.py:257
  57.9 1.2 collective-permute-start.11
  59.0 0.7 broadcast_in_dim.28
  59.7 6.4 %all-to-all-start.2 = ((f32[16,2,512]{2,1,0:T(2,128)}), f32[16,2,512]{2,1,0:T(2,128)S(1)}, u32[]{:S(2)}, u32[]{:S(2)}) async-start(f32[16,2,512]{2,1,0:T(2,128)} %broadcast_in_dim.28), calls=%async_computation.2 | async-start | bytes 131072 | tf_op jit(solution)/shard_map/all_to_all | solution.py:253
  66.1 6.4 %hash_1.1.table = f32[8,256]{1,0:T(8,128)S(1)} custom-call(s32[4,25]{1,0:T(4,128)S(1)} %pad_add_fusion.seeds, s32[1]{0:T(128)} %bitcast.16.meta, f32[25,4,128]{2,1,0:T(4,128)S(1)} %reshape.39.v, f32[8,256]{1,0:T(8,128)S(1)} %hash_0.1.table, f32[1,512]{1,0:T(1,128)S(1)} %bitcast.29), custom_call_target="tpu_custom_call" | custom-call | flops 6553600 | bytes 131072 | tf_op jit(solution)/shard_map/hash_1/pallas_call | solution.py:125
  72.5 6.4 %hash_2.1.refs_1_ = f32[8,256]{1,0:T(8,128)S(1)} custom-call(s32[4,25]{1,0:T(4,128)S(1)} %pad_add_fusion.seeds, s32[1]{0:T(128)} %bitcast.16.meta, f32[25,4,128]{2,1,0:T(4,128)S(1)} %reshape.39.v, f32[8,256]{1,0:T(8,128)S(1)} %hash_1.1.table, f32[1,512]{1,0:T(1,128)S(1)} %bitcast.30), custom_call_target="tpu_custom_call" | custom-call | flops 6553600 | bytes 131072 | tf_op jit(solution)/shard_map/hash_2/pallas_call | solution.py:125
  79.0 1.6 %step_0.1 = (f32[8,512]{1,0:T(8,128)S(1)}, f32[8,256]{1,0:T(8,128)S(1)}) custom-call(f32[16,2,512]{2,1,0:T(2,128)S(1)} %all-to-all-done.2.came, bf16[256,512]{1,0:T(8,128)(2,1)S(1)} %copy-done.1, f32[8,256]{1,0:T(8,128)S(1)} %hash_2.1.refs_1_, f32[4,4,16,512]{3,2,1,0:T(8,128)S(1)} %pad_maximum_fusion.1.refs_2_.refs_4_, ...), custom_call_target="tpu_custom_call" | custom-call | tf_op jit(solution)/shard_map/step_0/pallas_call | solution.py:202
  80.6 4.7 %collective-permute-start.13 = (f32[8,512]{1,0:T(8,128)S(1)}, f32[8,512]{1,0:T(8,128)S(1)}, u32[]{:S(2)}, u32[]{:S(2)}) collective-permute-start(f32[8,512]{1,0:T(8,128)S(1)} %get-tuple-element.36), channel_id=1, source_target_pairs={{0,3},{1,2},{16,19},{17,18},{32,35},{33,34},{48,51},{49,50},{64,67... | collective-permute-start | bytes 49160 | tf_op jit(solution)/shard_map/ppermute | solution.py:313
  85.4 1.3 collective-permute-start.12
  86.7 0.8 collective-permute-done.12.refs_0_
  87.5 0.7 collective-permute-start.15
  88.2 0.7 collective-permute-start.14
  88.9 6.4 %hash_3.1.refs_3_ = f32[8,256]{1,0:T(8,128)S(1)} custom-call(s32[4,25]{1,0:T(4,128)S(1)} %pad_add_fusion.seeds, s32[1]{0:T(128)} %bitcast.16.meta, f32[25,4,128]{2,1,0:T(4,128)S(1)} %reshape.39.v, f32[8,256]{1,0:T(8,128)S(1)} %get-tuple-element.39.table, f32[8,512]{1,0:T(8,128)S(1)} %get-tuple-element.38._), custom_call_target="tpu_custom_call" | custom-call | flops 6553600 | bytes 131072 | tf_op jit(solution)/shard_map/hash_3/pallas_call | solution.py:125
  95.4 0.7 collective-permute-start.17
  96.0 0.7 collective-permute-start.16
  96.7 6.4 %hash_4.1.refs_3_ = f32[8,256]{1,0:T(8,128)S(1)} custom-call(s32[4,25]{1,0:T(4,128)S(1)} %pad_add_fusion.seeds, s32[1]{0:T(128)} %bitcast.16.meta, f32[25,4,128]{2,1,0:T(4,128)S(1)} %reshape.39.v, f32[8,256]{1,0:T(8,128)S(1)} %get-tuple-element.41.table, f32[8,512]{1,0:T(8,128)S(1)} %get-tuple-element.40._), custom_call_target="tpu_custom_call" | custom-call | flops 6553600 | bytes 131072 | tf_op jit(solution)/shard_map/hash_4/pallas_call | solution.py:125
  103.2 0.7 collective-permute-start.19
  103.9 0.7 collective-permute-start.18
  104.6 6.4 %hash_5.1.refs_3_ = f32[8,256]{1,0:T(8,128)S(1)} custom-call(s32[4,25]{1,0:T(4,128)S(1)} %pad_add_fusion.seeds, s32[1]{0:T(128)} %bitcast.16.meta, f32[25,4,128]{2,1,0:T(4,128)S(1)} %reshape.39.v, f32[8,256]{1,0:T(8,128)S(1)} %get-tuple-element.43.table, f32[8,512]{1,0:T(8,128)S(1)} %get-tuple-element.42._), custom_call_target="tpu_custom_call" | custom-call | flops 6553600 | bytes 131072 | tf_op jit(solution)/shard_map/hash_5/pallas_call | solution.py:125
  111.1 0.7 collective-permute-start.21
  111.7 0.7 collective-permute-start.20
  112.5 0.7 collective-permute-start.23
  113.1 0.7 collective-permute-start.22
  113.8 6.4 %hash_6.1.refs_3_ = f32[8,256]{1,0:T(8,128)S(1)} custom-call(s32[4,25]{1,0:T(4,128)S(1)} %pad_add_fusion.seeds, s32[1]{0:T(128)} %bitcast.16.meta, f32[25,4,128]{2,1,0:T(4,128)S(1)} %reshape.39.v, f32[8,256]{1,0:T(8,128)S(1)} %get-tuple-element.47.table, f32[8,512]{1,0:T(8,128)S(1)} %get-tuple-element.46._), custom_call_target="tpu_custom_call" | custom-call | flops 6553600 | bytes 131072 | tf_op jit(solution)/shard_map/hash_6/pallas_call | solution.py:125
  120.3 0.8 collective-permute-start.25
  121.1 0.7 collective-permute-start.24
  121.9 0.6 copy-done.5
  122.5 1.5 %last.1 = f32[16,128]{1,0:T(8,128)} custom-call(f32[4]{0:T(128)S(1)} %copy-done.5, s32[64]{0:T(128)S(1)} %copy-done.7, f32[16,128]{1,0:T(8,128)S(1)} %bitcast.31, f32[25,4,128]{2,1,0:T(4,128)S(1)} %reshape.39.v, f32[16,2,512]{2,1,0:T(2,128)S(1)} %all-to-all-done.2.came, bf16[2048,256]{1,0:T(8,128)(2,1)S(1)} %copy-done.2, f32[8,256]{1,0:T(8,128)S(1)} %step_7.1.table), custom_call_target="tpu_custom_call" | custom-call | tf_op jit(solution)/shard_map/last/pallas_call | solution.py:242
  124.0 9.6 %all-to-all-start.3 = ((f32[16,1,128]{2,1,0:T(1,128)}), f32[16,1,128]{2,1,0:T(1,128)S(1)}, u32[]{:S(2)}, u32[]{:S(2)}) async-start(f32[16,1,128]{2,1,0:T(1,128)} %bitcast.20), calls=%async_computation.3 | async-start | bytes 16384 | tf_op jit(solution)/shard_map/all_to_all | solution.py:321
  133.6 0.6 slice.52
  134.2 6.5 %all-to-all-done.3 = f32[16,1,128]{2,1,0:T(1,128)S(1)} async-done(((f32[16,1,128]{2,1,0:T(1,128)}), f32[16,1,128]{2,1,0:T(1,128)S(1)}, u32[]{:S(2)}, u32[]{:S(2)}) %all-to-all-start.3) | async-done | bytes 8224 | tf_op jit(solution)/shard_map/all_to_all | solution.py:321
  (82 shorter events, 3.4 us)
Async XLA Ops:
  0.6 1.4 %copy-start = (f32[4,8]{1,0:T(4,128)S(1)}, f32[4,8]{1,0:T(4,128)}, u32[]{:S(2)}) copy-start(f32[4,8]{1,0:T(4,128)} %param.12) | copy-start | bytes 388
  0.7 0.7 copy-start.6
  1.4 0.7 copy-start.8
  2.3 0.5 copy-start.4
  5.0 17.6 %all-to-all-start = ((f32[16,18,512]{2,1,0:T(8,128)}), f32[16,18,512]{2,1,0:T(8,128)S(1)}, u32[]{:S(2)}, u32[]{:S(2)}) async-start(f32[16,18,512]{2,1,0:T(8,128)} %pad_maximum_fusion), calls=%async_computation | async-start | bytes 1572864 | tf_op jit(solution)/shard_map/all_to_all | solution.py:273
  11.7 0.7 copy-start.9
  11.7 0.7 copy-start.3
  22.9 16.8 %collective-permute-start.5 = (f32[3,16,512]{2,1,0:T(8,128)S(1)}, f32[3,16,512]{2,1,0:T(8,128)S(1)}, u32[]{:S(2)}, u32[]{:S(2)}) collective-permute-start(f32[3,16,512]{2,1,0:T(8,128)S(1)} %slice.49), channel_id=1, source_target_pairs={{0,192},{16,208},{32,224},{48,240},{64,128},{80,144},{96,160},{112... | collective-permute-start | bytes 294920 | tf_op jit(solution)/shard_map/ppermute | solution.py:257
  23.3 24.0 %collective-permute-start.4 = (f32[3,16,512]{2,1,0:T(8,128)S(1)}, f32[3,16,512]{2,1,0:T(8,128)S(1)}, u32[]{:S(2)}, u32[]{:S(2)}) collective-permute-start(f32[3,16,512]{2,1,0:T(8,128)S(1)} %slice.49), channel_id=1, source_target_pairs={{0,128},{16,144},{32,160},{48,176},{64,192},{80,208},{96,224},{112... | collective-permute-start | bytes 294920 | tf_op jit(solution)/shard_map/ppermute | solution.py:257
  25.7 21.6 %collective-permute-start.3 = (f32[3,16,512]{2,1,0:T(8,128)S(1)}, f32[3,16,512]{2,1,0:T(8,128)S(1)}, u32[]{:S(2)}, u32[]{:S(2)}) collective-permute-start(f32[3,16,512]{2,1,0:T(8,128)S(1)} %slice.49), channel_id=1, source_target_pairs={{0,64},{16,80},{32,96},{48,112},{64,0},{80,16},{96,32},{112,48},{1... | collective-permute-start | bytes 294920 | tf_op jit(solution)/shard_map/ppermute | solution.py:257
  26.3 21.1 %collective-permute-start.2 = (f32[4,16,512]{2,1,0:T(8,128)S(1)}, f32[4,16,512]{2,1,0:T(8,128)S(1)}, u32[]{:S(2)}, u32[]{:S(2)}) collective-permute-start(f32[4,16,512]{2,1,0:T(8,128)S(1)} %slice.48), channel_id=1, source_target_pairs={{0,48},{16,32},{32,16},{48,0},{64,112},{80,96},{96,80},{112,64},{1... | collective-permute-start | bytes 393224 | tf_op jit(solution)/shard_map/ppermute | solution.py:257
  26.6 20.8 %collective-permute-start.1 = (f32[4,16,512]{2,1,0:T(8,128)S(1)}, f32[4,16,512]{2,1,0:T(8,128)S(1)}, u32[]{:S(2)}, u32[]{:S(2)}) collective-permute-start(f32[4,16,512]{2,1,0:T(8,128)S(1)} %slice.48), channel_id=1, source_target_pairs={{0,32},{16,48},{32,0},{48,16},{64,96},{80,112},{96,64},{112,80},{1... | collective-permute-start | bytes 393224 | tf_op jit(solution)/shard_map/ppermute | solution.py:257
  28.7 18.6 %all-to-all-start.1 = ((f32[16,1,512]{2,1,0:T(1,128)}), f32[16,1,512]{2,1,0:T(1,128)S(1)}, u32[]{:S(2)}, u32[]{:S(2)}) async-start(f32[16,1,512]{2,1,0:T(1,128)} %first_rows.1._), calls=%async_computation.1 | async-start | bytes 65536 | tf_op jit(solution)/shard_map/all_to_all | solution.py:297
  39.8 7.6 %collective-permute-start = (f32[4,16,512]{2,1,0:T(8,128)S(1)}, f32[4,16,512]{2,1,0:T(8,128)S(1)}, u32[]{:S(2)}, u32[]{:S(2)}) collective-permute-start(f32[4,16,512]{2,1,0:T(8,128)S(1)} %slice.48), channel_id=1, source_target_pairs={{0,16},{16,0},{32,48},{48,32},{64,80},{80,64},{96,112},{112,96},{1... | collective-permute-start | bytes 393224 | tf_op jit(solution)/shard_map/ppermute | solution.py:257
  47.4 31.6 %copy-start.1 = (bf16[256,512]{1,0:T(8,128)(2,1)S(1)}, bf16[256,512]{1,0:T(8,128)(2,1)}, u32[]{:S(2)}) copy-start(bf16[256,512]{1,0:T(8,128)(2,1)} %refs_2_.13) | copy-start | bytes 786436
  47.4 10.4 %collective-permute-start.9 = (f32[4,3,16,512]{3,2,1,0:T(8,128)S(1)}, f32[4,3,16,512]{3,2,1,0:T(8,128)S(1)}, u32[]{:S(2)}, u32[]{:S(2)}) collective-permute-start(f32[4,3,16,512]{3,2,1,0:T(8,128)S(1)} %pad_maximum_fusion.2.refs_6_.refs_8_.refs_4_), channel_id=1, source_target_pairs={{0,16},{16,0},{32,48},{48,32},{64,80},{80,64},{96,112},{112,96},{1... | collective-permute-start | bytes 1179656 | tf_op jit(solution)/shard_map/ppermute | solution.py:257
  48.3 30.6 %collective-permute-start.8 = (f32[4,4,16,512]{3,2,1,0:T(8,128)S(1)}, f32[4,4,16,512]{3,2,1,0:T(8,128)S(1)}, u32[]{:S(2)}, u32[]{:S(2)}) collective-permute-start(f32[4,4,16,512]{3,2,1,0:T(8,128)S(1)} %pad_maximum_fusion.1.refs_2_.refs_4_), channel_id=1, source_target_pairs={{0,192},{16,208},{32,224},{48,240},{64,128},{80,144},{96,160},{112... | collective-permute-start | bytes 1572872 | tf_op jit(solution)/shard_map/ppermute | solution.py:257
  48.6 30.4 %collective-permute-start.7 = (f32[4,4,16,512]{3,2,1,0:T(8,128)S(1)}, f32[4,4,16,512]{3,2,1,0:T(8,128)S(1)}, u32[]{:S(2)}, u32[]{:S(2)}) collective-permute-start(f32[4,4,16,512]{3,2,1,0:T(8,128)S(1)} %pad_maximum_fusion.1.refs_2_.refs_4_), channel_id=1, source_target_pairs={{0,128},{16,144},{32,160},{48,176},{64,192},{80,208},{96,224},{112... | collective-permute-start | bytes 1572872 | tf_op jit(solution)/shard_map/ppermute | solution.py:257
  51.0 28.0 %collective-permute-start.6 = (f32[4,4,16,512]{3,2,1,0:T(8,128)S(1)}, f32[4,4,16,512]{3,2,1,0:T(8,128)}, u32[]{:S(2)}, u32[]{:S(2)}) collective-permute-start(f32[4,4,16,512]{3,2,1,0:T(8,128)S(1)} %pad_maximum_fusion.1.refs_2_.refs_4_), channel_id=1, source_target_pairs={{0,64},{16,80},{32,96},{48,112},{64,0},{80,16},{96,32},{112,48},{1... | collective-permute-start | bytes 1572872 | tf_op jit(solution)/shard_map/ppermute | solution.py:257
  51.6 27.4 %collective-permute-start.10 = (f32[4,3,16,512]{3,2,1,0:T(8,128)S(1)}, f32[4,3,16,512]{3,2,1,0:T(8,128)S(1)}, u32[]{:S(2)}, u32[]{:S(2)}) collective-permute-start(f32[4,3,16,512]{3,2,1,0:T(8,128)S(1)} %pad_maximum_fusion.2.refs_6_.refs_8_.refs_4_), channel_id=1, source_target_pairs={{0,32},{16,48},{32,0},{48,16},{64,96},{80,112},{96,64},{112,80},{1... | collective-permute-start | bytes 1179656 | tf_op jit(solution)/shard_map/ppermute | solution.py:257
  57.9 21.1 %collective-permute-start.11 = (f32[4,3,16,512]{3,2,1,0:T(8,128)S(1)}, f32[4,3,16,512]{3,2,1,0:T(8,128)S(1)}, u32[]{:S(2)}, u32[]{:S(2)}) collective-permute-start(f32[4,3,16,512]{3,2,1,0:T(8,128)S(1)} %pad_maximum_fusion.2.refs_6_.refs_8_.refs_4_), channel_id=1, source_target_pairs={{0,48},{16,32},{32,16},{48,0},{64,112},{80,96},{96,80},{112,64},{1... | collective-permute-start | bytes 1179656 | tf_op jit(solution)/shard_map/ppermute | solution.py:257
  59.7 19.3 %all-to-all-start.2 = ((f32[16,2,512]{2,1,0:T(2,128)}), f32[16,2,512]{2,1,0:T(2,128)S(1)}, u32[]{:S(2)}, u32[]{:S(2)}) async-start(f32[16,2,512]{2,1,0:T(2,128)} %broadcast_in_dim.28), calls=%async_computation.2 | async-start | bytes 131072 | tf_op jit(solution)/shard_map/all_to_all | solution.py:253
  80.6 6.0 %collective-permute-start.13 = (f32[8,512]{1,0:T(8,128)S(1)}, f32[8,512]{1,0:T(8,128)S(1)}, u32[]{:S(2)}, u32[]{:S(2)}) collective-permute-start(f32[8,512]{1,0:T(8,128)S(1)} %get-tuple-element.36), channel_id=1, source_target_pairs={{0,3},{1,2},{16,19},{17,18},{32,35},{33,34},{48,51},{49,50},{64,67... | collective-permute-start | bytes 49160 | tf_op jit(solution)/shard_map/ppermute | solution.py:313
  85.4 2.1 %collective-permute-start.12 = (f32[8,512]{1,0:T(8,128)S(1)}, f32[8,512]{1,0:T(8,128)S(1)}, u32[]{:S(2)}, u32[]{:S(2)}) collective-permute-start(f32[8,512]{1,0:T(8,128)S(1)} %get-tuple-element.36), channel_id=1, source_target_pairs={{0,2},{1,3},{16,18},{17,19},{32,34},{33,35},{48,50},{49,51},{64,66... | collective-permute-start | bytes 49160 | tf_op jit(solution)/shard_map/ppermute | solution.py:312
  87.5 7.8 %collective-permute-start.15 = (f32[8,512]{1,0:T(8,128)S(1)}, f32[8,512]{1,0:T(8,128)S(1)}, u32[]{:S(2)}, u32[]{:S(2)}) collective-permute-start(f32[8,512]{1,0:T(8,128)S(1)} %get-tuple-element.38._), channel_id=1, source_target_pairs={{2,5},{3,4},{18,21},{19,20},{34,37},{35,36},{50,53},{51,52},{66,69... | collective-permute-start | bytes 49160 | tf_op jit(solution)/shard_map/ppermute | solution.py:313
  88.2 7.1 %collective-permute-start.14 = (f32[8,512]{1,0:T(8,128)S(1)}, f32[8,512]{1,0:T(8,128)S(1)}, u32[]{:S(2)}, u32[]{:S(2)}) collective-permute-start(f32[8,512]{1,0:T(8,128)S(1)} %get-tuple-element.38._), channel_id=1, source_target_pairs={{2,4},{3,5},{18,20},{19,21},{34,36},{35,37},{50,52},{51,53},{66,68... | collective-permute-start | bytes 49160 | tf_op jit(solution)/shard_map/ppermute | solution.py:312
  95.4 7.8 %collective-permute-start.17 = (f32[8,512]{1,0:T(8,128)S(1)}, f32[8,512]{1,0:T(8,128)S(1)}, u32[]{:S(2)}, u32[]{:S(2)}) collective-permute-start(f32[8,512]{1,0:T(8,128)S(1)} %get-tuple-element.40._), channel_id=1, source_target_pairs={{4,7},{5,6},{20,23},{21,22},{36,39},{37,38},{52,55},{53,54},{68,71... | collective-permute-start | bytes 49160 | tf_op jit(solution)/shard_map/ppermute | solution.py:313
  96.0 7.1 %collective-permute-start.16 = (f32[8,512]{1,0:T(8,128)S(1)}, f32[8,512]{1,0:T(8,128)S(1)}, u32[]{:S(2)}, u32[]{:S(2)}) collective-permute-start(f32[8,512]{1,0:T(8,128)S(1)} %get-tuple-element.40._), channel_id=1, source_target_pairs={{4,6},{5,7},{20,22},{21,23},{36,38},{37,39},{52,54},{53,55},{68,70... | collective-permute-start | bytes 49160 | tf_op jit(solution)/shard_map/ppermute | solution.py:312
  103.2 7.8 %collective-permute-start.19 = (f32[8,512]{1,0:T(8,128)S(1)}, f32[8,512]{1,0:T(8,128)S(1)}, u32[]{:S(2)}, u32[]{:S(2)}) collective-permute-start(f32[8,512]{1,0:T(8,128)S(1)} %get-tuple-element.42._), channel_id=1, source_target_pairs={{6,9},{7,8},{22,25},{23,24},{38,41},{39,40},{54,57},{55,56},{70,73... | collective-permute-start | bytes 49160 | tf_op jit(solution)/shard_map/ppermute | solution.py:313
  103.9 7.1 %collective-permute-start.18 = (f32[8,512]{1,0:T(8,128)S(1)}, f32[8,512]{1,0:T(8,128)S(1)}, u32[]{:S(2)}, u32[]{:S(2)}) collective-permute-start(f32[8,512]{1,0:T(8,128)S(1)} %get-tuple-element.42._), channel_id=1, source_target_pairs={{6,8},{7,9},{22,24},{23,25},{38,40},{39,41},{54,56},{55,57},{70,72... | collective-permute-start | bytes 49160 | tf_op jit(solution)/shard_map/ppermute | solution.py:312
  111.1 1.3 collective-permute-start.21
  111.7 0.7 collective-permute-start.20
  112.5 7.8 %collective-permute-start.23 = (f32[8,512]{1,0:T(8,128)S(1)}, f32[8,512]{1,0:T(8,128)S(1)}, u32[]{:S(2)}, u32[]{:S(2)}) collective-permute-start(f32[8,512]{1,0:T(8,128)S(1)} %get-tuple-element.46._), channel_id=1, source_target_pairs={{10,13},{11,12},{26,29},{27,28},{42,45},{43,44},{58,61},{59,60},{7... | collective-permute-start | bytes 49160 | tf_op jit(solution)/shard_map/ppermute | solution.py:313
  113.1 7.1 %collective-permute-start.22 = (f32[8,512]{1,0:T(8,128)S(1)}, f32[8,512]{1,0:T(8,128)S(1)}, u32[]{:S(2)}, u32[]{:S(2)}) collective-permute-start(f32[8,512]{1,0:T(8,128)S(1)} %get-tuple-element.46._), channel_id=1, source_target_pairs={{10,12},{11,13},{26,28},{27,29},{42,44},{43,45},{58,60},{59,61},{7... | collective-permute-start | bytes 49160 | tf_op jit(solution)/shard_map/ppermute | solution.py:312
  120.2 1.6 %copy-start.2 = (bf16[2048,256]{1,0:T(8,128)(2,1)S(1)}, bf16[2048,256]{1,0:T(8,128)(2,1)}, u32[]{:S(2)}) copy-start(bf16[2048,256]{1,0:T(8,128)(2,1)} %panel.1) | copy-start | bytes 3145732
  120.3 1.5 %collective-permute-start.25 = (f32[8,512]{1,0:T(8,128)S(1)}, f32[8,512]{1,0:T(8,128)S(1)}, u32[]{:S(2)}, u32[]{:S(2)}) collective-permute-start(f32[8,512]{1,0:T(8,128)S(1)} %get-tuple-element.48), channel_id=1, source_target_pairs={{12,15},{13,14},{28,31},{29,30},{44,47},{45,46},{60,63},{61,62},{7... | collective-permute-start | bytes 49160 | tf_op jit(solution)/shard_map/ppermute | solution.py:313
  121.1 0.7 collective-permute-start.24
  121.9 0.7 copy-start.5
  121.9 0.7 copy-start.7
  124.0 16.6 %all-to-all-start.3 = ((f32[16,1,128]{2,1,0:T(1,128)}), f32[16,1,128]{2,1,0:T(1,128)S(1)}, u32[]{:S(2)}, u32[]{:S(2)}) async-start(f32[16,1,128]{2,1,0:T(1,128)} %bitcast.20), calls=%async_computation.3 | async-start | bytes 16384 | tf_op jit(solution)/shard_map/all_to_all | solution.py:321

commit v5 on v4

--- a/solution.py
+++ b/solution.py
@@ -98,6 +98,32 @@
     )(tile_owner, seeds, window, rhs, vector)
 
 
+def spread_kernel(owner, scales, vector, panel, out, held, sem):
+    fetch = pltpu.make_async_copy(panel.at[pl.ds(0, NB)], held, sem)
+    fetch.start()
+    block = lax.axis_index("pcol") >> 1
+    my_tile = (lax.axis_index("prow") - owner[0] + GRID) & (GRID - 1)
+    factor = jnp.where(my_tile > block, scales[0, block], jnp.float32(0.0))
+    length = vector.shape[1]
+    out[:, 16:17, :] = jnp.broadcast_to(vector[:, :NB][None], (GRID, 1, NB))
+    out[:, 17:18, :] = jnp.zeros((GRID, 1, NB), jnp.float32)
+    out[:, 17:18, :length - NB] = jnp.broadcast_to(vector[:, NB:][None], (GRID, 1, length - NB))
+    fetch.wait()
+    out[:, :16, :] = (held[...].astype(jnp.float32) * factor).T.reshape(GRID, 16, NB)
+
+
+def spread_parts(tile_owner, tile_scales, vector, panel):
+    return pl.pallas_call(
+        spread_kernel,
+        out_shape=jax.ShapeDtypeStruct((GRID, 18, NB), jnp.float32),
+        in_specs=[SMEM, SMEM, VMEM, ANY],
+        out_specs=VMEM,
+        scratch_shapes=[pltpu.VMEM((NB, 256), jnp.bfloat16), pltpu.SemaphoreType.DMA],
+        compiler_params=LIMIT,
+        name="spread_parts",
+    )(tile_owner, tile_scales, vector, panel)
+
+
 def hash_kernel(row, tile, start, seeds, meta, v, table, _, out, held):
     bias = jnp.sum(jnp.sum(v[...], axis=0), axis=0, keepdims=True) * jnp.float32(BIAS)
     begin = meta[0] if start is None else start
@@ -117,7 +143,7 @@
 
     lax.fori_loop(0, PIECE // STRIP, strip, 0)
     out[...] = table[...]
-    out[row:row + 1, :] = jnp.sum(held[...].T, axis=0, keepdims=True) * jnp.float32(UNIT)
+    out[row + 1:row + 2, :] = jnp.sum(held[...].T, axis=0, keepdims=True) * jnp.float32(UNIT)
 
 
 def hash_rows(seeds, meta, v, table, token, row):
@@ -180,7 +206,7 @@
                 update = update + jnp.where(col % 2 == 0, running, 0.0)
             total_out[...] = update
         eye = lax.broadcasted_iota(jnp.int32, (256, 256), 0) == lax.broadcasted_iota(jnp.int32, (256, 256), 1)
-        table_out[KB - 1:KB, :] = jnp.sum(jnp.where(eye, y, 0.0), axis=0, keepdims=True)
+        table_out[0:1, :] = jnp.sum(jnp.where(eye, y, 0.0), axis=0, keepdims=True)
 
     if k < KB - 1:
         @pl.when(jnp.logical_not(mine))
@@ -217,7 +243,7 @@
 def last_kernel(factor, owner, rhs, v, came, panel, table, out):
     row_index, col_index = lax.axis_index("prow"), lax.axis_index("pcol")
     my_tile = (row_index - owner[0] + GRID) & (GRID - 1)
-    y = table[KB - 1:KB, :]
+    y = table[0:1, :]
     residual = jnp.sum(came[:, :1, :], axis=0)
     theirs = came[(row_index + KB) & (GRID - 1), 1:, :]
     for at in range(0, ROWS, LANES):
@@ -228,13 +254,13 @@
         given = jnp.where(col_index == 0, rhs[n:n + 1, :], 0.0)
         given = given - jnp.where(my_tile == col_index, v[n // GROUPS, n % GROUPS:n % GROUPS + 1, :], 0.0)
         if at < NB:
-            shared = table[0:1, at:at + LANES] if at < PIECE else theirs[:, at - PIECE:at - PIECE + LANES]
+            shared = table[1:2, at:at + LANES] if at < PIECE else theirs[:, at - PIECE:at - PIECE + LANES]
             given = given - shared
             known = jnp.where(col_index == 2 * my_tile, residual[:, at:at + LANES], 0.0)
             given = jnp.where(my_tile < KB, known, given)
         else:
             piece, row = divmod(at - NB, PIECE)
-            given = given - table[piece + 1:piece + 2, row:row + LANES]
+            given = given - table[piece + 2:piece + 3, row:row + LANES]
         out[n:n + 1, :] = given - total
 
 
@@ -267,9 +293,7 @@
     scales = lax.dynamic_slice_in_dim(tile_scales, block, 1, 1)[:, 0]
     factor = jnp.where(my_tiles > block, scales, jnp.float32(0.0))
 
-    scaled = (panel[:NB].astype(jnp.float32) * factor[0]).T.reshape(GRID, 16, NB)
-    padded = jnp.pad(vector, (0, 2 * NB - vector.shape[0])).reshape(1, 2, NB)
-    sent = jnp.concatenate([scaled, jnp.broadcast_to(padded, (GRID, 2, NB))], axis=1)
+    sent = spread_parts(tile_owner, tile_scales, vector.reshape(1, -1), panel)
     came = lax.all_to_all(sent, "prow", 0, 0, tiled=True)
 
     edge = jnp.zeros((96,), jnp.float32)
@@ -300,7 +324,7 @@
     across = [exchange(near, m) for m in (4, 8, 12)]
     far, first = lax.optimization_barrier((far, first))
     tiles = [near] + across + [far, first, second, exchange(far, 3)]
-    came = to_all(jnp.concatenate([part, jnp.pad(table[:1], ((0, 0), (0, PIECE)))]), "prow")
+    came = to_all(jnp.concatenate([part, jnp.pad(table[1:2], ((0, 0), (0, PIECE)))]), "prow")
     row = 1
     for _ in range(AHEAD):
         table = hash_rows(seed_rows, meta, v, table, part, row)
@@ -319,7 +343,7 @@
 
     sums = last(factor, tile_owner, rhs.reshape(GRID, LANES), v, came, panel, table)
     updated = jnp.sum(lax.all_to_all(sums, "pcol", 0, 0, tiled=True), axis=0)
-    return (table[KB - 1], updated)
+    return (table[0], updated)
 
 
 def solution(mesh):

time: 143 us -> 142 us (level)
  other arithmetic: 2.84 us -> 0.82 us
  Pallas kernels: 58.4 us -> 60.2 us
    pallas_call x0 -> x1, Pallas kernels: none -> 1.71 us  [spread_parts(): pl.pallas_call(spread_kernel, out_shape=jax.ShapeDtypeStruct((GRID, 18, N...]
    unnamed x22 -> x20, local copies, waits for them, and re-layouts: 3.25 us -> 3.31 us
where the time goes in v5:
time: 142 us; the launch traced here: 141 us
  starting transfers between devices  60.3 us (42%)
  Pallas kernels  60.2 us (42%)
  waiting for transfers between devices  12.5 us (9%)
  local copies, waits for them, and re-layouts  5.64 us (4%)
  between operations  1.43 us (1%)
    pallas_call x7, Pallas kernels, hash_rows(): pl.pallas_call(functools.partial(hash_kernel, row, tile, start), out_shap...  45.1 us
    ppermute x12, starting transfers between devices, exchange(): return lax.ppermute(value, 'prow', [(i, i ^ mask) for i in range(GRID)])  12.8 us
    all_to_all x1, starting transfers between devices, body(): part = jnp.sum(lax.all_to_all(parts, 'pcol', 0, 0, tiled=True), axis=0)  11.1 us
    pallas_call x1, Pallas kernels, first_rows(): pl.pallas_call(first_kernel, out_shape=jax.ShapeDtypeStruct((GRID, 1, NB)...  10 us
    all_to_all x1, starting transfers between devices, body(): updated = jnp.sum(lax.all_to_all(sums, 'pcol', 0, 0, tiled=True), axis=0)  9.62 us
    ppermute x7, starting transfers between devices, body(): lax.ppermute(total, 'pcol', [(2 * k + h, 2 * k + 3 - h) for h in range(2)])  8.57 us
    all_to_all x1, starting transfers between devices, body(): came = lax.all_to_all(sent, 'prow', 0, 0, tiled=True)  6.56 us
    all_to_all x1, waiting for transfers between devices, body(): updated = jnp.sum(lax.all_to_all(sums, 'pcol', 0, 0, tiled=True), axis=0)  6.45 us
  transfers between devices with their start and end apart: 30, of which 3 were waited for; matrix products, arithmetic and copies ran while one was open for 1% of the time, Pallas kernels for 39%

profile of v5, /device:TPU:29, one launch (start us, length us, event | category | flops | bytes accessed | tf_op | source)
XLA Modules:
  0.0 140.8 jit_solution(15410608500555368566)
XLA Ops:
  0.7 0.7 reshape.32.vector
  1.4 1.2 copy-done.1
  2.6 1.7 %spread_parts.1 = f32[16,18,512]{2,1,0:T(8,128)} custom-call(s32[64]{0:T(128)S(1)} %copy-done.5, f32[4,8]{1,0:T(4,128)S(1)} %copy-done.4, f32[1,800]{1,0:T(1,128)S(1)} %reshape.32.vector, bf16[2048,256]{1,0:T(8,128)(2,1)S(1)} %copy-done.1), custom_call_target="tpu_custom_call" | custom-call | tf_op jit(solution)/shard_map/spread_parts/pallas_call | solution.py:116
  4.3 6.6 %all-to-all-start = ((f32[16,18,512]{2,1,0:T(8,128)}), f32[16,18,512]{2,1,0:T(8,128)S(1)}, u32[]{:S(2)}, u32[]{:S(2)}) async-start(f32[16,18,512]{2,1,0:T(8,128)} %spread_parts.1), calls=%async_computation | async-start | bytes 1572864 | tf_op jit(solution)/shard_map/all_to_all | solution.py:297
  10.9 0.7 copy-done.7
  11.8 0.6 copy-done.3
  12.6 10.0 %first_rows.1._ = f32[16,1,512]{2,1,0:T(1,128)} custom-call(s32[64]{0:T(128)S(1)} %copy-done.5, s32[64,25]{1,0:T(8,128)S(1)} %copy.12.seeds, f32[7,128]{1,0:T(8,128)S(1)} %dynamic-slice_bitcast_fusion.window, f32[1,512]{1,0:T(1,128)S(1)} %bitcast.28, f32[1,512]{1,0:T(1,128)S(1)} %bitcast.27), custom_call_target="tpu_custom_call" | custom-call | flops 6553600 | bytes 32768 | tf_op jit(solution)/shard_map/first_rows/pallas_call | solution.py:89
  23.3 2.4 %collective-permute-start.4 = (f32[3,16,512]{2,1,0:T(8,128)S(1)}, f32[3,16,512]{2,1,0:T(8,128)S(1)}, u32[]{:S(2)}, u32[]{:S(2)}) collective-permute-start(f32[3,16,512]{2,1,0:T(8,128)S(1)} %slice.41), channel_id=1, source_target_pairs={{0,128},{16,144},{32,160},{48,176},{64,192},{80,208},{96,224},{112... | collective-permute-start | bytes 294920 | tf_op jit(solution)/shard_map/ppermute | solution.py:283
  25.7 0.6 collective-permute-start.3
  26.6 2.1 %collective-permute-start.1 = (f32[4,16,512]{2,1,0:T(8,128)S(1)}, f32[4,16,512]{2,1,0:T(8,128)S(1)}, u32[]{:S(2)}, u32[]{:S(2)}) collective-permute-start(f32[4,16,512]{2,1,0:T(8,128)S(1)} %slice.40), channel_id=1, source_target_pairs={{0,32},{16,48},{32,0},{48,16},{64,96},{80,112},{96,64},{112,80},{1... | collective-permute-start | bytes 393224 | tf_op jit(solution)/shard_map/ppermute | solution.py:283
  28.7 11.1 %all-to-all-start.1 = ((f32[16,1,512]{2,1,0:T(1,128)}), f32[16,1,512]{2,1,0:T(1,128)S(1)}, u32[]{:S(2)}, u32[]{:S(2)}) async-start(f32[16,1,512]{2,1,0:T(1,128)} %first_rows.1._), calls=%async_computation.1 | async-start | bytes 65536 | tf_op jit(solution)/shard_map/all_to_all | solution.py:321
  39.8 1.0 collective-permute-start
  40.8 6.4 %hash_0.1.table = f32[8,256]{1,0:T(8,128)S(1)} custom-call(s32[4,25]{1,0:T(4,128)S(1)} %pad_add_fusion.seeds, s32[1]{0:T(128)} %bitcast.13.meta, f32[25,4,128]{2,1,0:T(4,128)S(1)} %reshape.37.v, f32[8,256]{1,0:T(8,128)S(1)} %broadcast_in_dim.17.table, f32[16,1,512]{2,1,0:T(1,128)} %first_rows.1._), custom_call_target="tpu_custom_call" | custom-call | flops 6553600 | bytes 131072 | tf_op jit(solution)/shard_map/hash_0/pallas_call | solution.py:151
  47.4 0.9 collective-permute-start.9
  48.6 2.4 %collective-permute-start.7 = (f32[4,4,16,512]{3,2,1,0:T(8,128)S(1)}, f32[4,4,16,512]{3,2,1,0:T(8,128)S(1)}, u32[]{:S(2)}, u32[]{:S(2)}) collective-permute-start(f32[4,4,16,512]{3,2,1,0:T(8,128)S(1)} %pad_maximum_fusion.refs_2_.refs_4_), channel_id=1, source_target_pairs={{0,128},{16,144},{32,160},{48,176},{64,192},{80,208},{96,224},{112... | collective-permute-start | bytes 1572872 | tf_op jit(solution)/shard_map/ppermute | solution.py:283
  51.0 0.6 collective-permute-start.6
  51.6 1.2 collective-permute-start.10
  52.8 5.1 %collective-permute-done.9.refs_7_.refs_9_.refs_5_ = f32[4,3,16,512]{3,2,1,0:T(8,128)S(1)} collective-permute-done((f32[4,3,16,512]{3,2,1,0:T(8,128)S(1)}, f32[4,3,16,512]{3,2,1,0:T(8,128)S(1)}, u32[]{:S(2)}, u32[]{:S(2)}) %collective-permute-start.9) | collective-permute-done | bytes 393248 | tf_op jit(solution)/shard_map/ppermute | solution.py:283
  57.9 0.8 collective-permute-start.11
  58.6 0.6 broadcast_in_dim.18
  59.3 6.4 %all-to-all-start.2 = ((f32[16,2,512]{2,1,0:T(2,128)}), f32[16,2,512]{2,1,0:T(2,128)S(1)}, u32[]{:S(2)}, u32[]{:S(2)}) async-start(f32[16,2,512]{2,1,0:T(2,128)} %broadcast_in_dim.18), calls=%async_computation.2 | async-start | bytes 131072 | tf_op jit(solution)/shard_map/all_to_all | solution.py:279
  65.7 6.4 %hash_1.1.table = f32[8,256]{1,0:T(8,128)S(1)} custom-call(s32[4,25]{1,0:T(4,128)S(1)} %pad_add_fusion.seeds, s32[1]{0:T(128)} %bitcast.13.meta, f32[25,4,128]{2,1,0:T(4,128)S(1)} %reshape.37.v, f32[8,256]{1,0:T(8,128)S(1)} %hash_0.1.table, f32[1,512]{1,0:T(1,128)S(1)} %bitcast.24), custom_call_target="tpu_custom_call" | custom-call | flops 6553600 | bytes 131072 | tf_op jit(solution)/shard_map/hash_1/pallas_call | solution.py:151
  72.1 6.4 %hash_2.1.refs_1_ = f32[8,256]{1,0:T(8,128)S(1)} custom-call(s32[4,25]{1,0:T(4,128)S(1)} %pad_add_fusion.seeds, s32[1]{0:T(128)} %bitcast.13.meta, f32[25,4,128]{2,1,0:T(4,128)S(1)} %reshape.37.v, f32[8,256]{1,0:T(8,128)S(1)} %hash_1.1.table, f32[1,512]{1,0:T(1,128)S(1)} %bitcast.25), custom_call_target="tpu_custom_call" | custom-call | flops 6553600 | bytes 131072 | tf_op jit(solution)/shard_map/hash_2/pallas_call | solution.py:151
  78.6 1.7 %step_0.1 = (f32[8,512]{1,0:T(8,128)S(1)}, f32[8,256]{1,0:T(8,128)S(1)}) custom-call(f32[16,2,512]{2,1,0:T(2,128)S(1)} %all-to-all-done.2.came, bf16[256,512]{1,0:T(8,128)(2,1)S(1)} %copy-done, f32[8,256]{1,0:T(8,128)S(1)} %hash_2.1.refs_1_, f32[4,4,16,512]{3,2,1,0:T(8,128)S(1)} %pad_maximum_fusion.refs_2_.refs_4_, ...), custom_call_target="tpu_custom_call" | custom-call | tf_op jit(solution)/shard_map/step_0/pallas_call | solution.py:228
  80.3 4.5 %collective-permute-start.13 = (f32[8,512]{1,0:T(8,128)S(1)}, f32[8,512]{1,0:T(8,128)S(1)}, u32[]{:S(2)}, u32[]{:S(2)}) collective-permute-start(f32[8,512]{1,0:T(8,128)S(1)} %get-tuple-element.36), channel_id=1, source_target_pairs={{0,3},{1,2},{16,19},{17,18},{32,35},{33,34},{48,51},{49,50},{64,67... | collective-permute-start | bytes 49160 | tf_op jit(solution)/shard_map/ppermute | solution.py:337
  84.8 1.3 collective-permute-start.12
  86.1 0.8 collective-permute-done.12.refs_0_
  87.0 0.7 collective-permute-start.15
  87.6 0.7 collective-permute-start.14
  88.3 6.4 %hash_3.1.refs_3_ = f32[8,256]{1,0:T(8,128)S(1)} custom-call(s32[4,25]{1,0:T(4,128)S(1)} %pad_add_fusion.seeds, s32[1]{0:T(128)} %bitcast.13.meta, f32[25,4,128]{2,1,0:T(4,128)S(1)} %reshape.37.v, f32[8,256]{1,0:T(8,128)S(1)} %get-tuple-element.39.table, f32[8,512]{1,0:T(8,128)S(1)} %get-tuple-element.38._), custom_call_target="tpu_custom_call" | custom-call | flops 6553600 | bytes 131072 | tf_op jit(solution)/shard_map/hash_3/pallas_call | solution.py:151
  94.8 0.7 collective-permute-start.17
  95.5 0.7 collective-permute-start.16
  96.1 6.4 %hash_4.1.refs_3_ = f32[8,256]{1,0:T(8,128)S(1)} custom-call(s32[4,25]{1,0:T(4,128)S(1)} %pad_add_fusion.seeds, s32[1]{0:T(128)} %bitcast.13.meta, f32[25,4,128]{2,1,0:T(4,128)S(1)} %reshape.37.v, f32[8,256]{1,0:T(8,128)S(1)} %get-tuple-element.41.table, f32[8,512]{1,0:T(8,128)S(1)} %get-tuple-element.40._), custom_call_target="tpu_custom_call" | custom-call | flops 6553600 | bytes 131072 | tf_op jit(solution)/shard_map/hash_4/pallas_call | solution.py:151
  102.7 0.7 collective-permute-start.19
  103.3 0.7 collective-permute-start.18
  104.0 6.4 %hash_5.1.refs_3_ = f32[8,256]{1,0:T(8,128)S(1)} custom-call(s32[4,25]{1,0:T(4,128)S(1)} %pad_add_fusion.seeds, s32[1]{0:T(128)} %bitcast.13.meta, f32[25,4,128]{2,1,0:T(4,128)S(1)} %reshape.37.v, f32[8,256]{1,0:T(8,128)S(1)} %get-tuple-element.43.table, f32[8,512]{1,0:T(8,128)S(1)} %get-tuple-element.42._), custom_call_target="tpu_custom_call" | custom-call | flops 6553600 | bytes 131072 | tf_op jit(solution)/shard_map/hash_5/pallas_call | solution.py:151
  110.5 0.7 collective-permute-start.21
  111.2 0.7 collective-permute-start.20
  111.9 0.7 collective-permute-start.23
  112.6 0.7 collective-permute-start.22
  113.4 6.4 %hash_6.1.refs_3_ = f32[8,256]{1,0:T(8,128)S(1)} custom-call(s32[4,25]{1,0:T(4,128)S(1)} %pad_add_fusion.seeds, s32[1]{0:T(128)} %bitcast.13.meta, f32[25,4,128]{2,1,0:T(4,128)S(1)} %reshape.37.v, f32[8,256]{1,0:T(8,128)S(1)} %get-tuple-element.47.table, f32[8,512]{1,0:T(8,128)S(1)} %get-tuple-element.46._), custom_call_target="tpu_custom_call" | custom-call | flops 6553600 | bytes 131072 | tf_op jit(solution)/shard_map/hash_6/pallas_call | solution.py:151
  120.0 0.8 collective-permute-start.25
  120.8 0.7 collective-permute-start.24
  121.5 0.6 copy-done.6
  122.2 1.5 %last.1 = f32[16,128]{1,0:T(8,128)} custom-call(f32[4]{0:T(128)S(1)} %compare_select_fusion.1.factor, s32[64]{0:T(128)S(1)} %copy-done.6, f32[16,128]{1,0:T(8,128)S(1)} %bitcast.26, f32[25,4,128]{2,1,0:T(4,128)S(1)} %reshape.37.v, f32[16,2,512]{2,1,0:T(2,128)S(1)} %all-to-all-done.2.came, bf16[2048,256]{1,0:T(8,128)(2,1)S(1)} %copy-done.2, ...), custom_call_target="tpu_custom_call" | custom-call | tf_op jit(solution)/shard_map/last/pallas_call | solution.py:268
  123.6 9.6 %all-to-all-start.3 = ((f32[16,1,128]{2,1,0:T(1,128)}), f32[16,1,128]{2,1,0:T(1,128)S(1)}, u32[]{:S(2)}, u32[]{:S(2)}) async-start(f32[16,1,128]{2,1,0:T(1,128)} %bitcast.17), calls=%async_computation.3 | async-start | bytes 16384 | tf_op jit(solution)/shard_map/all_to_all | solution.py:345
  133.3 0.6 slice.44
  133.8 6.4 %all-to-all-done.3 = f32[16,1,128]{2,1,0:T(1,128)S(1)} async-done(((f32[16,1,128]{2,1,0:T(1,128)}), f32[16,1,128]{2,1,0:T(1,128)S(1)}, u32[]{:S(2)}, u32[]{:S(2)}) %all-to-all-start.3) | async-done | bytes 8224 | tf_op jit(solution)/shard_map/all_to_all | solution.py:345
  (76 shorter events, 2.6 us)
Async XLA Ops:
  0.6 0.7 copy-start.5
  0.6 0.7 copy-start.4
  1.4 1.2 copy-start.1
  4.3 18.4 %all-to-all-start = ((f32[16,18,512]{2,1,0:T(8,128)}), f32[16,18,512]{2,1,0:T(8,128)S(1)}, u32[]{:S(2)}, u32[]{:S(2)}) async-start(f32[16,18,512]{2,1,0:T(8,128)} %spread_parts.1), calls=%async_computation | async-start | bytes 1572864 | tf_op jit(solution)/shard_map/all_to_all | solution.py:297
  10.9 0.7 copy-start.7
  11.7 0.7 copy-start.8
  11.7 0.7 copy-start.3
  23.0 16.8 %collective-permute-start.5 = (f32[3,16,512]{2,1,0:T(8,128)S(1)}, f32[3,16,512]{2,1,0:T(8,128)S(1)}, u32[]{:S(2)}, u32[]{:S(2)}) collective-permute-start(f32[3,16,512]{2,1,0:T(8,128)S(1)} %slice.41), channel_id=1, source_target_pairs={{0,192},{16,208},{32,224},{48,240},{64,128},{80,144},{96,160},{112... | collective-permute-start | bytes 294920 | tf_op jit(solution)/shard_map/ppermute | solution.py:283
  23.3 24.0 %collective-permute-start.4 = (f32[3,16,512]{2,1,0:T(8,128)S(1)}, f32[3,16,512]{2,1,0:T(8,128)S(1)}, u32[]{:S(2)}, u32[]{:S(2)}) collective-permute-start(f32[3,16,512]{2,1,0:T(8,128)S(1)} %slice.41), channel_id=1, source_target_pairs={{0,128},{16,144},{32,160},{48,176},{64,192},{80,208},{96,224},{112... | collective-permute-start | bytes 294920 | tf_op jit(solution)/shard_map/ppermute | solution.py:283
  25.7 21.6 %collective-permute-start.3 = (f32[3,16,512]{2,1,0:T(8,128)S(1)}, f32[3,16,512]{2,1,0:T(8,128)S(1)}, u32[]{:S(2)}, u32[]{:S(2)}) collective-permute-start(f32[3,16,512]{2,1,0:T(8,128)S(1)} %slice.41), channel_id=1, source_target_pairs={{0,64},{16,80},{32,96},{48,112},{64,0},{80,16},{96,32},{112,48},{1... | collective-permute-start | bytes 294920 | tf_op jit(solution)/shard_map/ppermute | solution.py:283
  26.3 21.1 %collective-permute-start.2 = (f32[4,16,512]{2,1,0:T(8,128)S(1)}, f32[4,16,512]{2,1,0:T(8,128)S(1)}, u32[]{:S(2)}, u32[]{:S(2)}) collective-permute-start(f32[4,16,512]{2,1,0:T(8,128)S(1)} %slice.40), channel_id=1, source_target_pairs={{0,48},{16,32},{32,16},{48,0},{64,112},{80,96},{96,80},{112,64},{1... | collective-permute-start | bytes 393224 | tf_op jit(solution)/shard_map/ppermute | solution.py:283
  26.6 20.8 %collective-permute-start.1 = (f32[4,16,512]{2,1,0:T(8,128)S(1)}, f32[4,16,512]{2,1,0:T(8,128)S(1)}, u32[]{:S(2)}, u32[]{:S(2)}) collective-permute-start(f32[4,16,512]{2,1,0:T(8,128)S(1)} %slice.40), channel_id=1, source_target_pairs={{0,32},{16,48},{32,0},{48,16},{64,96},{80,112},{96,64},{112,80},{1... | collective-permute-start | bytes 393224 | tf_op jit(solution)/shard_map/ppermute | solution.py:283
  28.7 18.6 %all-to-all-start.1 = ((f32[16,1,512]{2,1,0:T(1,128)}), f32[16,1,512]{2,1,0:T(1,128)S(1)}, u32[]{:S(2)}, u32[]{:S(2)}) async-start(f32[16,1,512]{2,1,0:T(1,128)} %first_rows.1._), calls=%async_computation.1 | async-start | bytes 65536 | tf_op jit(solution)/shard_map/all_to_all | solution.py:321
  39.8 7.6 %collective-permute-start = (f32[4,16,512]{2,1,0:T(8,128)S(1)}, f32[4,16,512]{2,1,0:T(8,128)S(1)}, u32[]{:S(2)}, u32[]{:S(2)}) collective-permute-start(f32[4,16,512]{2,1,0:T(8,128)S(1)} %slice.40), channel_id=1, source_target_pairs={{0,16},{16,0},{32,48},{48,32},{64,80},{80,64},{96,112},{112,96},{1... | collective-permute-start | bytes 393224 | tf_op jit(solution)/shard_map/ppermute | solution.py:283
  47.4 31.2 %copy-start = (bf16[256,512]{1,0:T(8,128)(2,1)S(1)}, bf16[256,512]{1,0:T(8,128)(2,1)}, u32[]{:S(2)}) copy-start(bf16[256,512]{1,0:T(8,128)(2,1)} %refs_2_.13) | copy-start | bytes 786436
  47.4 10.4 %collective-permute-start.9 = (f32[4,3,16,512]{3,2,1,0:T(8,128)S(1)}, f32[4,3,16,512]{3,2,1,0:T(8,128)S(1)}, u32[]{:S(2)}, u32[]{:S(2)}) collective-permute-start(f32[4,3,16,512]{3,2,1,0:T(8,128)S(1)} %pad_maximum_fusion.1.refs_6_.refs_8_.refs_4_), channel_id=1, source_target_pairs={{0,16},{16,0},{32,48},{48,32},{64,80},{80,64},{96,112},{112,96},{1... | collective-permute-start | bytes 1179656 | tf_op jit(solution)/shard_map/ppermute | solution.py:283
  48.3 30.2 %collective-permute-start.8 = (f32[4,4,16,512]{3,2,1,0:T(8,128)S(1)}, f32[4,4,16,512]{3,2,1,0:T(8,128)S(1)}, u32[]{:S(2)}, u32[]{:S(2)}) collective-permute-start(f32[4,4,16,512]{3,2,1,0:T(8,128)S(1)} %pad_maximum_fusion.refs_2_.refs_4_), channel_id=1, source_target_pairs={{0,192},{16,208},{32,224},{48,240},{64,128},{80,144},{96,160},{112... | collective-permute-start | bytes 1572872 | tf_op jit(solution)/shard_map/ppermute | solution.py:283
  48.6 30.0 %collective-permute-start.7 = (f32[4,4,16,512]{3,2,1,0:T(8,128)S(1)}, f32[4,4,16,512]{3,2,1,0:T(8,128)S(1)}, u32[]{:S(2)}, u32[]{:S(2)}) collective-permute-start(f32[4,4,16,512]{3,2,1,0:T(8,128)S(1)} %pad_maximum_fusion.refs_2_.refs_4_), channel_id=1, source_target_pairs={{0,128},{16,144},{32,160},{48,176},{64,192},{80,208},{96,224},{112... | collective-permute-start | bytes 1572872 | tf_op jit(solution)/shard_map/ppermute | solution.py:283
  51.0 27.6 %collective-permute-start.6 = (f32[4,4,16,512]{3,2,1,0:T(8,128)S(1)}, f32[4,4,16,512]{3,2,1,0:T(8,128)}, u32[]{:S(2)}, u32[]{:S(2)}) collective-permute-start(f32[4,4,16,512]{3,2,1,0:T(8,128)S(1)} %pad_maximum_fusion.refs_2_.refs_4_), channel_id=1, source_target_pairs={{0,64},{16,80},{32,96},{48,112},{64,0},{80,16},{96,32},{112,48},{1... | collective-permute-start | bytes 1572872 | tf_op jit(solution)/shard_map/ppermute | solution.py:283
  51.6 27.0 %collective-permute-start.10 = (f32[4,3,16,512]{3,2,1,0:T(8,128)S(1)}, f32[4,3,16,512]{3,2,1,0:T(8,128)S(1)}, u32[]{:S(2)}, u32[]{:S(2)}) collective-permute-start(f32[4,3,16,512]{3,2,1,0:T(8,128)S(1)} %pad_maximum_fusion.1.refs_6_.refs_8_.refs_4_), channel_id=1, source_target_pairs={{0,32},{16,48},{32,0},{48,16},{64,96},{80,112},{96,64},{112,80},{1... | collective-permute-start | bytes 1179656 | tf_op jit(solution)/shard_map/ppermute | solution.py:283
  57.9 20.7 %collective-permute-start.11 = (f32[4,3,16,512]{3,2,1,0:T(8,128)S(1)}, f32[4,3,16,512]{3,2,1,0:T(8,128)S(1)}, u32[]{:S(2)}, u32[]{:S(2)}) collective-permute-start(f32[4,3,16,512]{3,2,1,0:T(8,128)S(1)} %pad_maximum_fusion.1.refs_6_.refs_8_.refs_4_), channel_id=1, source_target_pairs={{0,48},{16,32},{32,16},{48,0},{64,112},{80,96},{96,80},{112,64},{1... | collective-permute-start | bytes 1179656 | tf_op jit(solution)/shard_map/ppermute | solution.py:283
  59.3 19.3 %all-to-all-start.2 = ((f32[16,2,512]{2,1,0:T(2,128)}), f32[16,2,512]{2,1,0:T(2,128)S(1)}, u32[]{:S(2)}, u32[]{:S(2)}) async-start(f32[16,2,512]{2,1,0:T(2,128)} %broadcast_in_dim.18), calls=%async_computation.2 | async-start | bytes 131072 | tf_op jit(solution)/shard_map/all_to_all | solution.py:279
  80.3 5.8 %collective-permute-start.13 = (f32[8,512]{1,0:T(8,128)S(1)}, f32[8,512]{1,0:T(8,128)S(1)}, u32[]{:S(2)}, u32[]{:S(2)}) collective-permute-start(f32[8,512]{1,0:T(8,128)S(1)} %get-tuple-element.36), channel_id=1, source_target_pairs={{0,3},{1,2},{16,19},{17,18},{32,35},{33,34},{48,51},{49,50},{64,67... | collective-permute-start | bytes 49160 | tf_op jit(solution)/shard_map/ppermute | solution.py:337
  84.8 2.1 %collective-permute-start.12 = (f32[8,512]{1,0:T(8,128)S(1)}, f32[8,512]{1,0:T(8,128)S(1)}, u32[]{:S(2)}, u32[]{:S(2)}) collective-permute-start(f32[8,512]{1,0:T(8,128)S(1)} %get-tuple-element.36), channel_id=1, source_target_pairs={{0,2},{1,3},{16,18},{17,19},{32,34},{33,35},{48,50},{49,51},{64,66... | collective-permute-start | bytes 49160 | tf_op jit(solution)/shard_map/ppermute | solution.py:336
  87.0 7.8 %collective-permute-start.15 = (f32[8,512]{1,0:T(8,128)S(1)}, f32[8,512]{1,0:T(8,128)S(1)}, u32[]{:S(2)}, u32[]{:S(2)}) collective-permute-start(f32[8,512]{1,0:T(8,128)S(1)} %get-tuple-element.38._), channel_id=1, source_target_pairs={{2,5},{3,4},{18,21},{19,20},{34,37},{35,36},{50,53},{51,52},{66,69... | collective-permute-start | bytes 49160 | tf_op jit(solution)/shard_map/ppermute | solution.py:337
  87.6 7.1 %collective-permute-start.14 = (f32[8,512]{1,0:T(8,128)S(1)}, f32[8,512]{1,0:T(8,128)S(1)}, u32[]{:S(2)}, u32[]{:S(2)}) collective-permute-start(f32[8,512]{1,0:T(8,128)S(1)} %get-tuple-element.38._), channel_id=1, source_target_pairs={{2,4},{3,5},{18,20},{19,21},{34,36},{35,37},{50,52},{51,53},{66,68... | collective-permute-start | bytes 49160 | tf_op jit(solution)/shard_map/ppermute | solution.py:336
  94.8 7.8 %collective-permute-start.17 = (f32[8,512]{1,0:T(8,128)S(1)}, f32[8,512]{1,0:T(8,128)S(1)}, u32[]{:S(2)}, u32[]{:S(2)}) collective-permute-start(f32[8,512]{1,0:T(8,128)S(1)} %get-tuple-element.40._), channel_id=1, source_target_pairs={{4,7},{5,6},{20,23},{21,22},{36,39},{37,38},{52,55},{53,54},{68,71... | collective-permute-start | bytes 49160 | tf_op jit(solution)/shard_map/ppermute | solution.py:337
  95.5 7.1 %collective-permute-start.16 = (f32[8,512]{1,0:T(8,128)S(1)}, f32[8,512]{1,0:T(8,128)S(1)}, u32[]{:S(2)}, u32[]{:S(2)}) collective-permute-start(f32[8,512]{1,0:T(8,128)S(1)} %get-tuple-element.40._), channel_id=1, source_target_pairs={{4,6},{5,7},{20,22},{21,23},{36,38},{37,39},{52,54},{53,55},{68,70... | collective-permute-start | bytes 49160 | tf_op jit(solution)/shard_map/ppermute | solution.py:336
  102.7 7.8 %collective-permute-start.19 = (f32[8,512]{1,0:T(8,128)S(1)}, f32[8,512]{1,0:T(8,128)S(1)}, u32[]{:S(2)}, u32[]{:S(2)}) collective-permute-start(f32[8,512]{1,0:T(8,128)S(1)} %get-tuple-element.42._), channel_id=1, source_target_pairs={{6,9},{7,8},{22,25},{23,24},{38,41},{39,40},{54,57},{55,56},{70,73... | collective-permute-start | bytes 49160 | tf_op jit(solution)/shard_map/ppermute | solution.py:337
  103.3 7.1 %collective-permute-start.18 = (f32[8,512]{1,0:T(8,128)S(1)}, f32[8,512]{1,0:T(8,128)S(1)}, u32[]{:S(2)}, u32[]{:S(2)}) collective-permute-start(f32[8,512]{1,0:T(8,128)S(1)} %get-tuple-element.42._), channel_id=1, source_target_pairs={{6,8},{7,9},{22,24},{23,25},{38,40},{39,41},{54,56},{55,57},{70,72... | collective-permute-start | bytes 49160 | tf_op jit(solution)/shard_map/ppermute | solution.py:336
  110.5 1.3 collective-permute-start.21
  111.2 0.7 collective-permute-start.20
  111.9 8.0 %collective-permute-start.23 = (f32[8,512]{1,0:T(8,128)S(1)}, f32[8,512]{1,0:T(8,128)S(1)}, u32[]{:S(2)}, u32[]{:S(2)}) collective-permute-start(f32[8,512]{1,0:T(8,128)S(1)} %get-tuple-element.46._), channel_id=1, source_target_pairs={{10,13},{11,12},{26,29},{27,28},{42,45},{43,44},{58,61},{59,60},{7... | collective-permute-start | bytes 49160 | tf_op jit(solution)/shard_map/ppermute | solution.py:337
  112.6 7.4 %collective-permute-start.22 = (f32[8,512]{1,0:T(8,128)S(1)}, f32[8,512]{1,0:T(8,128)S(1)}, u32[]{:S(2)}, u32[]{:S(2)}) collective-permute-start(f32[8,512]{1,0:T(8,128)S(1)} %get-tuple-element.46._), channel_id=1, source_target_pairs={{10,12},{11,13},{26,28},{27,29},{42,44},{43,45},{58,60},{59,61},{7... | collective-permute-start | bytes 49160 | tf_op jit(solution)/shard_map/ppermute | solution.py:336
  119.9 1.6 %copy-start.2 = (bf16[2048,256]{1,0:T(8,128)(2,1)S(1)}, bf16[2048,256]{1,0:T(8,128)(2,1)}, u32[]{:S(2)}) copy-start(bf16[2048,256]{1,0:T(8,128)(2,1)} %panel.3) | copy-start | bytes 3145732
  120.0 1.5 %collective-permute-start.25 = (f32[8,512]{1,0:T(8,128)S(1)}, f32[8,512]{1,0:T(8,128)S(1)}, u32[]{:S(2)}, u32[]{:S(2)}) collective-permute-start(f32[8,512]{1,0:T(8,128)S(1)} %get-tuple-element.48), channel_id=1, source_target_pairs={{12,15},{13,14},{28,31},{29,30},{44,47},{45,46},{60,63},{61,62},{7... | collective-permute-start | bytes 49160 | tf_op jit(solution)/shard_map/ppermute | solution.py:337
  120.8 0.7 collective-permute-start.24
  121.5 0.7 copy-start.6
  123.6 16.6 %all-to-all-start.3 = ((f32[16,1,128]{2,1,0:T(1,128)}), f32[16,1,128]{2,1,0:T(1,128)S(1)}, u32[]{:S(2)}, u32[]{:S(2)}) async-start(f32[16,1,128]{2,1,0:T(1,128)} %bitcast.17), calls=%async_computation.3 | async-start | bytes 16384 | tf_op jit(solution)/shard_map/all_to_all | solution.py:345

commit v6 on v5

--- a/solution.py
+++ b/solution.py
@@ -22,7 +22,7 @@
 WIDE = 64
 WINDOW = 7
 AHEAD = 2
-GAPS = (1, 2, 3, 5)
+GAPS = (1, 2, 4)
 BIAS = -127.5
 
 VMEM = pl.BlockSpec(memory_space=pltpu.VMEM)
@@ -320,12 +320,14 @@
     table = hash_rows(seed_rows, meta, v, jnp.zeros((KB, PIECE), jnp.float32), parts, 0)
     part = jnp.sum(lax.all_to_all(parts, "pcol", 0, 0, tiled=True), axis=0)
     near, far, part, table = lax.optimization_barrier((near, far, part, table))
+    shared_sum = table[1:2]
     first, second = exchange(far, 1), exchange(far, 2)
     across = [exchange(near, m) for m in (4, 8, 12)]
-    far, first = lax.optimization_barrier((far, first))
+    table = hash_rows(seed_rows, meta, v, table, part, 1)
+    far, first, table = lax.optimization_barrier((far, first, table))
     tiles = [near] + across + [far, first, second, exchange(far, 3)]
-    came = to_all(jnp.concatenate([part, jnp.pad(table[1:2], ((0, 0), (0, PIECE)))]), "prow")
-    row = 1
+    came = to_all(jnp.concatenate([part, jnp.pad(shared_sum, ((0, 0), (0, PIECE)))]), "prow")
+    row = 2
     for _ in range(AHEAD):
         table = hash_rows(seed_rows, meta, v, table, part, row)
         row += 1

time: 142 us -> 144 us (1.014)
  starting transfers between devices: 60.3 us -> 66.6 us
  waiting for transfers between devices: 12.5 us -> 7.36 us
    all_to_all x1, starting transfers between devices: 9.62 us -> 14.8 us  [body(): updated = jnp.sum(lax.all_to_all(sums, 'pcol', 0, 0, tiled=True), axis=0)]
    ppermute x12, waiting for transfers between devices: 5.14 us -> 0.03 us  [exchange(): return lax.ppermute(value, 'prow', [(i, i ^ mask) for i in range(GRID)])]
  transfers between devices with their start and end apart: 30 -> 30, of which waited for: 3 -> 2; matrix products, arithmetic and copies ran while one was open for 1% -> 1% of each run, Pallas kernels for 39% -> 39%
where the time goes in v6:
time: 144 us; the launch traced here: 142 us
  starting transfers between devices  66.6 us (46%)
  Pallas kernels  60.3 us (42%)
  waiting for transfers between devices  7.36 us (5%)
  local copies, waits for them, and re-layouts  5.64 us (4%)
  between operations  1.44 us (1%)
    pallas_call x7, Pallas kernels, hash_rows(): pl.pallas_call(functools.partial(hash_kernel, row, tile, start), out_shap...  45.1 us
    all_to_all x1, starting transfers between devices, body(): updated = jnp.sum(lax.all_to_all(sums, 'pcol', 0, 0, tiled=True), axis=0)  14.8 us
    ppermute x12, starting transfers between devices, exchange(): return lax.ppermute(value, 'prow', [(i, i ^ mask) for i in range(GRID)])  14 us
    all_to_all x1, starting transfers between devices, body(): part = jnp.sum(lax.all_to_all(parts, 'pcol', 0, 0, tiled=True), axis=0)  11.1 us
    pallas_call x1, Pallas kernels, first_rows(): pl.pallas_call(first_kernel, out_shape=jax.ShapeDtypeStruct((GRID, 1, NB)...  10 us
    ppermute x7, starting transfers between devices, body(): lax.ppermute(total, 'pcol', [(2 * k + h, 2 * k + 3 - h) for h in range(2)])  8.51 us
    all_to_all x1, starting transfers between devices, body(): came = lax.all_to_all(sent, 'prow', 0, 0, tiled=True)  6.56 us
    all_to_all x1, waiting for transfers between devices, body(): updated = jnp.sum(lax.all_to_all(sums, 'pcol', 0, 0, tiled=True), axis=0)  6.45 us
  transfers between devices with their start and end apart: 30, of which 2 were waited for; matrix products, arithmetic and copies ran while one was open for 1% of the time, Pallas kernels for 39%

profile of v6, /device:TPU:29, one launch (start us, length us, event | category | flops | bytes accessed | tf_op | source)
XLA Modules:
  0.0 142.2 jit_solution(298391115860383966)
XLA Ops:
  0.7 0.7 reshape.32.vector
  1.4 1.2 copy-done.1
  2.6 1.7 %spread_parts.1 = f32[16,18,512]{2,1,0:T(8,128)} custom-call(s32[64]{0:T(128)S(1)} %copy-done.5, f32[4,8]{1,0:T(4,128)S(1)} %copy-done.4, f32[1,800]{1,0:T(1,128)S(1)} %reshape.32.vector, bf16[2048,256]{1,0:T(8,128)(2,1)S(1)} %copy-done.1), custom_call_target="tpu_custom_call" | custom-call | tf_op jit(solution)/shard_map/spread_parts/pallas_call | solution.py:116
  4.3 6.6 %all-to-all-start = ((f32[16,18,512]{2,1,0:T(8,128)}), f32[16,18,512]{2,1,0:T(8,128)S(1)}, u32[]{:S(2)}, u32[]{:S(2)}) async-start(f32[16,18,512]{2,1,0:T(8,128)} %spread_parts.1), calls=%async_computation | async-start | bytes 1572864 | tf_op jit(solution)/shard_map/all_to_all | solution.py:297
  10.9 0.7 copy-done.7
  11.8 0.6 copy-done.3
  12.6 10.0 %first_rows.1._ = f32[16,1,512]{2,1,0:T(1,128)} custom-call(s32[64]{0:T(128)S(1)} %copy-done.5, s32[64,25]{1,0:T(8,128)S(1)} %copy.12.seeds, f32[7,128]{1,0:T(8,128)S(1)} %dynamic-slice_bitcast_fusion.window, f32[1,512]{1,0:T(1,128)S(1)} %bitcast.29, f32[1,512]{1,0:T(1,128)S(1)} %bitcast.28), custom_call_target="tpu_custom_call" | custom-call | flops 6553600 | bytes 32768 | tf_op jit(solution)/shard_map/first_rows/pallas_call | solution.py:89
  23.3 2.4 %collective-permute-start.4 = (f32[3,16,512]{2,1,0:T(8,128)S(1)}, f32[3,16,512]{2,1,0:T(8,128)S(1)}, u32[]{:S(2)}, u32[]{:S(2)}) collective-permute-start(f32[3,16,512]{2,1,0:T(8,128)S(1)} %slice.41), channel_id=1, source_target_pairs={{0,128},{16,144},{32,160},{48,176},{64,192},{80,208},{96,224},{112... | collective-permute-start | bytes 294920 | tf_op jit(solution)/shard_map/ppermute | solution.py:283
  25.7 0.6 collective-permute-start.3
  26.6 2.1 %collective-permute-start.1 = (f32[4,16,512]{2,1,0:T(8,128)S(1)}, f32[4,16,512]{2,1,0:T(8,128)S(1)}, u32[]{:S(2)}, u32[]{:S(2)}) collective-permute-start(f32[4,16,512]{2,1,0:T(8,128)S(1)} %slice.40), channel_id=1, source_target_pairs={{0,32},{16,48},{32,0},{48,16},{64,96},{80,112},{96,64},{112,80},{1... | collective-permute-start | bytes 393224 | tf_op jit(solution)/shard_map/ppermute | solution.py:283
  28.7 11.1 %all-to-all-start.1 = ((f32[16,1,512]{2,1,0:T(1,128)}), f32[16,1,512]{2,1,0:T(1,128)S(1)}, u32[]{:S(2)}, u32[]{:S(2)}) async-start(f32[16,1,512]{2,1,0:T(1,128)} %first_rows.1._), calls=%async_computation.1 | async-start | bytes 65536 | tf_op jit(solution)/shard_map/all_to_all | solution.py:321
  39.8 1.0 collective-permute-start
  40.8 6.4 %hash_0.1.table = f32[8,256]{1,0:T(8,128)S(1)} custom-call(s32[4,25]{1,0:T(4,128)S(1)} %pad_add_fusion.seeds, s32[1]{0:T(128)} %bitcast.13.meta, f32[25,4,128]{2,1,0:T(4,128)S(1)} %reshape.37.v, f32[8,256]{1,0:T(8,128)S(1)} %broadcast_in_dim.17.table, f32[16,1,512]{2,1,0:T(1,128)} %first_rows.1._), custom_call_target="tpu_custom_call" | custom-call | flops 6553600 | bytes 131072 | tf_op jit(solution)/shard_map/hash_0/pallas_call | solution.py:151
  47.4 0.9 collective-permute-start.6
  48.6 2.4 %collective-permute-start.8 = (f32[4,4,16,512]{3,2,1,0:T(8,128)S(1)}, f32[4,4,16,512]{3,2,1,0:T(8,128)S(1)}, u32[]{:S(2)}, u32[]{:S(2)}) collective-permute-start(f32[4,4,16,512]{3,2,1,0:T(8,128)S(1)} %pad_maximum_fusion.refs_2_.refs_4_), channel_id=1, source_target_pairs={{0,128},{16,144},{32,160},{48,176},{64,192},{80,208},{96,224},{112... | collective-permute-start | bytes 1572872 | tf_op jit(solution)/shard_map/ppermute | solution.py:283
  51.0 0.6 collective-permute-start.7
  51.6 1.2 collective-permute-start.10
  52.8 6.4 %hash_1.1.table = f32[8,256]{1,0:T(8,128)S(1)} custom-call(s32[4,25]{1,0:T(4,128)S(1)} %pad_add_fusion.seeds, s32[1]{0:T(128)} %bitcast.13.meta, f32[25,4,128]{2,1,0:T(4,128)S(1)} %reshape.37.v, f32[8,256]{1,0:T(8,128)S(1)} %hash_0.1.table, f32[1,512]{1,0:T(1,128)S(1)} %bitcast.23), custom_call_target="tpu_custom_call" | custom-call | flops 6553600 | bytes 131072 | tf_op jit(solution)/shard_map/hash_1/pallas_call | solution.py:151
  59.2 2.0 %collective-permute-start.11 = (f32[4,3,16,512]{3,2,1,0:T(8,128)S(1)}, f32[4,3,16,512]{3,2,1,0:T(8,128)S(1)}, u32[]{:S(2)}, u32[]{:S(2)}) collective-permute-start(f32[4,3,16,512]{3,2,1,0:T(8,128)S(1)} %pad_maximum_fusion.1.refs_6_.refs_8_.refs_4_), channel_id=1, source_target_pairs={{0,48},{16,32},{32,16},{48,0},{64,112},{80,96},{96,80},{112,64},{1... | collective-permute-start | bytes 1179656 | tf_op jit(solution)/shard_map/ppermute | solution.py:283
  61.2 0.6 broadcast_in_dim.18
  61.8 6.4 %all-to-all-start.2 = ((f32[16,2,512]{2,1,0:T(2,128)}), f32[16,2,512]{2,1,0:T(2,128)S(1)}, u32[]{:S(2)}, u32[]{:S(2)}) async-start(f32[16,2,512]{2,1,0:T(2,128)} %broadcast_in_dim.18), calls=%async_computation.2 | async-start | bytes 131072 | tf_op jit(solution)/shard_map/all_to_all | solution.py:279
  68.2 6.4 %hash_2.1.table = f32[8,256]{1,0:T(8,128)S(1)} custom-call(s32[4,25]{1,0:T(4,128)S(1)} %pad_add_fusion.seeds, s32[1]{0:T(128)} %bitcast.13.meta, f32[25,4,128]{2,1,0:T(4,128)S(1)} %reshape.37.v, f32[8,256]{1,0:T(8,128)S(1)} %hash_1.1.table, f32[1,512]{1,0:T(1,128)S(1)} %bitcast.25), custom_call_target="tpu_custom_call" | custom-call | flops 6553600 | bytes 131072 | tf_op jit(solution)/shard_map/hash_2/pallas_call | solution.py:151
  74.7 6.4 %hash_3.1.refs_1_ = f32[8,256]{1,0:T(8,128)S(1)} custom-call(s32[4,25]{1,0:T(4,128)S(1)} %pad_add_fusion.seeds, s32[1]{0:T(128)} %bitcast.13.meta, f32[25,4,128]{2,1,0:T(4,128)S(1)} %reshape.37.v, f32[8,256]{1,0:T(8,128)S(1)} %hash_2.1.table, f32[1,512]{1,0:T(1,128)S(1)} %bitcast.26), custom_call_target="tpu_custom_call" | custom-call | flops 6553600 | bytes 131072 | tf_op jit(solution)/shard_map/hash_3/pallas_call | solution.py:151
  81.2 1.9 %step_0.1 = (f32[8,512]{1,0:T(8,128)S(1)}, f32[8,256]{1,0:T(8,128)S(1)}) custom-call(f32[16,2,512]{2,1,0:T(2,128)S(1)} %all-to-all-done.2.came, bf16[256,512]{1,0:T(8,128)(2,1)S(1)} %copy-done, f32[8,256]{1,0:T(8,128)S(1)} %hash_3.1.refs_1_, f32[4,4,16,512]{3,2,1,0:T(8,128)S(1)} %pad_maximum_fusion.refs_2_.refs_4_, ...), custom_call_target="tpu_custom_call" | custom-call | tf_op jit(solution)/shard_map/step_0/pallas_call | solution.py:228
  83.0 4.4 %collective-permute-start.13 = (f32[8,512]{1,0:T(8,128)S(1)}, f32[8,512]{1,0:T(8,128)S(1)}, u32[]{:S(2)}, u32[]{:S(2)}) collective-permute-start(f32[8,512]{1,0:T(8,128)S(1)} %get-tuple-element.38), channel_id=1, source_target_pairs={{0,3},{1,2},{16,19},{17,18},{32,35},{33,34},{48,51},{49,50},{64,67... | collective-permute-start | bytes 49160 | tf_op jit(solution)/shard_map/ppermute | solution.py:339
  87.4 1.3 collective-permute-start.12
  88.7 0.8 collective-permute-done.12.refs_0_
  89.6 0.7 collective-permute-start.15
  90.3 0.7 collective-permute-start.14
  90.9 6.4 %hash_4.1.refs_3_ = f32[8,256]{1,0:T(8,128)S(1)} custom-call(s32[4,25]{1,0:T(4,128)S(1)} %pad_add_fusion.seeds, s32[1]{0:T(128)} %bitcast.13.meta, f32[25,4,128]{2,1,0:T(4,128)S(1)} %reshape.37.v, f32[8,256]{1,0:T(8,128)S(1)} %get-tuple-element.41.table, f32[8,512]{1,0:T(8,128)S(1)} %get-tuple-element.40._), custom_call_target="tpu_custom_call" | custom-call | flops 6553600 | bytes 131072 | tf_op jit(solution)/shard_map/hash_4/pallas_call | solution.py:151
  97.5 0.7 collective-permute-start.17
  98.1 0.7 collective-permute-start.16
  98.8 6.4 %hash_5.1.refs_3_ = f32[8,256]{1,0:T(8,128)S(1)} custom-call(s32[4,25]{1,0:T(4,128)S(1)} %pad_add_fusion.seeds, s32[1]{0:T(128)} %bitcast.13.meta, f32[25,4,128]{2,1,0:T(4,128)S(1)} %reshape.37.v, f32[8,256]{1,0:T(8,128)S(1)} %get-tuple-element.43.table, f32[8,512]{1,0:T(8,128)S(1)} %get-tuple-element.42._), custom_call_target="tpu_custom_call" | custom-call | flops 6553600 | bytes 131072 | tf_op jit(solution)/shard_map/hash_5/pallas_call | solution.py:151
  105.3 0.7 collective-permute-start.19
  106.0 0.7 collective-permute-start.18
  106.7 0.7 collective-permute-start.21
  107.4 0.7 collective-permute-start.20
  108.0 6.4 %hash_6.1.refs_3_ = f32[8,256]{1,0:T(8,128)S(1)} custom-call(s32[4,25]{1,0:T(4,128)S(1)} %pad_add_fusion.seeds, s32[1]{0:T(128)} %bitcast.13.meta, f32[25,4,128]{2,1,0:T(4,128)S(1)} %reshape.37.v, f32[8,256]{1,0:T(8,128)S(1)} %get-tuple-element.47.table, f32[8,512]{1,0:T(8,128)S(1)} %get-tuple-element.46._), custom_call_target="tpu_custom_call" | custom-call | flops 6553600 | bytes 131072 | tf_op jit(solution)/shard_map/hash_6/pallas_call | solution.py:151
  114.6 0.7 collective-permute-start.23
  115.2 0.7 collective-permute-start.22
  116.2 0.8 collective-permute-start.25
  117.0 0.7 collective-permute-start.24
  117.7 0.6 copy-done.6
  118.4 1.5 %last.1 = f32[16,128]{1,0:T(8,128)} custom-call(f32[4]{0:T(128)S(1)} %compare_select_fusion.1.factor, s32[64]{0:T(128)S(1)} %copy-done.6, f32[16,128]{1,0:T(8,128)S(1)} %bitcast.27, f32[25,4,128]{2,1,0:T(4,128)S(1)} %reshape.37.v, f32[16,2,512]{2,1,0:T(2,128)S(1)} %all-to-all-done.2.came, bf16[2048,256]{1,0:T(8,128)(2,1)S(1)} %copy-done.2, ...), custom_call_target="tpu_custom_call" | custom-call | tf_op jit(solution)/shard_map/last/pallas_call | solution.py:268
  119.9 14.8 %all-to-all-start.3 = ((f32[16,1,128]{2,1,0:T(1,128)}), f32[16,1,128]{2,1,0:T(1,128)S(1)}, u32[]{:S(2)}, u32[]{:S(2)}) async-start(f32[16,1,128]{2,1,0:T(1,128)} %bitcast.17), calls=%async_computation.3 | async-start | bytes 16384 | tf_op jit(solution)/shard_map/all_to_all | solution.py:347
  134.6 0.6 slice.44
  135.2 6.4 %all-to-all-done.3 = f32[16,1,128]{2,1,0:T(1,128)S(1)} async-done(((f32[16,1,128]{2,1,0:T(1,128)}), f32[16,1,128]{2,1,0:T(1,128)S(1)}, u32[]{:S(2)}, u32[]{:S(2)}) %all-to-all-start.3) | async-done | bytes 8224 | tf_op jit(solution)/shard_map/all_to_all | solution.py:347
  141.6 0.5 reduce_sum.22
  (76 shorter events, 2.1 us)
Async XLA Ops:
  0.6 0.7 copy-start.5
  0.6 0.7 copy-start.4
  1.4 1.2 copy-start.1
  4.3 18.4 %all-to-all-start = ((f32[16,18,512]{2,1,0:T(8,128)}), f32[16,18,512]{2,1,0:T(8,128)S(1)}, u32[]{:S(2)}, u32[]{:S(2)}) async-start(f32[16,18,512]{2,1,0:T(8,128)} %spread_parts.1), calls=%async_computation | async-start | bytes 1572864 | tf_op jit(solution)/shard_map/all_to_all | solution.py:297
  10.9 0.7 copy-start.7
  11.7 0.7 copy-start.8
  11.7 0.7 copy-start.3
  23.0 16.8 %collective-permute-start.5 = (f32[3,16,512]{2,1,0:T(8,128)S(1)}, f32[3,16,512]{2,1,0:T(8,128)S(1)}, u32[]{:S(2)}, u32[]{:S(2)}) collective-permute-start(f32[3,16,512]{2,1,0:T(8,128)S(1)} %slice.41), channel_id=1, source_target_pairs={{0,192},{16,208},{32,224},{48,240},{64,128},{80,144},{96,160},{112... | collective-permute-start | bytes 294920 | tf_op jit(solution)/shard_map/ppermute | solution.py:283
  23.3 24.0 %collective-permute-start.4 = (f32[3,16,512]{2,1,0:T(8,128)S(1)}, f32[3,16,512]{2,1,0:T(8,128)S(1)}, u32[]{:S(2)}, u32[]{:S(2)}) collective-permute-start(f32[3,16,512]{2,1,0:T(8,128)S(1)} %slice.41), channel_id=1, source_target_pairs={{0,128},{16,144},{32,160},{48,176},{64,192},{80,208},{96,224},{112... | collective-permute-start | bytes 294920 | tf_op jit(solution)/shard_map/ppermute | solution.py:283
  25.7 21.6 %collective-permute-start.3 = (f32[3,16,512]{2,1,0:T(8,128)S(1)}, f32[3,16,512]{2,1,0:T(8,128)S(1)}, u32[]{:S(2)}, u32[]{:S(2)}) collective-permute-start(f32[3,16,512]{2,1,0:T(8,128)S(1)} %slice.41), channel_id=1, source_target_pairs={{0,64},{16,80},{32,96},{48,112},{64,0},{80,16},{96,32},{112,48},{1... | collective-permute-start | bytes 294920 | tf_op jit(solution)/shard_map/ppermute | solution.py:283
  26.3 21.1 %collective-permute-start.2 = (f32[4,16,512]{2,1,0:T(8,128)S(1)}, f32[4,16,512]{2,1,0:T(8,128)S(1)}, u32[]{:S(2)}, u32[]{:S(2)}) collective-permute-start(f32[4,16,512]{2,1,0:T(8,128)S(1)} %slice.40), channel_id=1, source_target_pairs={{0,48},{16,32},{32,16},{48,0},{64,112},{80,96},{96,80},{112,64},{1... | collective-permute-start | bytes 393224 | tf_op jit(solution)/shard_map/ppermute | solution.py:283
  26.6 20.8 %collective-permute-start.1 = (f32[4,16,512]{2,1,0:T(8,128)S(1)}, f32[4,16,512]{2,1,0:T(8,128)S(1)}, u32[]{:S(2)}, u32[]{:S(2)}) collective-permute-start(f32[4,16,512]{2,1,0:T(8,128)S(1)} %slice.40), channel_id=1, source_target_pairs={{0,32},{16,48},{32,0},{48,16},{64,96},{80,112},{96,64},{112,80},{1... | collective-permute-start | bytes 393224 | tf_op jit(solution)/shard_map/ppermute | solution.py:283
  28.7 18.6 %all-to-all-start.1 = ((f32[16,1,512]{2,1,0:T(1,128)}), f32[16,1,512]{2,1,0:T(1,128)S(1)}, u32[]{:S(2)}, u32[]{:S(2)}) async-start(f32[16,1,512]{2,1,0:T(1,128)} %first_rows.1._), calls=%async_computation.1 | async-start | bytes 65536 | tf_op jit(solution)/shard_map/all_to_all | solution.py:321
  39.8 7.6 %collective-permute-start = (f32[4,16,512]{2,1,0:T(8,128)S(1)}, f32[4,16,512]{2,1,0:T(8,128)S(1)}, u32[]{:S(2)}, u32[]{:S(2)}) collective-permute-start(f32[4,16,512]{2,1,0:T(8,128)S(1)} %slice.40), channel_id=1, source_target_pairs={{0,16},{16,0},{32,48},{48,32},{64,80},{80,64},{96,112},{112,96},{1... | collective-permute-start | bytes 393224 | tf_op jit(solution)/shard_map/ppermute | solution.py:283
  47.4 33.7 %copy-start = (bf16[256,512]{1,0:T(8,128)(2,1)S(1)}, bf16[256,512]{1,0:T(8,128)(2,1)}, u32[]{:S(2)}) copy-start(bf16[256,512]{1,0:T(8,128)(2,1)} %refs_2_.13) | copy-start | bytes 786436
  47.4 11.7 %collective-permute-start.6 = (f32[4,3,16,512]{3,2,1,0:T(8,128)S(1)}, f32[4,3,16,512]{3,2,1,0:T(8,128)S(1)}, u32[]{:S(2)}, u32[]{:S(2)}) collective-permute-start(f32[4,3,16,512]{3,2,1,0:T(8,128)S(1)} %pad_maximum_fusion.1.refs_6_.refs_8_.refs_4_), channel_id=1, source_target_pairs={{0,16},{16,0},{32,48},{48,32},{64,80},{80,64},{96,112},{112,96},{1... | collective-permute-start | bytes 1179656 | tf_op jit(solution)/shard_map/ppermute | solution.py:283
  48.3 32.8 %collective-permute-start.9 = (f32[4,4,16,512]{3,2,1,0:T(8,128)S(1)}, f32[4,4,16,512]{3,2,1,0:T(8,128)S(1)}, u32[]{:S(2)}, u32[]{:S(2)}) collective-permute-start(f32[4,4,16,512]{3,2,1,0:T(8,128)S(1)} %pad_maximum_fusion.refs_2_.refs_4_), channel_id=1, source_target_pairs={{0,192},{16,208},{32,224},{48,240},{64,128},{80,144},{96,160},{112... | collective-permute-start | bytes 1572872 | tf_op jit(solution)/shard_map/ppermute | solution.py:283
  48.6 32.5 %collective-permute-start.8 = (f32[4,4,16,512]{3,2,1,0:T(8,128)S(1)}, f32[4,4,16,512]{3,2,1,0:T(8,128)S(1)}, u32[]{:S(2)}, u32[]{:S(2)}) collective-permute-start(f32[4,4,16,512]{3,2,1,0:T(8,128)S(1)} %pad_maximum_fusion.refs_2_.refs_4_), channel_id=1, source_target_pairs={{0,128},{16,144},{32,160},{48,176},{64,192},{80,208},{96,224},{112... | collective-permute-start | bytes 1572872 | tf_op jit(solution)/shard_map/ppermute | solution.py:283
  51.0 30.1 %collective-permute-start.7 = (f32[4,4,16,512]{3,2,1,0:T(8,128)S(1)}, f32[4,4,16,512]{3,2,1,0:T(8,128)}, u32[]{:S(2)}, u32[]{:S(2)}) collective-permute-start(f32[4,4,16,512]{3,2,1,0:T(8,128)S(1)} %pad_maximum_fusion.refs_2_.refs_4_), channel_id=1, source_target_pairs={{0,64},{16,80},{32,96},{48,112},{64,0},{80,16},{96,32},{112,48},{1... | collective-permute-start | bytes 1572872 | tf_op jit(solution)/shard_map/ppermute | solution.py:283
  51.6 29.5 %collective-permute-start.10 = (f32[4,3,16,512]{3,2,1,0:T(8,128)S(1)}, f32[4,3,16,512]{3,2,1,0:T(8,128)S(1)}, u32[]{:S(2)}, u32[]{:S(2)}) collective-permute-start(f32[4,3,16,512]{3,2,1,0:T(8,128)S(1)} %pad_maximum_fusion.1.refs_6_.refs_8_.refs_4_), channel_id=1, source_target_pairs={{0,32},{16,48},{32,0},{48,16},{64,96},{80,112},{96,64},{112,80},{1... | collective-permute-start | bytes 1179656 | tf_op jit(solution)/shard_map/ppermute | solution.py:283
  59.2 21.9 %collective-permute-start.11 = (f32[4,3,16,512]{3,2,1,0:T(8,128)S(1)}, f32[4,3,16,512]{3,2,1,0:T(8,128)S(1)}, u32[]{:S(2)}, u32[]{:S(2)}) collective-permute-start(f32[4,3,16,512]{3,2,1,0:T(8,128)S(1)} %pad_maximum_fusion.1.refs_6_.refs_8_.refs_4_), channel_id=1, source_target_pairs={{0,48},{16,32},{32,16},{48,0},{64,112},{80,96},{96,80},{112,64},{1... | collective-permute-start | bytes 1179656 | tf_op jit(solution)/shard_map/ppermute | solution.py:283
  61.8 19.3 %all-to-all-start.2 = ((f32[16,2,512]{2,1,0:T(2,128)}), f32[16,2,512]{2,1,0:T(2,128)S(1)}, u32[]{:S(2)}, u32[]{:S(2)}) async-start(f32[16,2,512]{2,1,0:T(2,128)} %broadcast_in_dim.18), calls=%async_computation.2 | async-start | bytes 131072 | tf_op jit(solution)/shard_map/all_to_all | solution.py:279
  83.0 5.7 %collective-permute-start.13 = (f32[8,512]{1,0:T(8,128)S(1)}, f32[8,512]{1,0:T(8,128)S(1)}, u32[]{:S(2)}, u32[]{:S(2)}) collective-permute-start(f32[8,512]{1,0:T(8,128)S(1)} %get-tuple-element.38), channel_id=1, source_target_pairs={{0,3},{1,2},{16,19},{17,18},{32,35},{33,34},{48,51},{49,50},{64,67... | collective-permute-start | bytes 49160 | tf_op jit(solution)/shard_map/ppermute | solution.py:339
  87.4 2.1 %collective-permute-start.12 = (f32[8,512]{1,0:T(8,128)S(1)}, f32[8,512]{1,0:T(8,128)S(1)}, u32[]{:S(2)}, u32[]{:S(2)}) collective-permute-start(f32[8,512]{1,0:T(8,128)S(1)} %get-tuple-element.38), channel_id=1, source_target_pairs={{0,2},{1,3},{16,18},{17,19},{32,34},{33,35},{48,50},{49,51},{64,66... | collective-permute-start | bytes 49160 | tf_op jit(solution)/shard_map/ppermute | solution.py:338
  89.6 7.8 %collective-permute-start.15 = (f32[8,512]{1,0:T(8,128)S(1)}, f32[8,512]{1,0:T(8,128)S(1)}, u32[]{:S(2)}, u32[]{:S(2)}) collective-permute-start(f32[8,512]{1,0:T(8,128)S(1)} %get-tuple-element.40._), channel_id=1, source_target_pairs={{2,5},{3,4},{18,21},{19,20},{34,37},{35,36},{50,53},{51,52},{66,69... | collective-permute-start | bytes 49160 | tf_op jit(solution)/shard_map/ppermute | solution.py:339
  90.3 7.1 %collective-permute-start.14 = (f32[8,512]{1,0:T(8,128)S(1)}, f32[8,512]{1,0:T(8,128)S(1)}, u32[]{:S(2)}, u32[]{:S(2)}) collective-permute-start(f32[8,512]{1,0:T(8,128)S(1)} %get-tuple-element.40._), channel_id=1, source_target_pairs={{2,4},{3,5},{18,20},{19,21},{34,36},{35,37},{50,52},{51,53},{66,68... | collective-permute-start | bytes 49160 | tf_op jit(solution)/shard_map/ppermute | solution.py:338
  97.5 7.8 %collective-permute-start.17 = (f32[8,512]{1,0:T(8,128)S(1)}, f32[8,512]{1,0:T(8,128)S(1)}, u32[]{:S(2)}, u32[]{:S(2)}) collective-permute-start(f32[8,512]{1,0:T(8,128)S(1)} %get-tuple-element.42._), channel_id=1, source_target_pairs={{4,7},{5,6},{20,23},{21,22},{36,39},{37,38},{52,55},{53,54},{68,71... | collective-permute-start | bytes 49160 | tf_op jit(solution)/shard_map/ppermute | solution.py:339
  98.1 7.1 %collective-permute-start.16 = (f32[8,512]{1,0:T(8,128)S(1)}, f32[8,512]{1,0:T(8,128)S(1)}, u32[]{:S(2)}, u32[]{:S(2)}) collective-permute-start(f32[8,512]{1,0:T(8,128)S(1)} %get-tuple-element.42._), channel_id=1, source_target_pairs={{4,6},{5,7},{20,22},{21,23},{36,38},{37,39},{52,54},{53,55},{68,70... | collective-permute-start | bytes 49160 | tf_op jit(solution)/shard_map/ppermute | solution.py:338
  105.3 1.3 collective-permute-start.19
  106.0 0.7 collective-permute-start.18
  106.7 7.8 %collective-permute-start.21 = (f32[8,512]{1,0:T(8,128)S(1)}, f32[8,512]{1,0:T(8,128)S(1)}, u32[]{:S(2)}, u32[]{:S(2)}) collective-permute-start(f32[8,512]{1,0:T(8,128)S(1)} %get-tuple-element.46._), channel_id=1, source_target_pairs={{8,11},{9,10},{24,27},{25,26},{40,43},{41,42},{56,59},{57,58},{72,... | collective-permute-start | bytes 49160 | tf_op jit(solution)/shard_map/ppermute | solution.py:339
  107.4 7.1 %collective-permute-start.20 = (f32[8,512]{1,0:T(8,128)S(1)}, f32[8,512]{1,0:T(8,128)S(1)}, u32[]{:S(2)}, u32[]{:S(2)}) collective-permute-start(f32[8,512]{1,0:T(8,128)S(1)} %get-tuple-element.46._), channel_id=1, source_target_pairs={{8,10},{9,11},{24,26},{25,27},{40,42},{41,43},{56,58},{57,59},{72,... | collective-permute-start | bytes 49160 | tf_op jit(solution)/shard_map/ppermute | solution.py:338
  114.6 1.5 %collective-permute-start.23 = (f32[8,512]{1,0:T(8,128)S(1)}, f32[8,512]{1,0:T(8,128)S(1)}, u32[]{:S(2)}, u32[]{:S(2)}) collective-permute-start(f32[8,512]{1,0:T(8,128)S(1)} %get-tuple-element.48), channel_id=1, source_target_pairs={{10,13},{11,12},{26,29},{27,28},{42,45},{43,44},{58,61},{59,60},{7... | collective-permute-start | bytes 49160 | tf_op jit(solution)/shard_map/ppermute | solution.py:339
  115.2 0.9 collective-permute-start.22
  116.1 1.6 %copy-start.2 = (bf16[2048,256]{1,0:T(8,128)(2,1)S(1)}, bf16[2048,256]{1,0:T(8,128)(2,1)}, u32[]{:S(2)}) copy-start(bf16[2048,256]{1,0:T(8,128)(2,1)} %panel.3) | copy-start | bytes 3145732
  116.2 1.5 %collective-permute-start.25 = (f32[8,512]{1,0:T(8,128)S(1)}, f32[8,512]{1,0:T(8,128)S(1)}, u32[]{:S(2)}, u32[]{:S(2)}) collective-permute-start(f32[8,512]{1,0:T(8,128)S(1)} %get-tuple-element.50), channel_id=1, source_target_pairs={{12,15},{13,14},{28,31},{29,30},{44,47},{45,46},{60,63},{61,62},{7... | collective-permute-start | bytes 49160 | tf_op jit(solution)/shard_map/ppermute | solution.py:339
  117.0 0.7 collective-permute-start.24
  117.7 0.7 copy-start.6
  119.9 21.8 %all-to-all-start.3 = ((f32[16,1,128]{2,1,0:T(1,128)}), f32[16,1,128]{2,1,0:T(1,128)S(1)}, u32[]{:S(2)}, u32[]{:S(2)}) async-start(f32[16,1,128]{2,1,0:T(1,128)} %bitcast.17), calls=%async_computation.3 | async-start | bytes 16384 | tf_op jit(solution)/shard_map/all_to_all | solution.py:347
